TPU v7x, 32 devices: a whole 2x2x4 slice. The times are simulated.
32 devices in a mesh: dp: 2 (over y), ctx: 16 (over z, x, core).
Axes of the slice: x: 2, y: 2, z: 4, core: 2. Of those that a mesh axis runs over, the one named last changes fastest.
Arguments:
- tokens: bfloat16 [4, 512, 2, 1024], P('dp', 'ctx'), may hold values from -6 to 6
- segments: int32 [4, 512, 2], P('dp'), may hold values from 0 to 16, as said below
- lengths: int32 [4], P('dp'), may hold values from 512 to 768, as said below
- attn_in: bfloat16 [2048, 1024], P(('dp', 'ctx')), may hold values from -0.1875 to 0.1875
- attn_out: bfloat16 [1024, 1024], P(('dp', 'ctx')), may hold values from -0.75 to 0.75
- gains: bfloat16 [2176], P(('dp', 'ctx')), may hold values from 0.5 to 1.5
- ffn_weights: bfloat16 [4608, 3, 1024], P(('dp', 'ctx')), may hold values from -0.1875 to 0.1875
- cotangent: bfloat16 [4, 512, 2, 1024], P('dp', 'ctx'), may hold values from -6 to 6
Outputs:
- block_out: bfloat16 [4, 512, 2, 1024], P('dp', 'ctx')
- tokens_grad: float32 [4, 512, 2, 1024], P('dp', 'ctx')
- attn_in_grad: float32 [2048, 1024], P(('dp', 'ctx'))
- attn_out_grad: float32 [1024, 1024], P(('dp', 'ctx'))
- gains_grad: float32 [2176], P(('dp', 'ctx'))
- ffn_grad: float32 [4608, 3, 1024], P(('dp', 'ctx'))
Inputs may be any that keep to these rules, and one draw needn't show every extreme that they name: `segments`: in each sequence, taken in order of position, the ids never fall and begin at 0. `lengths`: one sequence has exactly the largest length.
All inputs are finite; a program needn't handle non-finite values.
Results may differ from a plain program's by a relative error of at most 0.028.
Values may be sent and summed in bfloat16 or wider, within the bound.
A program may use at most 448 MiB of HBM per device.

v0:
```python
import math

import jax
import jax.numpy as jnp
from jax import lax
from jax.sharding import PartitionSpec as P

FF = 4608
HEADS = 16
KV_HEADS = 8
HEAD_DIM = 64
QKV_ROWS = 2048


EPS = 1e-05
ROPE_BASE = 1000000.0
MASKED = -1e30


def root_mean(values):
    return lax.rsqrt(jnp.mean(values * values, axis=-1, keepdims=True) + EPS)


def rotate(values, cosine, sine):
    width = values.shape[-1] // 2
    first = values[..., :width]
    second = values[..., width:]
    return jnp.concatenate(
        [first * cosine - second * sine, second * cosine + first * sine], axis=-1
    )


def tables(positions):
    width = HEAD_DIM // 2
    freq = ROPE_BASE ** (-jnp.arange(width, dtype=jnp.float32) * 2.0 / HEAD_DIM)
    angle = positions.astype(jnp.float32)[..., None] * freq
    return (jnp.cos(angle), jnp.sin(angle))


def prepare(query_raw, key_raw, query_gain, key_gain, cosine, sine):
    query_norm = query_raw * root_mean(query_raw) * query_gain
    key_norm = key_raw * root_mean(key_raw) * key_gain
    return (
        rotate(query_norm, cosine[:, None, None], sine[:, None, None]),
        rotate(key_norm, cosine[:, None], sine[:, None]),
    )


def positions_of(first_row, count, block_len, ctx_count):
    rows = first_row + jnp.arange(count, dtype=jnp.int32)
    mirror = (2 * ctx_count - 1 - rows // block_len) * block_len + rows % block_len
    return jnp.stack([rows, mirror], axis=1)


def allowed(query_place, key_place, query_doc, key_doc, lengths):
    causal = key_place[None, None, :] <= query_place[None, :, None]
    live = (key_place[None, None, :] < lengths[:, None, None]) | (
        key_place[None, None, :] == query_place[None, :, None]
    )
    return causal & live & (query_doc[:, :, None] == key_doc[:, None, :])


def norm_back(grad, normed, scale_rows, gain):
    weighted = grad * gain
    inner = jnp.mean(weighted * normed, axis=-1, keepdims=True)
    return (scale_rows * (weighted - normed * inner), jnp.sum(grad * normed, axis=0))


def span_of(rows_total, block_len):
    return math.gcd(rows_total, 4 * block_len)


def unit_forward(rows_in, units):

    def step(carry, piece, start):
        both = jnp.einsum("rd,cjd->rjc", rows_in, piece[:, :2], preferred_element_type=jnp.float32)
        hidden = (jax.nn.silu(both[:, 0]) * both[:, 1]).astype(jnp.bfloat16)
        out_sum = jnp.einsum("rc,cd->rd", hidden, piece[:, 2], preferred_element_type=jnp.float32)
        return (out_sum, both)

    initial = (
        jnp.zeros(rows_in.shape, jnp.float32),
        jnp.zeros((rows_in.shape[0], 2, units), jnp.float32),
    )
    return (step, initial)


def unit_backward(grads_in, kept):

    def step(carry, piece, start):
        gate = kept[:, 0]
        upward = kept[:, 1]
        sigmoid = jax.nn.sigmoid(gate)
        d_hidden = jnp.einsum(
            "rd,cd->rc", grads_in, piece[:, 2], preferred_element_type=jnp.float32
        )
        d_gate = d_hidden * upward * sigmoid * (1.0 + gate * (1.0 - sigmoid))
        d_up = d_hidden * jax.nn.silu(gate)
        d_both = jnp.stack([d_gate, d_up], axis=1).astype(jnp.bfloat16)
        back_sum = jnp.einsum(
            "rjc,cjd->rd", d_both, piece[:, :2], preferred_element_type=jnp.float32
        )
        return (back_sum, d_both)

    initial = (
        jnp.zeros((grads_in.shape[0], grads_in.shape[1]), jnp.float32),
        jnp.zeros(kept.shape, jnp.bfloat16),
    )
    return (step, initial)


def unit_terms(rows_in, grads_in, kept, stored):
    hidden = (jax.nn.silu(kept[:, 0]) * kept[:, 1]).astype(jnp.bfloat16)
    front = jnp.einsum("rjc,rd->cjd", stored, rows_in, preferred_element_type=jnp.float32)
    back = jnp.einsum("rc,rd->cd", hidden, grads_in, preferred_element_type=jnp.float32)
    return jnp.concatenate([front, back[:, None]], axis=1)


def on_device(tokens, segments, lengths, attn_in, attn_out, gains, ffn_weights, cotangent):
    batches, block_len, halves, width = tokens.shape
    ctx_count = lax.axis_size("ctx")
    here = lax.axis_index("ctx")
    group = HEADS // KV_HEADS
    count = batches * block_len * halves
    local = halves * block_len
    scale = HEAD_DIM ** (-0.5)
    weight_in, weight_out, gain_all = (
        lax.all_gather(attn_in, ("dp", "ctx"), axis=0, tiled=True),
        lax.all_gather(attn_out, ("dp", "ctx"), axis=0, tiled=True),
        lax.all_gather(gains, ("dp", "ctx"), axis=0, tiled=True),
    )
    gain_all = gain_all.astype(jnp.float32)
    attn_gain = gain_all[:width]
    ffn_gain = gain_all[width : 2 * width]
    query_gain = gain_all[2 * width : 2 * width + HEAD_DIM]
    key_gain = gain_all[2 * width + HEAD_DIM :]
    query_place = positions_of(here * block_len, block_len, block_len, ctx_count).reshape(local)
    query_doc = lax.dynamic_slice_in_dim(segments, here * block_len, block_len, 1).reshape(
        batches, local
    )
    row_place = jnp.broadcast_to(query_place, (batches, local))
    valid = (row_place < lengths[:, None]).reshape(count).astype(jnp.float32)
    cosine, sine = tables(row_place.reshape(count))
    inputs = tokens.astype(jnp.float32).reshape(count, width)
    first_scale = root_mean(inputs)
    first_normed = inputs * first_scale
    first = (first_normed * attn_gain).astype(jnp.bfloat16)
    projected = jnp.einsum("rd,fd->rf", first, weight_in, preferred_element_type=jnp.float32)
    projected = projected.reshape(count, KV_HEADS, group + 2, HEAD_DIM)

    def prepare_here(query_raw, key_raw, gain_query, gain_key):
        return prepare(query_raw, key_raw, gain_query, gain_key, cosine, sine)

    (query_rot, key_rot), prepare_pull = jax.vjp(
        prepare_here, projected[:, :, :group], projected[:, :, group], query_gain, key_gain
    )
    queries = query_rot.astype(jnp.bfloat16).reshape(batches, local, KV_HEADS, group, HEAD_DIM)
    keys_here = key_rot.astype(jnp.bfloat16).reshape(batches, local, KV_HEADS, HEAD_DIM)
    values_here = (
        projected[:, :, group + 1].astype(jnp.bfloat16).reshape(batches, local, KV_HEADS, HEAD_DIM)
    )
    key_pack = jnp.stack(
        [
            keys_here.reshape(batches, block_len, halves, KV_HEADS * HEAD_DIM),
            values_here.reshape(batches, block_len, halves, KV_HEADS * HEAD_DIM),
        ],
        axis=3,
    )

    def span_keys(piece, offset, row_start, span):
        block = lax.dynamic_slice_in_dim(piece, offset, span, 1)
        keys = block[:, :, :, 0].reshape(batches, span * 2, KV_HEADS, HEAD_DIM)
        values = block[:, :, :, 1].reshape(batches, span * 2, KV_HEADS, HEAD_DIM)
        key_place = positions_of(row_start, span, block_len, ctx_count).reshape(span * 2)
        key_doc = lax.dynamic_slice_in_dim(segments, row_start, span, 1).reshape(batches, span * 2)
        return (keys, values, key_place, key_doc)

    def forward_tile(state, keys, values, mask):
        peak, total, summed = state
        wide = mask[:, :, None, None, :]
        scores = (
            jnp.einsum("bqgjd,bkgd->bqgjk", queries, keys, preferred_element_type=jnp.float32)
            * scale
        )
        scores = jnp.where(wide, scores, MASKED)
        new_peak = jnp.maximum(peak, jnp.max(scores, axis=-1))
        weights = jnp.where(wide, jnp.exp(scores - new_peak[..., None]), 0.0)
        fade = jnp.exp(peak - new_peak)
        total = total * fade + jnp.sum(weights, axis=-1)
        summed = summed * fade[..., None] + jnp.einsum(
            "bqgjk,bkgd->bqgjd",
            weights.astype(jnp.bfloat16),
            values,
            preferred_element_type=jnp.float32,
        )
        return (new_peak, total, summed)

    stat_shape = (batches, local, KV_HEADS, group)
    start_state = (
        jnp.full(stat_shape, MASKED, jnp.float32),
        jnp.zeros(stat_shape, jnp.float32),
        jnp.zeros(stat_shape + (HEAD_DIM,), jnp.float32),
    )
    piece = lax.all_gather(key_pack, "ctx", axis=1, tiled=True)
    span = span_of(piece.shape[1], block_len)

    def forward_visit(index, inner):
        keys, values, key_place, key_doc = span_keys(piece, index * span, index * span, span)
        mask = allowed(query_place, key_place, query_doc, key_doc, lengths)
        return lax.cond(
            jnp.any(mask),
            lambda carried: forward_tile(carried, keys, values, mask),
            lambda carried: carried,
            inner,
        )

    peak, total, summed = lax.fori_loop(0, piece.shape[1] // span, forward_visit, start_state)
    log_total = peak + jnp.log(total)
    attended = summed / total[..., None]
    mixed = attended.astype(jnp.bfloat16).reshape(count, HEADS * HEAD_DIM)
    state = inputs + jnp.einsum("rf,fd->rd", mixed, weight_out, preferred_element_type=jnp.float32)
    second_scale = root_mean(state)
    second_normed = state * second_scale
    second = (second_normed * ffn_gain).astype(jnp.bfloat16)
    grad_out = cotangent.astype(jnp.float32).reshape(count, width) * valid[:, None]
    grad_low = grad_out.astype(jnp.bfloat16)
    step, initial = unit_forward(second, FF)
    ffn_sum, kept = step(
        initial, lax.all_gather(ffn_weights, ("dp", "ctx"), axis=0, tiled=True), jnp.int32(0)
    )
    back_step, back_initial = unit_backward(grad_low, kept)
    second_grad, stored = back_step(
        back_initial, lax.all_gather(ffn_weights, ("dp", "ctx"), axis=0, tiled=True), jnp.int32(0)
    )
    ffn_grad = lax.psum_scatter(
        unit_terms(second, grad_low, kept, stored), ("dp", "ctx"), scatter_dimension=0, tiled=True
    )
    block_out = (state + ffn_sum).astype(jnp.bfloat16)
    norm_grad, ffn_gain_grad = norm_back(second_grad, second_normed, second_scale, ffn_gain)
    state_grad = grad_out + norm_grad
    attended_grad = state_grad.astype(jnp.bfloat16)
    mixed_grad = jnp.einsum(
        "rd,fd->rf", attended_grad, weight_out, preferred_element_type=jnp.float32
    ).astype(jnp.bfloat16)
    out_term = jnp.einsum("rf,rd->fd", mixed, attended_grad, preferred_element_type=jnp.float32)
    mixed_grad = mixed_grad.reshape(batches, local, KV_HEADS, group, HEAD_DIM)
    delta = jnp.sum(mixed_grad.astype(jnp.float32) * attended, axis=-1)

    def query_tile(carried, keys, values, mask):
        wide = mask[:, :, None, None, :]
        scores = (
            jnp.einsum("bqgjd,bkgd->bqgjk", queries, keys, preferred_element_type=jnp.float32)
            * scale
        )
        weights = jnp.where(wide, jnp.exp(scores - log_total[..., None]), 0.0)
        pulled = jnp.einsum(
            "bqgjd,bkgd->bqgjk", mixed_grad, values, preferred_element_type=jnp.float32
        )
        score_grad = (weights * (pulled - delta[..., None])).astype(jnp.bfloat16)
        return carried + jnp.einsum(
            "bqgjk,bkgd->bqgjd", score_grad, keys, preferred_element_type=jnp.float32
        )

    def query_piece(carried, piece):
        span = span_of(piece.shape[1], block_len)

        def query_visit(index, inner):
            keys, values, key_place, key_doc = span_keys(piece, index * span, index * span, span)
            mask = allowed(query_place, key_place, query_doc, key_doc, lengths)
            return lax.cond(
                jnp.any(mask),
                lambda held: query_tile(held, keys, values, mask),
                lambda held: held,
                inner,
            )

        return lax.fori_loop(0, piece.shape[1] // span, query_visit, carried)

    query_grad = (
        query_piece(
            jnp.zeros(stat_shape + (HEAD_DIM,), jnp.float32),
            lax.all_gather(key_pack, "ctx", axis=1, tiled=True),
        )
        * scale
    )
    query_pack = jnp.stack(
        [
            queries.reshape(batches, block_len, halves, HEADS * HEAD_DIM),
            mixed_grad.reshape(batches, block_len, halves, HEADS * HEAD_DIM),
        ],
        axis=3,
    ).astype(jnp.float32)
    stat_pack = jnp.stack(
        [
            log_total.reshape(batches, block_len, halves, HEADS),
            delta.reshape(batches, block_len, halves, HEADS),
        ],
        axis=3,
    )

    def key_tile(carried, query_block, grad_block, log_block, delta_block, mask):
        key_sum, value_sum = carried
        wide = mask[:, :, None, None, :]
        scores = (
            jnp.einsum(
                "bqgjd,bkgd->bqgjk", query_block, keys_here, preferred_element_type=jnp.float32
            )
            * scale
        )
        weights = jnp.where(wide, jnp.exp(scores - log_block[..., None]), 0.0)
        pulled = jnp.einsum(
            "bqgjd,bkgd->bqgjk", grad_block, values_here, preferred_element_type=jnp.float32
        )
        score_grad = (weights * (pulled - delta_block[..., None])).astype(jnp.bfloat16)
        key_sum = key_sum + jnp.einsum(
            "bqgjk,bqgjd->bkgd", score_grad, query_block, preferred_element_type=jnp.float32
        )
        value_sum = value_sum + jnp.einsum(
            "bqgjk,bqgjd->bkgd",
            weights.astype(jnp.bfloat16),
            grad_block,
            preferred_element_type=jnp.float32,
        )
        return (key_sum, value_sum)

    key_zero = jnp.zeros((batches, local, KV_HEADS, HEAD_DIM), jnp.float32)
    query_part = lax.all_gather(query_pack.astype(jnp.bfloat16), "ctx", axis=1, tiled=True).astype(
        jnp.float32
    )
    stat_part = lax.all_gather(stat_pack.astype(jnp.bfloat16), "ctx", axis=1, tiled=True).astype(
        jnp.float32
    )
    key_span = span_of(query_part.shape[1], block_len)

    def key_visit(index, inner):
        row_start = index * key_span
        block = lax.dynamic_slice_in_dim(query_part, index * key_span, key_span, 1)
        stats = lax.dynamic_slice_in_dim(stat_part, index * key_span, key_span, 1)
        remote_place = positions_of(row_start, key_span, block_len, ctx_count).reshape(key_span * 2)
        remote_doc = lax.dynamic_slice_in_dim(segments, row_start, key_span, 1).reshape(
            batches, key_span * 2
        )
        query_block = (
            block[:, :, :, 0]
            .astype(jnp.bfloat16)
            .reshape(batches, key_span * 2, KV_HEADS, group, HEAD_DIM)
        )
        grad_block = (
            block[:, :, :, 1]
            .astype(jnp.bfloat16)
            .reshape(batches, key_span * 2, KV_HEADS, group, HEAD_DIM)
        )
        log_block = stats[:, :, :, 0].reshape(batches, key_span * 2, KV_HEADS, group)
        delta_block = stats[:, :, :, 1].reshape(batches, key_span * 2, KV_HEADS, group)
        mask = allowed(remote_place, query_place, remote_doc, query_doc, lengths)
        return lax.cond(
            jnp.any(mask),
            lambda held: key_tile(held, query_block, grad_block, log_block, delta_block, mask),
            lambda held: held,
            inner,
        )

    key_sum, value_sum = lax.fori_loop(
        0, query_part.shape[1] // key_span, key_visit, (key_zero, key_zero)
    )
    query_raw_grad, key_raw_grad, query_gain_grad, key_gain_grad = prepare_pull(
        (
            query_grad.reshape(count, KV_HEADS, group, HEAD_DIM),
            (key_sum * scale).reshape(count, KV_HEADS, HEAD_DIM),
        )
    )
    projected_grad = jnp.concatenate(
        [query_raw_grad, key_raw_grad[:, :, None], value_sum.reshape(count, KV_HEADS, 1, HEAD_DIM)],
        axis=2,
    )
    projected_grad = projected_grad.reshape(count, QKV_ROWS).astype(jnp.bfloat16)
    first_grad = jnp.einsum(
        "rf,fd->rd", projected_grad, weight_in, preferred_element_type=jnp.float32
    )
    in_term = jnp.einsum("rf,rd->fd", projected_grad, first, preferred_element_type=jnp.float32)
    input_norm_grad, attn_gain_grad = norm_back(first_grad, first_normed, first_scale, attn_gain)
    tokens_grad = state_grad + input_norm_grad
    gain_term = jnp.concatenate([attn_gain_grad, ffn_gain_grad, query_gain_grad, key_gain_grad])
    attn_in_grad, attn_out_grad, gains_grad = (
        lax.psum_scatter(in_term, ("dp", "ctx"), scatter_dimension=0, tiled=True),
        lax.psum_scatter(out_term, ("dp", "ctx"), scatter_dimension=0, tiled=True),
        lax.psum_scatter(gain_term, ("dp", "ctx"), scatter_dimension=0, tiled=True),
    )
    return (
        block_out.reshape(batches, block_len, halves, width),
        tokens_grad.reshape(batches, block_len, halves, width),
        attn_in_grad,
        attn_out_grad,
        gains_grad,
        ffn_grad,
    )


def solution(mesh):
    placed = (
        P("dp", "ctx", None, None),
        P("dp", None, None),
        P("dp"),
        P(("dp", "ctx"), None),
        P(("dp", "ctx"), None),
        P(("dp", "ctx")),
        P(("dp", "ctx"), None, None),
        P("dp", "ctx", None, None),
    )
    return jax.shard_map(
        on_device,
        mesh=mesh,
        in_specs=placed,
        out_specs=(
            P("dp", "ctx", None, None),
            P("dp", "ctx", None, None),
            P(("dp", "ctx"), None),
            P(("dp", "ctx"), None),
            P(("dp", "ctx")),
            P(("dp", "ctx"), None, None),
        ),
        check_vma=False,
    )
```

profile of v0, /device:TPU:0, one launch (start us, length us, event | category | flops | bytes accessed | tf_op | source)
XLA Modules:
  0.0 1912.6 jit_solution(2845462751203193392)
XLA Ops:
  9.1 42.8 %all-reduce.4 = bf16[2176]{0:T(1024)(128)(2,1)S(1)} all-reduce(bf16[2176]{0:T(1024)(128)(2,1)S(1)} %dynamic-update-slice), channel_id=1, replica_groups=mesh['dp'=2,'ctx'=16] {'dp','ctx'}, use_global_device_ids=true, to_apply=%add.4 | all-reduce | flops 2176 | bytes 8704
  54.9 20.8 %all-gather.6.cloned.1.call-done = bf16[2048,1024]{1,0:T(8,128)(2,1)} async-done(((bf16[64,1024]{1,0:T(8,128)(2,1)}), bf16[2048,1024]{1,0:T(8,128)(2,1)}) %all-gather.6.cloned.1.call-update) | async-done | bytes 4194320 | tf_op jit(solution)/shard_map/all_gather | solution.py:128
  93.8 38.3 %all-gather.8.cloned.1.call-done = bf16[2,512,2,2,512]{4,2,1,0,3:T(2,128)(2,1)} async-done(((bf16[2,32,2,2,512]{4,2,1,0,3:T(2,128)(2,1)}), bf16[2,512,2,2,512]{4,2,1,0,3:T(2,128)(2,1)}) %all-gather.8.cloned.1.call-update) | async-done | bytes 4194320 | tf_op jit(solution)/shard_map/all_gather | solution.py:204
  133.2 20.4 %while.57 = (s32[]{:T(128)}, f32[2,64,8,2]{1,3,2,0:T(2,128)S(1)}, f32[2,64,8,2]{1,3,2,0:T(2,128)S(1)}, f32[2,64,8,2,64]{4,1,3,2,0:T(8,128)}, s32[32,2]{1,0:T(8,1...) while((s32[]{:T(128)}, f32[2,64,8,2]{1,3,2,0:T(2,128)S(1)}, ...), condition=%wide.wide.region_9.10_spmd, body=%wide.wide.region_3.9_spmd.sunk | while | flops 141500032 | bytes 13194333 | solution.py:217
  156.2 33.7 %all-gather.10.cloned.1.call-done = bf16[1024,1024]{1,0:T(8,128)(2,1)} async-done(((bf16[32,1024]{1,0:T(8,128)(2,1)}), bf16[1024,1024]{1,0:T(8,128)(2,1)}) %all-gather.10.cloned.1.call-update) | async-done | bytes 2097168 | tf_op jit(solution)/shard_map/all_gather | solution.py:129
  192.1 169.2 %all-gather.12.cloned.1.call-done = bf16[4608,3,1024]{2,0,1:T(8,128)(2,1)} async-done(((bf16[144,3,1024]{2,0,1:T(8,128)(2,1)}), bf16[4608,3,1024]{2,0,1:T(8,128)(2,1)}) %all-gather.12.cloned.1.call-update) | async-done | bytes 28311568 | tf_op jit(solution)/shard_map/all_gather | solution.py:229
  361.3 10.1 fusion.52
  380.4 9.0 multiply_reduce_fusion.2
  405.7 15.0 convolution_bitcast_fusion.3
  420.8 38.0 %pad_maximum_fusion = f32[4608,3,1024]{0,2,1:T(8,128)} fusion(f32[4608,1,1024]{0,2,1:T(8,128)} %convolution_bitcast_fusion.4, f32[4608,2,1024]{0,2,1:T(8,128)} %convolution_bitcast_fusion.3), kind=kLoop, calls=%fused_computation.97 | loop fusion | flops 14155776 | bytes 113246208 | tf_op jit(solution)/shard_map/concatenate | solution.py:116
  458.8 79.9 %copy.344 = f32[4608,3,1024]{2,1,0:T(4,128)} copy(f32[4608,3,1024]{0,2,1:T(8,128)} %pad_maximum_fusion) | data formatting | bytes 113246208 | tf_op jit(solution)/shard_map/concatenate | solution.py:116
  552.1 20.9 %while.58 = (s32[]{:T(128)}, f32[2,64,8,2,64]{4,1,3,2,0:T(8,128)}, s32[32,2]{1,0:T(8,128)}, s32[2]{0:T(128)S(1)}, s32[2,32,2]{2,1,0:T(8,128)}, /*index=5*/s32[2,...) while((s32[]{:T(128)}, f32[2,64,8,2,64]{4,1,3,2,0:T(8,128)}, ...), condition=%wide.wide.region_17.18_spmd, body=%wide.wide.region_13.17_spmd.sunk | while | flops 204803712 | bytes 12751933 | solution.py:277
  555.3 9.1 conditional.10
  578.3 56.3 %all_gather.29 = bf16[2,512,2,2,16]{4,3,2,0,1:T(2,128)(2,1)S(1)} all-gather(bf16[2,32,2,2,16]{4,3,2,0,1:T(2,128)(2,1)S(1)} %copy.335), channel_id=1, replica_groups=mesh['dp'=2,'ctx'=16] {'ctx'}, dimensions={1}, use_global_device_ids=true | all-gather | bytes 139264 | tf_op jit(solution)/shard_map/all_gather | solution.py:330
  634.6 16.1 copy.338
  653.3 169.2 %while.59 = (s32[]{:T(128)}, f32[2,64,8,64]{3,1,2,0:T(8,128)}, f32[2,64,8,64]{3,1,2,0:T(8,128)}, s32[32,2]{1,0:T(8,128)}, s32[2]{0:T(128)S(1)}, /*index=5*/s32[2...) while((s32[]{:T(128)}, f32[2,64,8,64]{3,1,2,0:T(8,128)}, ...), condition=%wide.wide.region_23.24_spmd, body=%wide.wide.region_19.23_spmd.sunk | while | flops 272436480 | bytes 29052512 | solution.py:363
  656.4 39.3 %conditional.11 = ((f32[2,64,8,64]{3,1,2,0:T(8,128)}, f32[2,64,8,64]{3,1,2,0:T(8,128)})) conditional(s32[]{:T(128)} %convert_element_type.286, (f32[2,64,8,64]{3,1,2,0:T(8,128)}, f32[2,64,8,64]{3,1,2,0:T(8,128)}) %tuple.254, (pred[2,256,64]{1,2,0:T(8,128)(4,1)S(1)}, bf16[2,512,2,2,1024]{4,2,1,0,3:T(2,128)(2,1)}, s32[]{:T(128)}, ...), branch_computations={%region_21.21_spmd, %region_22.22_spmd} | conditional | flops 272236544 | bytes 28934192 | solution.py:356
  698.7 39.2 %conditional.11 = ((f32[2,64,8,64]{3,1,2,0:T(8,128)}, f32[2,64,8,64]{3,1,2,0:T(8,128)})) conditional(s32[]{:T(128)} %convert_element_type.286, (f32[2,64,8,64]{3,1,2,0:T(8,128)}, f32[2,64,8,64]{3,1,2,0:T(8,128)}) %tuple.254, (pred[2,256,64]{1,2,0:T(8,128)(4,1)S(1)}, bf16[2,512,2,2,1024]{4,2,1,0,3:T(2,128)(2,1)}, s32[]{:T(128)}, ...), branch_computations={%region_21.21_spmd, %region_22.22_spmd} | conditional | flops 272236544 | bytes 28934192 | solution.py:356
  740.8 39.2 %conditional.11 = ((f32[2,64,8,64]{3,1,2,0:T(8,128)}, f32[2,64,8,64]{3,1,2,0:T(8,128)})) conditional(s32[]{:T(128)} %convert_element_type.286, (f32[2,64,8,64]{3,1,2,0:T(8,128)}, f32[2,64,8,64]{3,1,2,0:T(8,128)}) %tuple.254, (pred[2,256,64]{1,2,0:T(8,128)(4,1)S(1)}, bf16[2,512,2,2,1024]{4,2,1,0,3:T(2,128)(2,1)}, s32[]{:T(128)}, ...), branch_computations={%region_21.21_spmd, %region_22.22_spmd} | conditional | flops 272236544 | bytes 28934192 | solution.py:356
  783.0 39.3 %conditional.11 = ((f32[2,64,8,64]{3,1,2,0:T(8,128)}, f32[2,64,8,64]{3,1,2,0:T(8,128)})) conditional(s32[]{:T(128)} %convert_element_type.286, (f32[2,64,8,64]{3,1,2,0:T(8,128)}, f32[2,64,8,64]{3,1,2,0:T(8,128)}) %tuple.254, (pred[2,256,64]{1,2,0:T(8,128)(4,1)S(1)}, bf16[2,512,2,2,1024]{4,2,1,0,3:T(2,128)(2,1)}, s32[]{:T(128)}, ...), branch_computations={%region_21.21_spmd, %region_22.22_spmd} | conditional | flops 272236544 | bytes 28934192 | solution.py:356
  843.0 38.3 %all-reduce.5 = f32[2176]{0:T(1024)S(1)} all-reduce(f32[2176]{0:T(1024)S(1)} %concatenate.42), channel_id=4, replica_groups=mesh['dp'=2,'ctx'=16] {'dp','ctx'}, use_global_device_ids=true, to_apply=%region_32.33.clone | all-reduce | flops 2176 | bytes 17408
  881.9 731.7 %all-reduce.9.cloned.1.call-done = f32[4608,3,1024]{2,1,0:T(4,128)} async-done(((f32[4608,3,1024]{2,1,0:T(4,128)}), f32[4608,3,1024]{2,1,0:T(4,128)}) %all-reduce.9.cloned.1.call-update) | async-done | bytes 56623120
  1618.0 139.5 %reduce-scatter.5.cloned.1.call-done = f32[32,1024]{1,0:T(8,128)} async-done(((f32[1024,1024]{1,0:T(8,128)}), f32[32,1024]{1,0:T(8,128)}) %reduce-scatter.5.cloned.1.call-update) | async-done | bytes 131088 | tf_op jit(solution)/shard_map/reduce_scatter | solution.py:386
  1757.5 148.0 %reduce-scatter.3.cloned.1.call-done = f32[64,1024]{1,0:T(8,128)} async-done(((f32[2048,1024]{1,0:T(8,128)}), f32[64,1024]{1,0:T(8,128)}) %reduce-scatter.3.cloned.1.call-update) | async-done | bytes 262160 | tf_op jit(solution)/shard_map/reduce_scatter | solution.py:385
  (456 shorter events, 310.1 us)
Async XLA Ops:
  7.2 68.6 %all-gather.6.cloned.1.call-start = ((), (), s32[]{:S(2)}) async-start(), calls=%async_computation.2 | async-start | bytes 4325376 | tf_op jit(solution)/shard_map/all_gather | solution.py:128
  7.9 124.2 %all-gather.8.cloned.1.call-start = ((), (), s32[]{:S(2)}) async-start(), calls=%async_computation.3 | async-start | bytes 4456448 | tf_op jit(solution)/shard_map/all_gather | solution.py:204
  8.1 78.1 %copy-start.33 = (s32[32,2]{1,0:T(8,128)}, s32[32,2]{1,0:T(8,128)S(1)}, u32[]{:S(2)}) copy-start(s32[32,2]{1,0:T(8,128)S(1)} %copy.317) | copy-start | bytes 772
  53.2 26.0 %copy-start.55 = (f32[1024]{0:T(1024)}, f32[1024]{0:T(1024)S(1)}, u32[]{:S(2)}) copy-start(f32[1024]{0:T(1024)S(1)} %get-tuple-element.1429) | copy-start | bytes 12292
  53.2 22.5 %copy-start.45 = (f32[2,32,2]{2,1,0:T(8,128)}, f32[2,32,2]{2,1,0:T(8,128)S(1)}, u32[]{:S(2)}) copy-start(f32[2,32,2]{2,1,0:T(8,128)S(1)} %add_rsqrt_fusion) | copy-start | bytes 1540
  54.6 21.2 %copy-start.19 = (bf16[2,32,2,1024]{3,2,1,0:T(2,128)(2,1)}, bf16[2,32,2,1024]{3,2,1,0:T(2,128)(2,1)S(1)}, u32[]{:S(2)}) copy-start(bf16[2,32,2,1024]{3,2,1,0:T(2,128)(2,1)S(1)} %multiply_convert_fusion.3) | copy-start | bytes 786436
  54.8 25.7 %copy-start.64 = (f32[64]{0:T(128)}, f32[64]{0:T(128)S(1)}, u32[]{:S(2)}) copy-start(f32[64]{0:T(128)S(1)} %get-tuple-element.1431) | copy-start | bytes 772
  54.8 34.5 %copy-start.61 = (f32[64]{0:T(128)}, f32[64]{0:T(128)S(1)}, u32[]{:S(2)}) copy-start(f32[64]{0:T(128)S(1)} %get-tuple-element.1430) | copy-start | bytes 772
  54.9 35.1 %copy-start.41 = (f32[128,32]{0,1:T(8,128)}, f32[128,32]{0,1:T(8,128)S(1)}, u32[]{:S(2)}) copy-start(f32[128,32]{0,1:T(8,128)S(1)} %get-tuple-element.1432) | copy-start | bytes 49156
  54.9 35.1 %copy-start.43 = (f32[128,32]{0,1:T(8,128)}, f32[128,32]{0,1:T(8,128)S(1)}, u32[]{:S(2)}) copy-start(f32[128,32]{0,1:T(8,128)S(1)} %get-tuple-element.1433) | copy-start | bytes 49156
  79.2 10.1 copy-start.2
  82.8 107.1 %all-gather.10.cloned.1.call-start = ((), (), s32[]{:S(2)}) async-start(), calls=%async_computation.4 | async-start | bytes 2162688 | tf_op jit(solution)/shard_map/all_gather | solution.py:129
  83.5 277.8 %all-gather.12.cloned.1.call-start = ((), (), s32[]{:S(2)}) async-start(), calls=%async_computation.5 | async-start | bytes 29196288 | tf_op jit(solution)/shard_map/all_gather | solution.py:229
  84.1 567.5 %all-gather.14.cloned.1.call-start = ((), (), s32[]{:S(2)}) async-start(), calls=%async_computation.6 | async-start | bytes 8912896 | tf_op jit(solution)/shard_map/all_gather | solution.py:327
  153.6 38.4 %copy-start.17 = (f32[2,64,8,2]{1,3,2,0:T(2,128)}, f32[2,64,8,2]{1,3,2,0:T(2,128)S(1)}, u32[]{:S(2)}) copy-start(f32[2,64,8,2]{1,3,2,0:T(2,128)S(1)} %get-tuple-element.1006) | copy-start | bytes 24580
  153.7 38.4 %copy-start.22 = (f32[2,64,8,2]{1,3,2,0:T(2,128)}, f32[2,64,8,2]{1,3,2,0:T(2,128)S(1)}, u32[]{:S(2)}) copy-start(f32[2,64,8,2]{1,3,2,0:T(2,128)S(1)} %get-tuple-element.1005) | copy-start | bytes 24580
  153.7 36.2 %copy-start.8 = (f32[128,1024]{1,0:T(8,128)S(1)}, f32[128,1024]{1,0:T(8,128)}, u32[]{:S(2)}) copy-start(f32[128,1024]{1,0:T(8,128)} %reshape.1109) | copy-start | bytes 1572868
  156.2 215.2 %copy-start.14 = (bf16[128,1024]{1,0:T(8,128)(2,1)}, bf16[128,1024]{1,0:T(8,128)(2,1)S(1)}, u32[]{:S(2)}) copy-start(bf16[128,1024]{1,0:T(8,128)(2,1)S(1)} %reshape.1111) | copy-start | bytes 786436
  192.1 213.7 %copy-start.5 = (f32[128,1024]{1,0:T(8,128)}, f32[128,1024]{1,0:T(8,128)S(1)}, u32[]{:S(2)}) copy-start(f32[128,1024]{1,0:T(8,128)S(1)} %get-tuple-element.1435) | copy-start | bytes 1572868
  380.3 9.1 copy-start.26
  391.0 157.1 %copy-start.10 = (f32[128,1024]{1,0:T(8,128)}, f32[128,1024]{1,0:T(8,128)S(1)}, u32[]{:S(2)}) copy-start(f32[128,1024]{1,0:T(8,128)S(1)} %multiply_add_fusion.2) | copy-start | bytes 1572868
  393.7 1219.9 %all-reduce.9.cloned.1.call-start = ((), (), s32[]{:S(2)}) async-start(), calls=%async_computation.9 | async-start | bytes 150994944
  538.8 1218.7 %reduce-scatter.5.cloned.1.call-start = ((), (), s32[]{:S(2)}) async-start(), calls=%async_computation.8 | async-start | bytes 4325376 | tf_op jit(solution)/shard_map/reduce_scatter | solution.py:386
  550.8 1354.7 %reduce-scatter.3.cloned.1.call-start = ((), (), s32[]{:S(2)}) async-start(), calls=%async_computation.7 | async-start | bytes 8650752 | tf_op jit(solution)/shard_map/reduce_scatter | solution.py:385
  (52 other events, 144.6 us)
Sparse Core Ops, SparseCore 0:
  10.8 64.8 all-gather.5
  82.9 49.1 all-gather.7
  134.9 54.9 all-gather.9
  192.7 168.5 all-gather.11
  393.8 73.0 all-gather.13
  538.9 1074.6 all-reduce.8
  1616.5 140.9 reduce-scatter.4
  1760.4 145.1 reduce-scatter.2
where the time goes:
time: 1920 us; the launch traced here: 1910 us
  waiting for transfers between devices  1280 us (67%)
  local copies, waits for them, and re-layouts  288 us (15%)
  blocking collectives  137 us (7%)
  matrix products  110 us (6%)
  other arithmetic  69.7 us (4%)
    unnamed x9, waiting for transfers between devices  734 us
    all_gather x1, waiting for transfers between devices, on_device(): lax.all_gather(ffn_weights, ('dp', 'ctx'), axis=0, tiled=True)  169 us
    reduce_scatter x1, waiting for transfers between devices, on_device(): lax.psum_scatter(in_term, ('dp', 'ctx'), scatter_dimension=0, tiled=True)  148 us
    reduce_scatter x1, waiting for transfers between devices, on_device(): lax.psum_scatter(out_term, ('dp', 'ctx'), scatter_dimension=0, tiled=True)  139 us
    unnamed x2, blocking collectives  81.1 us
    concatenate x1, local copies, waits for them, and re-layouts, unit_terms(): return jnp.concatenate([front, back[:, None]], axis=1)  79.9 us
    all_gather x1, blocking collectives, on_device(): lax.all_gather(stat_pack.astype(jnp.bfloat16), 'ctx', axis=1, tiled=True)  56.3 us
  transfers between devices with their start and end apart: 8, of which 7 were waited for; matrix products, arithmetic and copies ran while one was open for 22% of the time, Pallas kernels for 0%

commit v1 on v0

v1 whole, which is shorter than its diff:
```python
import jax
import jax.numpy as jnp
import numpy as np
from jax import lax
from jax.sharding import Mesh
from jax.sharding import PartitionSpec as P

FF = 4608
HEADS = 16
KV_HEADS = 8
HEAD_DIM = 64
GROUP = HEADS // KV_HEADS
QKV_ROWS = 2048

EPS = 1e-05
ROPE_BASE = 1000000.0
MASKED = -1e30
BF = jnp.bfloat16
F32 = jnp.float32


def root_mean(values):
    return lax.rsqrt(jnp.mean(values * values, axis=-1, keepdims=True) + EPS)


def rotate(values, cosine, sine):
    width = values.shape[-1] // 2
    first = values[..., :width]
    second = values[..., width:]
    return jnp.concatenate(
        [first * cosine - second * sine, second * cosine + first * sine], axis=-1
    )


def tables(positions):
    width = HEAD_DIM // 2
    freq = ROPE_BASE ** (-jnp.arange(width, dtype=F32) * 2.0 / HEAD_DIM)
    angle = positions.astype(F32)[..., None] * freq
    return (jnp.cos(angle), jnp.sin(angle))


def prepare(query_raw, key_raw, query_gain, key_gain, cosine, sine):
    query_norm = query_raw * root_mean(query_raw) * query_gain
    key_norm = key_raw * root_mean(key_raw) * key_gain
    return (
        rotate(query_norm, cosine[:, None], sine[:, None]),
        rotate(key_norm, cosine, sine),
    )


def norm_back(grad, normed, scale_rows, gain):
    weighted = grad * gain
    inner = jnp.mean(weighted * normed, axis=-1, keepdims=True)
    return (scale_rows * (weighted - normed * inner), jnp.sum(grad * normed, axis=0))


def dot(a, b, ca, cb):
    return lax.dot_general(a, b, (((ca,), (cb,)), ((), ())), preferred_element_type=F32)


TEAM = ("dp", "s", "q")
EVERY = ("dp", "s", "q", "g")


def spread(local, block_len):
    mine = lax.all_to_all(local, "s", 0, 0, tiled=True)
    return lax.all_gather(mine, "g", axis=0, tiled=False)


def on_device(tokens, segments, lengths, attn_in, attn_out, gains, ffn_weights, cotangent):
    batches, block_len, halves, width = tokens.shape
    seq = lax.axis_index("s")
    quarter = lax.axis_index("q")
    head = lax.axis_index("g")
    quarters = lax.axis_size("q")
    heads = lax.axis_size("g")
    ctx_count = 2 * quarters * heads
    scale = HEAD_DIM ** (-0.5)
    weight_in = lax.all_gather(attn_in, EVERY, axis=0, tiled=True)
    weight_out = lax.all_gather(attn_out, EVERY, axis=0, tiled=True)
    gain_all = lax.all_gather(gains, EVERY, axis=0, tiled=True).astype(F32)
    attn_gain = gain_all[:width]
    ffn_gain = gain_all[width : 2 * width]
    query_gain = gain_all[2 * width : 2 * width + HEAD_DIM]
    key_gain = gain_all[2 * width + HEAD_DIM :]
    head_rows = (GROUP + 2) * HEAD_DIM
    out_rows = GROUP * HEAD_DIM
    weight_head = lax.dynamic_slice_in_dim(weight_in, head * head_rows, head_rows, 0)
    weight_mix = lax.dynamic_slice_in_dim(weight_out, head * out_rows, out_rows, 0)

    inputs = spread(tokens, block_len)
    count = inputs.size // width
    inputs = inputs.reshape(count, width).astype(F32)
    cot = spread(cotangent, block_len).reshape(count, width).astype(F32)

    def places(which):
        owner_g = jnp.arange(heads, dtype=jnp.int32)[:, None, None, None]
        owner_s = jnp.arange(2, dtype=jnp.int32)[None, :, None, None]
        row = jnp.arange(block_len, dtype=jnp.int32)[None, None, :, None]
        half = jnp.arange(2, dtype=jnp.int32)[None, None, None, :]
        owner = owner_s * (quarters * heads) + which * heads + owner_g
        block = jnp.where(half == 0, owner, 2 * ctx_count - 1 - owner)
        return (
            (block * block_len + row).reshape(count),
            jnp.broadcast_to((owner * block_len + row) * 2 + half, (heads, 2, block_len, 2)).reshape(count),
        )

    docs = lax.dynamic_index_in_dim(segments, seq, 0, False).reshape(-1)
    length = lax.dynamic_index_in_dim(lengths, seq, 0, False)
    place, slot = places(quarter)
    key_place, key_slot = jax.vmap(places)(jnp.arange(quarters, dtype=jnp.int32))
    key_place = key_place.reshape(-1)
    query_doc = docs[slot]
    key_doc = docs[key_slot.reshape(-1)]
    causal = key_place[None, :] <= place[:, None]
    live = (key_place[None, :] < length) | (key_place[None, :] == place[:, None])
    mask = causal & live & (query_doc[:, None] == key_doc[None, :])
    valid = (place < length).astype(F32)[:, None]

    first_scale = root_mean(inputs)
    first_normed = inputs * first_scale
    first = (first_normed * attn_gain).astype(BF)
    projected = dot(first, weight_head, 1, 1).reshape(count, GROUP + 2, HEAD_DIM)
    cosine, sine = tables(place)

    def prepare_here(query_raw, key_raw, gain_query, gain_key):
        return prepare(query_raw, key_raw, gain_query, gain_key, cosine, sine)

    (query_rot, key_rot), prepare_pull = jax.vjp(
        prepare_here, projected[:, :GROUP], projected[:, GROUP], query_gain, key_gain
    )
    queries = query_rot.astype(BF)
    pair = jnp.stack([key_rot.astype(BF), projected[:, GROUP + 1].astype(BF)])
    pair = lax.all_gather(pair, "q", axis=1, tiled=True)
    keys, values = pair[0], pair[1]

    scores = jnp.einsum("qjd,kd->jqk", queries, keys, preferred_element_type=F32) * scale
    scores = jnp.where(mask[None], scores, MASKED)
    peak = jnp.max(scores, axis=-1, keepdims=True)
    expo = jnp.where(mask[None], jnp.exp(scores - peak), 0.0)
    weights = expo / jnp.sum(expo, axis=-1, keepdims=True)
    attended = jnp.einsum("jqk,kd->qjd", weights.astype(BF), values, preferred_element_type=F32)
    mixed_here = attended.astype(BF).reshape(count, out_rows)
    mixed = lax.all_gather(mixed_here, "g", axis=1, tiled=True)
    state = inputs + dot(mixed, weight_out, 1, 0)
    second_scale = root_mean(state)
    second_normed = state * second_scale
    second = (second_normed * ffn_gain).astype(BF)
    grad_out = cot * valid
    grad_low = grad_out.astype(BF)

    units = lax.all_gather(ffn_weights, TEAM, axis=0, tiled=True)
    unit_gate, unit_up, unit_down = units[:, 0], units[:, 1], units[:, 2]
    gate = dot(second, unit_gate, 1, 1)
    upward = dot(second, unit_up, 1, 1)
    sigmoid = jax.nn.sigmoid(gate)
    hidden = (gate * sigmoid * upward).astype(BF)
    d_hidden = dot(grad_low, unit_down, 1, 1)
    d_gate = (d_hidden * upward * sigmoid * (1.0 + gate * (1.0 - sigmoid))).astype(BF)
    d_up = (d_hidden * gate * sigmoid).astype(BF)
    d_second = dot(d_gate, unit_gate, 1, 0) + dot(d_up, unit_up, 1, 0)
    own = count // heads

    def gathered(values):
        return lax.psum_scatter(values.astype(BF), "g", scatter_dimension=0, tiled=True).astype(F32)

    def own_rows(values):
        return lax.dynamic_slice_in_dim(values, head * own, own, 0)

    def home(values):
        back = values.reshape(2, block_len, halves, width)
        return lax.all_to_all(back, "s", 0, 0, tiled=True)

    ffn_sum = gathered(dot(hidden, unit_down, 1, 0))
    block_out = home((own_rows(state) + ffn_sum).astype(BF))
    ffn_grad = lax.psum_scatter(
        jnp.stack([dot(d_gate, second, 0, 0), dot(d_up, second, 0, 0), dot(hidden, grad_low, 0, 0)], axis=1),
        TEAM,
        scatter_dimension=0,
        tiled=True,
    )
    norm_grad, ffn_gain_grad = norm_back(
        gathered(d_second), own_rows(second_normed), own_rows(second_scale), ffn_gain
    )
    state_grad = own_rows(grad_out) + norm_grad
    attended_grad = lax.all_gather(state_grad.astype(BF), "g", axis=0, tiled=True)
    mixed_grad = dot(attended_grad, weight_mix, 1, 1).astype(BF)
    out_term = dot(mixed_here, attended_grad, 0, 0)
    mixed_grad = mixed_grad.reshape(count, GROUP, HEAD_DIM)
    delta = jnp.sum(mixed_grad.astype(F32) * attended, axis=-1).T[:, :, None]
    pulled = jnp.einsum("qjd,kd->jqk", mixed_grad, values, preferred_element_type=F32)
    score_grad = (weights * (pulled - delta)).astype(BF)
    query_grad = jnp.einsum("jqk,kd->qjd", score_grad, keys, preferred_element_type=F32) * scale
    key_grad = jnp.einsum("jqk,qjd->kd", score_grad, queries, preferred_element_type=F32) * scale
    value_grad = jnp.einsum("jqk,qjd->kd", weights.astype(BF), mixed_grad, preferred_element_type=F32)
    if quarters > 1:
        key_grad = lax.psum_scatter(key_grad, "q", scatter_dimension=0, tiled=True)
        value_grad = lax.psum_scatter(value_grad, "q", scatter_dimension=0, tiled=True)
    query_raw_grad, key_raw_grad, query_gain_grad, key_gain_grad = prepare_pull((query_grad, key_grad))
    projected_grad = jnp.concatenate(
        [query_raw_grad.reshape(count, out_rows), key_raw_grad, value_grad], axis=1
    ).astype(BF)
    first_grad = gathered(dot(projected_grad, weight_head, 1, 0))
    in_term = dot(projected_grad, first, 0, 0)
    input_norm_grad, attn_gain_grad = norm_back(
        first_grad, own_rows(first_normed), own_rows(first_scale), attn_gain
    )
    tokens_grad = home(state_grad + input_norm_grad)
    gain_term = jnp.concatenate([attn_gain_grad, ffn_gain_grad, query_gain_grad, key_gain_grad])

    def placed(term, rows):
        whole = jnp.zeros((rows, width), F32)
        return lax.dynamic_update_slice_in_dim(whole, term, head * term.shape[0], 0)

    return (
        block_out,
        tokens_grad,
        lax.psum_scatter(placed(in_term, QKV_ROWS), EVERY, scatter_dimension=0, tiled=True),
        lax.psum_scatter(placed(out_term, HEADS * HEAD_DIM), EVERY, scatter_dimension=0, tiled=True),
        lax.psum_scatter(gain_term, EVERY, scatter_dimension=0, tiled=True),
        ffn_grad,
    )


def solution(mesh):
    dp, ctx = mesh.devices.shape
    team = Mesh(mesh.devices.reshape(dp, 2, ctx // (2 * KV_HEADS), KV_HEADS), EVERY)
    ring = ("s", "q", "g")
    placed = (
        P("dp", ring, None, None),
        P("dp", None, None),
        P("dp"),
        P(EVERY, None),
        P(EVERY, None),
        P(EVERY),
        P(EVERY, None, None),
        P("dp", ring, None, None),
    )
    return jax.shard_map(
        on_device,
        mesh=team,
        in_specs=placed,
        out_specs=(
            P("dp", ring, None, None),
            P("dp", ring, None, None),
            P(EVERY, None),
            P(EVERY, None),
            P(EVERY),
            P(EVERY, None, None),
        ),
        check_vma=False,
    )
```

time: 1920 us -> 886 us (0.46)
  waiting for transfers between devices: 1280 us -> 564 us
  local copies, waits for them, and re-layouts: 288 us -> 58.3 us
  matrix products: 110 us -> 57.2 us
  other arithmetic: 69.7 us -> 50.2 us
    unnamed x9 -> x13, waiting for transfers between devices: 734 us -> 1.91 us
    reduce_scatter x2 -> x6, waiting for transfers between devices: 288 us -> 406 us  [the longest x1 148 us: on_device(): lax.psum_scatter(placed(in_term, QKV_ROWS), EVERY, scatter_dimension=0, t...]
    all_gather x5 -> x7, waiting for transfers between devices: 262 us -> 156 us  [the longest x1 67.7 us: on_device(): units = lax.all_gather(ffn_weights, TEAM, axis=0, tiled=True)]
    concatenate x11 -> x0, local copies, waits for them, and re-layouts: 82.2 us -> none  [the longest x1 79.9 us: unit_terms(): return jnp.concatenate([front, back[:, None]], axis=1)]
    dot_general x28 -> x20, matrix products: 110 us -> 50.9 us  [the longest x15 40.8 us: dot(): lax.dot_general(a, b, (((ca,), (cb,)), ((), ())), preferred_element_type=...]
    all_gather x1 -> x0, blocking collectives: 56.3 us -> none  [on_device(): lax.all_gather(stat_pack.astype(jnp.bfloat16), 'ctx', axis=1, tiled=True)]
    convert_element_type x27 -> x6, local copies, waits for them, and re-layouts: 67.2 us -> 25 us  [the longest x2 10.3 us: on_device(): inputs = inputs.reshape(count, width).astype(F32)]
    concatenate x5 -> x0, other arithmetic: 39.3 us -> none  [the longest x1 38 us: unit_terms(): return jnp.concatenate([front, back[:, None]], axis=1)]
  transfers between devices with their start and end apart: 8 -> 15, of which waited for: 7 -> 10; matrix products, arithmetic and copies ran while one was open for 22% -> 15% of each run, Pallas kernels for 0% -> 0%
where the time goes in v1:
time: 886 us; the launch traced here: 877 us
  waiting for transfers between devices  564 us (64%)
  blocking collectives  124 us (14%)
  local copies, waits for them, and re-layouts  58.3 us (7%)
  matrix products  57.2 us (6%)
  other arithmetic  50.2 us (6%)
  between operations  15.1 us (2%)
    reduce_scatter x1, waiting for transfers between devices, on_device(): lax.psum_scatter(placed(in_term, QKV_ROWS), EVERY, scatter_dimension=0, t...  148 us
    reduce_scatter x1, waiting for transfers between devices, on_device(): lax.psum_scatter(placed(out_term, HEADS * HEAD_DIM), EVERY, scatter_dimen...  143 us
    unnamed x2, blocking collectives  98.2 us
    reduce_scatter x1, waiting for transfers between devices, on_device(): lax.psum_scatter(jnp.stack([dot(d_gate, second, 0, 0), dot(d_up, second,...  77 us
    all_gather x1, waiting for transfers between devices, on_device(): units = lax.all_gather(ffn_weights, TEAM, axis=0, tiled=True)  67.7 us
    dot_general x15, matrix products, dot(): lax.dot_general(a, b, (((ca,), (cb,)), ((), ())), preferred_element_type=...  40.8 us
    all_gather x1, waiting for transfers between devices, on_device(): weight_out = lax.all_gather(attn_out, EVERY, axis=0, tiled=True)  39 us
    reduce_scatter x3, waiting for transfers between devices, gathered(): lax.psum_scatter(values.astype(BF), 'g', scatter_dimension=0, tiled=True)  37.9 us
  transfers between devices with their start and end apart: 15, of which 10 were waited for; matrix products, arithmetic and copies ran while one was open for 15% of the time, Pallas kernels for 0%

profile of v1, /device:TPU:0, one launch (start us, length us, event | category | flops | bytes accessed | tf_op | source)
XLA Modules:
  0.0 876.6 jit_solution(6487094855781637210)
XLA Ops:
  8.2 14.1 %all_to_all.20 = bf16[2,32,2,1024]{3,1,2,0:T(8,128)(2,1)} all-to-all(bf16[2,32,2,1024]{3,1,2,0:T(8,128)(2,1)S(1)} %copy.73), channel_id=1, replica_groups=mesh['dp'=2,'s'=2,'q'=1,'g'=8] {'s'}, dimensions={0} | all-to-all | bytes 524288 | tf_op jit(solution)/shard_map/all_to_all | solution.py:66
  24.2 11.5 %all_to_all.21 = bf16[2,32,2,1024]{3,1,2,0:T(8,128)(2,1)} all-to-all(bf16[2,32,2,1024]{3,1,2,0:T(8,128)(2,1)S(1)} %copy.80), channel_id=1, replica_groups=mesh['dp'=2,'s'=2,'q'=1,'g'=8] {'s'}, dimensions={0} | all-to-all | bytes 524288 | tf_op jit(solution)/shard_map/all_to_all | solution.py:66
  37.2 38.1 %all-reduce.4 = bf16[2176]{0:T(1024)(128)(2,1)S(1)} all-reduce(bf16[2176]{0:T(1024)(128)(2,1)S(1)} %dynamic-update-slice), channel_id=1, replica_groups=mesh['dp'=2,'s'=2,'q'=1,'g'=8] {'dp','s','q','g'}, use_global_device_ids=true, to_apply=%add.4 | all-reduce | flops 2176 | bytes 8704
  90.9 7.9 fusion.6
  101.0 8.6 all-gather.10.cloned.1.call-done
  115.4 6.3 fusion.83
  122.4 4.7 fusion.10
  138.1 6.1 reshape.641
  151.6 39.0 %all-gather.14.cloned.1.call-done = bf16[1024,1024]{1,0:T(8,128)(2,1)} async-done(((bf16[32,1024]{1,0:T(8,128)(2,1)}), bf16[1024,1024]{1,0:T(8,128)(2,1)}) %all-gather.14.cloned.1.call-update) | async-done | bytes 2097168 | tf_op jit(solution)/shard_map/all_gather | solution.py:80
  190.6 22.4 %all-gather.12.cloned.1.call-done = bf16[1024,1024]{0,1:T(8,128)(2,1)} async-done(((bf16[1024,128]{0,1:T(8,128)(2,1)}), bf16[1024,1024]{0,1:T(8,128)(2,1)}) %all-gather.12.cloned.1.call-update) | async-done | bytes 2097168 | tf_op jit(solution)/shard_map/all_gather | solution.py:144
  213.1 6.2 multiply_reduce_fusion
  223.8 67.7 %all-gather.16.cloned.1.call-done = bf16[576,3,1024]{2,0,1:T(8,128)(2,1)} async-done(((bf16[144,3,1024]{2,0,1:T(8,128)(2,1)}), bf16[576,3,1024]{2,0,1:T(8,128)(2,1)}) %all-gather.16.cloned.1.call-update) | async-done | bytes 3538960 | tf_op jit(solution)/shard_map/all_gather | solution.py:152
  310.5 6.1 reshape.642
  316.6 4.7 broadcast_multiply_fusion.1
  322.1 13.5 %reduce-scatter.9.cloned.1.call-done = bf16[128,1024]{1,0:T(8,128)(2,1)} async-done(((bf16[1024,1024]{1,0:T(8,128)(2,1)}), bf16[128,1024]{1,0:T(8,128)(2,1)}) %reduce-scatter.9.cloned.1.call-update) | async-done | bytes 262160 | tf_op jit(solution)/shard_map/reduce_scatter | solution.py:165
  339.1 4.5 convolution_convert_fusion.1
  343.7 18.3 %all-gather.18.cloned.1.call-done = bf16[1024,1024]{1,0:T(8,128)(2,1)} async-done(((bf16[128,1024]{1,0:T(8,128)(2,1)}), bf16[1024,1024]{1,0:T(8,128)(2,1)}) %all-gather.18.cloned.1.call-update) | async-done | bytes 2097168 | tf_op jit(solution)/shard_map/all_gather | solution.py:186
  364.5 4.7 fusion.2
  395.5 4.6 broadcast_in_dim.231
  407.8 24.4 %reduce-scatter.11.cloned.1.call-done = bf16[128,1024]{1,0:T(8,128)(2,1)} async-done(((bf16[1024,1024]{1,0:T(8,128)(2,1)}), bf16[128,1024]{1,0:T(8,128)(2,1)}) %reduce-scatter.11.cloned.1.call-update) | async-done | bytes 262160 | tf_op jit(solution)/shard_map/reduce_scatter | solution.py:165
  440.0 60.1 %all-reduce.5 = f32[2176]{0:T(1024)S(1)} all-reduce(f32[2176]{0:T(1024)S(1)} %concatenate.22), channel_id=9, replica_groups=mesh['dp'=2,'s'=2,'q'=1,'g'=8] {'dp','s','q','g'}, use_global_device_ids=true, to_apply=%region_20.21.clone | all-reduce | flops 2176 | bytes 17408
  500.6 77.0 %reduce-scatter.17.cloned.1.call-done = f32[144,3,1024]{2,0,1:T(8,128)} async-done(((f32[576,3,1024]{2,0,1:T(8,128)}), f32[144,3,1024]{2,0,1:T(8,128)}) %reduce-scatter.17.cloned.1.call-update) | async-done | bytes 1769488 | tf_op jit(solution)/shard_map/reduce_scatter | solution.py:176
  577.6 142.7 %reduce-scatter.15.cloned.1.call-done = f32[32,1024]{1,0:T(8,128)} async-done(((f32[1024,1024]{1,0:T(8,128)}), f32[32,1024]{1,0:T(8,128)}) %reduce-scatter.15.cloned.1.call-update) | async-done | bytes 131088 | tf_op jit(solution)/shard_map/reduce_scatter | solution.py:219
  720.3 148.0 %reduce-scatter.13.cloned.1.call-done = f32[64,1024]{1,0:T(8,128)} async-done(((f32[2048,1024]{1,0:T(8,128)}), f32[64,1024]{1,0:T(8,128)}) %reduce-scatter.13.cloned.1.call-update) | async-done | bytes 262160 | tf_op jit(solution)/shard_map/reduce_scatter | solution.py:218
  (238 shorter events, 120.4 us)
Async XLA Ops:
  7.2 69.2 %copy-start = (s32[2,512,2]{1,2,0:T(2,128)S(1)}, s32[2,512,2]{1,2,0:T(2,128)}, u32[]{:S(2)}) copy-start(s32[2,512,2]{1,2,0:T(2,128)} %param.9) | copy-start | bytes 24580
  7.2 70.2 %copy-start.50 = (s32[2]{0:T(128)S(1)}, s32[2]{0:T(128)}, u32[]{:S(2)}) copy-start(s32[2]{0:T(128)} %param.10) | copy-start | bytes 28
  7.2 79.1 %all-gather.20.cloned.1.call-start = ((), (), s32[]{:S(2)}) async-start(), calls=%async_computation.21 | async-start | bytes 2359296 | tf_op jit(solution)/shard_map/all_gather | solution.py:67
  22.4 87.3 %all-gather.10.cloned.1.call-start = ((), (), s32[]{:S(2)}) async-start(), calls=%async_computation.10 | async-start | bytes 4325376 | tf_op jit(solution)/shard_map/all_gather | solution.py:79
  23.1 121.1 %all-gather.22.cloned.1.call-start = ((), (), s32[]{:S(2)}) async-start(), calls=%async_computation.22 | async-start | bytes 2359296 | tf_op jit(solution)/shard_map/all_gather | solution.py:67
  35.6 155.0 %all-gather.14.cloned.1.call-start = ((), (), s32[]{:S(2)}) async-start(), calls=%async_computation.12 | async-start | bytes 2162688 | tf_op jit(solution)/shard_map/all_gather | solution.py:80
  36.2 176.9 %all-gather.12.cloned.1.call-start = ((), (), s32[]{:S(2)}) async-start(), calls=%async_computation.11 | async-start | bytes 2359296 | tf_op jit(solution)/shard_map/all_gather | solution.py:144
  75.8 38.1 %copy-start.43 = (f32[64]{0:T(128)}, f32[64]{0:T(128)S(1)}, u32[]{:S(2)}) copy-start(f32[64]{0:T(128)S(1)} %get-tuple-element.29) | copy-start | bytes 772
  130.8 160.7 %all-gather.16.cloned.1.call-start = ((), (), s32[]{:S(2)}) async-start(), calls=%async_computation.13 | async-start | bytes 4423680 | tf_op jit(solution)/shard_map/all_gather | solution.py:152
  131.4 204.1 %reduce-scatter.9.cloned.1.call-start = ((), (), s32[]{:S(2)}) async-start(), calls=%async_computation.15 | async-start | bytes 2359296 | tf_op jit(solution)/shard_map/reduce_scatter | solution.py:165
  223.8 67.7 %copy-start.15 = (bf16[1024,1024]{1,0:T(8,128)(2,1)}, bf16[1024,1024]{1,0:T(8,128)(2,1)S(1)}, u32[]{:S(2)}) copy-start(bf16[1024,1024]{1,0:T(8,128)(2,1)S(1)} %get-tuple-element.16) | copy-start | bytes 6291460
  306.1 55.9 %all-gather.18.cloned.1.call-start = ((), (), s32[]{:S(2)}) async-start(), calls=%async_computation.16 | async-start | bytes 2359296 | tf_op jit(solution)/shard_map/all_gather | solution.py:186
  316.6 22.5 %copy-start.54 = (bf16[1024,576]{0,1:T(8,128)(2,1)S(1)}, bf16[1024,576]{0,1:T(8,128)(2,1)}, u32[]{:S(2)}) copy-start(bf16[1024,576]{0,1:T(8,128)(2,1)} %get-tuple-element.20) | copy-start | bytes 3538948
  339.0 63.0 %reduce-scatter.7.cloned.1.call-start = ((), (), s32[]{:S(2)}) async-start(), calls=%async_computation.14 | async-start | bytes 2359296 | tf_op jit(solution)/shard_map/reduce_scatter | solution.py:165
  339.1 22.9 %copy-start.11 = (f32[1024,2,64]{0,2,1:T(8,128)S(1)}, f32[1024,2,64]{0,2,1:T(8,128)}, u32[]{:S(2)}) copy-start(f32[1024,2,64]{0,2,1:T(8,128)} %get-tuple-element.41) | copy-start | bytes 1572868
  343.7 20.8 %copy-start.46 = (f32[2,1024]{1,0:T(2,128)S(1)}, f32[2,1024]{1,0:T(2,128)}, u32[]{:S(2)}) copy-start(f32[2,1024]{1,0:T(2,128)} %copy-done.45) | copy-start | bytes 24580
  343.7 88.5 %reduce-scatter.11.cloned.1.call-start = ((), (), s32[]{:S(2)}) async-start(), calls=%async_computation.17 | async-start | bytes 2359296 | tf_op jit(solution)/shard_map/reduce_scatter | solution.py:165
  378.0 199.6 %reduce-scatter.17.cloned.1.call-start = ((), (), s32[]{:S(2)}) async-start(), calls=%async_computation.20 | async-start | bytes 8847360 | tf_op jit(solution)/shard_map/reduce_scatter | solution.py:176
  388.8 331.6 %reduce-scatter.15.cloned.1.call-start = ((), (), s32[]{:S(2)}) async-start(), calls=%async_computation.19 | async-start | bytes 4325376 | tf_op jit(solution)/shard_map/reduce_scatter | solution.py:219
  392.7 475.6 %reduce-scatter.13.cloned.1.call-start = ((), (), s32[]{:S(2)}) async-start(), calls=%async_computation.18 | async-start | bytes 8650752 | tf_op jit(solution)/shard_map/reduce_scatter | solution.py:218
  401.8 31.7 %copy-start.13 = (bf16[128,1024]{1,0:T(8,128)(2,1)S(1)}, bf16[128,1024]{1,0:T(8,128)(2,1)}, u32[]{:S(2)}) copy-start(bf16[128,1024]{1,0:T(8,128)(2,1)} %reduce-scatter.9.cloned.1.call-done) | copy-start | bytes 786436
  404.0 32.4 %all-to-all-start.1 = ((bf16[2,32,2,1024]{3,2,1,0:T(2,128)(2,1)}), bf16[2,32,2,1024]{3,2,1,0:T(2,128)(2,1)S(1)}, u32[]{:S(2)}, u32[]{:S(2)}) async-start(bf16[2,32,2,1024]{3,2,1,0:T(2,128)(2,1)} %reshape.637), calls=%async_computation.2 | async-start | bytes 524288 | tf_op jit(solution)/shard_map/all_to_all | solution.py:172
  407.8 462.0 %copy-start.1 = (s32[2,512,2]{1,2,0:T(2,128)S(1)}, s32[2,512,2]{1,2,0:T(2,128)}, u32[]{:S(2)}) copy-start(s32[2,512,2]{1,2,0:T(2,128)} %param.9) | copy-start | bytes 24580
  436.4 64.3 %all-to-all-start.3 = ((f32[2,32,2,1024]{3,2,1,0:T(2,128)}), f32[2,32,2,1024]{3,2,1,0:T(2,128)S(1)}, u32[]{:S(2)}, u32[]{:S(2)}) async-start(f32[2,32,2,1024]{3,2,1,0:T(2,128)} %reshape.640), calls=%async_computation.6 | async-start | bytes 1048576 | tf_op jit(solution)/shard_map/all_to_all | solution.py:172
  (47 other events, 150.5 us)
Sparse Core Ops, SparseCore 0:
  22.5 22.9 all-gather.19
  48.3 61.2 all-gather.9
  111.2 20.1 all-gather.21
  134.1 56.5 all-gather.13
  192.7 20.3 all-gather.11
  214.8 76.6 all-gather.15
  306.3 29.2 reduce-scatter.8
  339.2 22.7 all-gather.17
  364.3 30.3 reduce-scatter.6
  396.9 35.2 reduce-scatter.10
  435.8 141.7 reduce-scatter.16
  580.3 139.9 reduce-scatter.14
  723.2 145.0 reduce-scatter.12

commit v2 on v1

--- a/solution.py
+++ b/solution.py
@@ -2,6 +2,8 @@
 import jax.numpy as jnp
 import numpy as np
 from jax import lax
+from jax.experimental import pallas as pl
+from jax.experimental.pallas import tpu as pltpu
 from jax.sharding import Mesh
 from jax.sharding import PartitionSpec as P
 
@@ -222,31 +224,751 @@
     )
 
 
+LANES = 128
+HALF_LANES = 64
+
+
+def _nt(a, b):
+    return lax.dot_general(a, b, (((1,), (1,)), ((), ())), preferred_element_type=F32)
+
+
+def _nn(a, b):
+    return lax.dot_general(a, b, (((1,), (0,)), ((), ())), preferred_element_type=F32)
+
+
+def _tn(a, b):
+    return lax.dot_general(a, b, (((0,), (0,)), ((), ())), preferred_element_type=F32)
+
+
+MESH = pl.DeviceIdType.MESH
+COPIES = 320
+
+
+class Wires:
+    def __init__(self, sems):
+        self.sems = sems
+        self.used = 0
+        self.pending = []
+
+    def sem(self):
+        self.used += 1
+        return self.sems.at[self.used - 1]
+
+    def send(self, src, dst, to, arrives):
+        copy = pltpu.make_async_remote_copy(
+            src_ref=src, dst_ref=dst, send_sem=self.sem(), recv_sem=arrives,
+            device_id=to, device_id_type=MESH,
+        )
+        copy.start()
+        self.pending.append(copy)
+        return copy
+
+    def local(self, src, dst, arrives):
+        copy = pltpu.make_async_copy(src, dst, arrives)
+        copy.start()
+        return copy
+
+    def arrived(self, ref, sem):
+        pltpu.make_async_copy(ref, ref, sem).wait()
+
+    def finish(self, copies=None):
+        copies = list(self.pending if copies is None else copies)
+        for copy in copies:
+            copy.wait_send()
+        done = {id(copy) for copy in copies}
+        self.pending = [copy for copy in self.pending if id(copy) not in done]
+
+
+def block_kernel(
+    tok, cot, win, wout, gain, wffn, doc_col, doc_row, length, cos_t, sin_t,
+    o_block, o_tokens, o_in, o_out, o_gain, o_ffn,
+    x, rel_t, rel_c, wa, w2, wall, wf, gb, grow, first2, raw, po,
+    q0, q1, kk, vv, prob, att, mxs, mix, sec2, dy2, acts, asend,
+    dsb, osb, dsr, osr, gr, gs, gt, dstate, dmb, daf, dmix,
+    dkk, dvv, dqq, dpj, dpx, dfb, dfr, igs, ags, agr, agz, agt,
+    bos, obs, bor, tgs, tgr, gg, ggq, gsum, ggy, ggz, sems,
+):
+    dp = lax.axis_index("dp")
+    c = lax.axis_index("ctx")
+    zh = lax.div(c, 8)
+    g = lax.rem(c, 8)
+    j = lax.div(g, 2)
+    k = lax.rem(c, 2)
+    chips = (j, j + 1 - 2 * lax.rem(j, 2), j + 2 - 4 * lax.div(j, 2), 3 - j)
+    cores = (k, 1 - k)
+
+    def quad(d, e):
+        return (dp, zh * 8 + 2 * chips[d] + cores[e])
+
+    sib = quad(0, 1)
+    zp = (dp, lax.rem(c + 8, 16))
+    zps = (dp, 8 * (1 - zh) + 2 * j + 1 - k)
+    yp = (1 - dp, c)
+    team = 2 * dp + zh
+    team_y = 2 * (1 - dp) + zh
+    team_z = 2 * dp + 1 - zh
+    team_d = 3 - team
+    czp = lax.rem(c + 8, 16)
+    w = Wires(sems)
+    others = [(d, e) for d in range(4) for e in range(2) if (d, e) != (0, 0)]
+
+    def piece(chip):
+        return chip + k * (3 - 2 * chip)
+
+    def row_block(owner, half):
+        return owner + half * (15 - 2 * owner)
+
+    barrier = pltpu.get_barrier_semaphore()
+    peers = [quad(d, e) for d, e in others] + [zp, zps, yp]
+    for peer in peers:
+        pl.semaphore_signal(barrier, inc=1, device_id=peer, device_id_type=MESH)
+    pl.semaphore_wait(barrier, len(peers))
+
+    def scatter_rows(src_of, dst_of, owner, sem):
+        for e in range(2):
+            half = cores[e]
+            start = pl.multiple_of(row_block(owner, half) * 32, 32)
+            for d in range(4):
+                dst = dst_of(half, start)
+                if (d, e) == (0, 0):
+                    w.local(src_of(half), dst, sem)
+                else:
+                    w.send(src_of(half), dst, quad(d, e), sem)
+
+    x_dst = lambda half, start: x.at[pl.ds(start, 32)]
+    dy_dst = lambda half, start: dy2.at[pl.ds(pl.multiple_of(512 * half + start, 32), 32)]
+    s_rel_t, s_rel_c, s_x0, s_x1, s_c0, s_c1 = (w.sem() for _ in range(6))
+    w.send(tok.at[1 - zh], rel_t, zp, s_rel_t)
+    s_wa = [w.sem() for _ in range(4)]
+    s_wo = [w.sem() for _ in range(4)]
+    s_g = [w.sem() for _ in range(4)]
+    exchanges = (
+        (win, lambda t: wa.at[t], s_wa),
+        (gain, lambda t: gb.at[t, g], s_g),
+        (wout, lambda t: wall.at[t, j, k], s_wo),
+    )
+    for src, at, sem in exchanges[:2]:
+        w.send(src, at(team), yp, sem[0])
+        w.send(src, at(team), zp, sem[1])
+        w.local(src, at(team), sem[3])
+    scatter_rows(lambda half: tok.at[zh, half], x_dst, c, s_x0)
+    src, at, sem = exchanges[2]
+    w.send(src, at(team), yp, sem[0])
+    w.send(src, at(team), zp, sem[1])
+    w.local(src, at(team), sem[3])
+    held = []
+    s_f = [[[w.sem() for _ in range(3)] for _ in range(4)] for _ in range(2)]
+
+    def unit(kind, parity, slot):
+        return wf.at[kind, parity, pl.ds(144 * slot, 144)]
+
+    for kind in range(3):
+        w.send(wffn.at[kind], unit(kind, k, 1), yp, s_f[0][1][kind])
+        w.local(wffn.at[kind], unit(kind, k, 0), s_f[0][0][kind])
+        w.send(wffn.at[kind], unit(kind, k, 0), sib, s_f[1][0][kind])
+    for kind in range(3):
+        wf[kind, 0, pl.ds(576, 64), :] = jnp.zeros((64, 1024), BF)
+        wf[kind, 1, pl.ds(576, 64), :] = jnp.zeros((64, 1024), BF)
+
+    w.arrived(rel_t, s_rel_t)
+    scatter_rows(lambda half: rel_t.at[half], x_dst, czp, s_x1)
+    for src, at, sem in exchanges[:2]:
+        w.arrived(at(team_z), sem[1])
+        w.send(at(team_z), at(team_z), yp, sem[2])
+    w.send(cot.at[1 - zh], rel_c, zp, s_rel_c)
+    for kind in range(3):
+        w.send(wffn.at[kind], unit(kind, k, 2), zp, s_f[0][2][kind])
+    for src, at, sem in exchanges[:2]:
+        w.arrived(at(team_y), sem[0])
+        w.arrived(at(team_d), sem[2])
+        w.arrived(at(team), sem[3])
+    s_w2 = w.sem()
+    s_gq = w.sem()
+    w2_rows = pl.ds(pl.multiple_of(64 * g, 64), 64)
+    w.local(wa.at[j], w2.at[w2_rows], s_w2)
+    for d, e in others:
+        w.send(wa.at[chips[d]], w2.at[w2_rows], quad(d, e), s_w2)
+        w.send(gb.at[:, g], gb.at[:, g], quad(d, e), s_gq)
+    scatter_rows(lambda half: cot.at[zh, half], dy_dst, c, s_c0)
+    src, at, sem = exchanges[2]
+    w.arrived(at(team_z), sem[1])
+    w.send(at(team_z), at(team_z), yp, sem[2])
+
+    lane = lax.broadcasted_iota(jnp.int32, (1, LANES), 1)
+    low_row = lane < HALF_LANES
+    w.arrived(gb.at[:, pl.ds(0, 7)], s_gq)
+    chunks = [jnp.zeros((1, LANES), F32) for _ in range(18)]
+    for i in range(32):
+        row = gb[i // 8, i % 8, 0:1, :]
+        place, shift = divmod(68 * i, LANES)
+        moved = pltpu.roll(row, shift, 1) if shift else row
+        chunks[place] = chunks[place] + jnp.where(lane >= shift, moved, 0.0)
+        if shift + 68 > LANES:
+            chunks[place + 1] = chunks[place + 1] + jnp.where(lane < shift, moved, 0.0)
+    for n in range(8):
+        grow[0:1, LANES * n : LANES * (n + 1)] = chunks[n]
+        grow[1:2, LANES * n : LANES * (n + 1)] = chunks[8 + n]
+    flipped = pltpu.roll(chunks[16], HALF_LANES, 1)
+    grow[2:3, 0:LANES] = jnp.where(low_row, chunks[16], flipped)
+    grow[2:3, LANES : 2 * LANES] = jnp.where(low_row, flipped, chunks[16])
+    attn_gain = grow[0:1, :]
+    ffn_gain = grow[1:2, :]
+    query_gain = grow[2:3, 0:LANES]
+    key_gain = grow[2:3, LANES : 2 * LANES]
+
+    my_rows = pl.multiple_of(512 * k, 512)
+    other_rows = pl.multiple_of(512 * (1 - k), 512)
+    w.arrived(x.at[pl.ds(0, 256)], s_x0)
+    w.arrived(x.at[pl.ds(256, 256)], s_x1)
+    w.arrived(w2, s_w2)
+    own_head = pl.ds(pl.multiple_of(256 * k, 256), 256)
+    sib_head = pl.ds(pl.multiple_of(256 * (1 - k), 256), 256)
+
+    def project(t, carry):
+        rows = pl.multiple_of(t * 256, 256)
+        values = x[pl.ds(rows, 256), :].astype(F32)
+        scale = lax.rsqrt(jnp.mean(values * values, axis=1, keepdims=True) + EPS)
+        first = (values * scale * attn_gain).astype(BF)
+        mine = pl.multiple_of(my_rows + rows, 256)
+        first2[pl.ds(mine, 256), :] = first
+        po[pl.ds(rows, 256), :] = _nt(first, w2[sib_head, :])
+        raw[pl.ds(mine, 256), :] = _nt(first, w2[own_head, :])
+        return carry
+
+    lax.fori_loop(0, 2, project, 0)
+    s_raw, s_first = w.sem(), w.sem()
+    w.send(po, raw.at[pl.ds(my_rows, 512)], sib, s_raw)
+
+    src, at, sem = exchanges[2]
+    w.arrived(at(team_y), sem[0])
+    w.arrived(at(team_d), sem[2])
+    w.arrived(at(team), sem[3])
+    s_wq, s_ws = [w.sem() for _ in range(3)], w.sem()
+    for d in (1, 2, 3):
+        w.send(wall.at[:, j, k], wall.at[:, j, k], quad(d, 0), s_wq[d - 1])
+    w.arrived(rel_c, s_rel_c)
+    scatter_rows(lambda half: rel_c.at[half], dy_dst, czp, s_c1)
+
+    low = lax.broadcasted_iota(jnp.int32, (256, LANES), 1) < HALF_LANES
+    quarter = lax.rem(lax.broadcasted_iota(jnp.int32, (256, LANES), 1), HALF_LANES) < 32
+
+    def swap(v):
+        return jnp.where(quarter, pltpu.roll(v, 96, 1), pltpu.roll(v, 32, 1))
+
+    def head_sum(v):
+        first = jnp.sum(jnp.where(low, v, 0.0), axis=1, keepdims=True)
+        second = jnp.sum(jnp.where(low, 0.0, v), axis=1, keepdims=True)
+        return jnp.where(low, first, second)
+
+    def inverse_root(v):
+        return lax.rsqrt(head_sum(v * v) * (1.0 / HEAD_DIM) + EPS)
+
+    w.arrived(raw.at[pl.ds(0, 512)], s_raw)
+
+    def rotate_rows(t, carry):
+        rows = pl.ds(pl.multiple_of(t * 256, 256), 256)
+        cosine, sine = cos_t[rows, :], sin_t[rows, :]
+        query = raw[rows, 0:LANES]
+        both = raw[rows, LANES : 2 * LANES]
+        query = query * inverse_root(query) * query_gain
+        query = (query * cosine + swap(query) * sine) * (HEAD_DIM**-0.5)
+        q0[rows, :] = jnp.where(low, query, 0.0).astype(BF)
+        q1[rows, :] = jnp.where(low, 0.0, query).astype(BF)
+        key = both * inverse_root(both) * key_gain
+        key = key * cosine + swap(key) * sine
+        kk[rows, :] = jnp.where(low, key, pltpu.roll(key, HALF_LANES, 1)).astype(BF)
+        vv[rows, :] = jnp.where(low, pltpu.roll(both, HALF_LANES, 1), both).astype(BF)
+        return carry
+
+    lax.fori_loop(0, 4, rotate_rows, 0)
+    w.send(first2.at[pl.ds(my_rows, 512)], first2.at[pl.ds(my_rows, 512)], sib, s_first)
+
+    s_mix = w.sem()
+    head_lanes = pl.ds(pl.multiple_of(LANES * g, LANES), LANES)
+
+    def forward_tile(t):
+        lo, n = 256 * t, 256 * (t + 1)
+        place = lax.broadcasted_iota(jnp.int32, (256, n), 0) + lo
+        key_place = lax.broadcasted_iota(jnp.int32, (256, n), 1)
+        same = doc_col[lo : lo + 256, :] == doc_row[0:1, 0:n]
+        mask = (same & (key_place <= place)) | (key_place == place)
+        outs = []
+        for h, q in enumerate((q0, q1)):
+            scores = jnp.where(mask, _nt(q[lo : lo + 256, :], kk[0:n, :]), MASKED)
+            peak = jnp.max(scores, axis=1, keepdims=True)
+            expo = jnp.exp(scores - peak)
+            weights = (expo * (1.0 / jnp.sum(expo, axis=1, keepdims=True))).astype(BF)
+            prob[h, lo : lo + 256, 0:n] = weights
+            outs.append(_nn(weights, vv[0:n, :]))
+        attended = jnp.where(low, outs[0], outs[1])
+        att[lo : lo + 256, :] = attended
+        mxs[lo : lo + 256, :] = attended.astype(BF)
+        half = t // 2
+        dst = mix.at[pl.ds(256 * (t % 2), 256), head_lanes]
+        src = mxs.at[pl.ds(lo, 256)]
+        for d in (1, 2, 3):
+            w.send(src, dst, (dp, zh * 8 + 2 * chips[d] + half), s_mix)
+        away = pltpu.make_async_remote_copy(
+            src_ref=src, dst_ref=dst, send_sem=w.sem(), recv_sem=s_mix, device_id=sib, device_id_type=MESH
+        )
+        pl.when(k == half)(lambda: pltpu.make_async_copy(src, dst, s_mix).start())
+        pl.when(k != half)(away.start)
+        late.append((half, away))
+
+    late, late_grads = [], []
+    forward_tile(3)
+    for d in (1, 2, 3):
+        w.arrived(wall.at[:, j, k], s_wq[d - 1])
+    w.send(wall.at[:, :, k], wall.at[:, :, k], sib, s_ws)
+    w.arrived(unit(0, k, 2), s_f[0][2][0])
+    held.append(w.send(unit(0, k, 2), unit(0, k, 3), yp, s_f[0][3][0]))
+    forward_tile(1)
+    forward_tile(2)
+    forward_tile(0)
+
+    w.arrived(dy2.at[pl.ds(0, 256)], s_c0)
+    w.arrived(dy2.at[pl.ds(0, 256)], s_c1)
+    limit = length[0:1, 0:1]
+
+    def drop_rows(t, carry):
+        rows = pl.ds(pl.multiple_of(my_rows + t * 128, 128), 128)
+        place = lax.broadcasted_iota(jnp.int32, (128, 1), 0) + (my_rows + t * 128)
+        kept = (place < limit).astype(F32)
+        dy2[rows, :] = (dy2[rows, :].astype(F32) * kept).astype(BF)
+        return carry
+
+    lax.fori_loop(0, 4, drop_rows, 0)
+    s_dy, s_sec = w.sem(), w.sem()
+    w.send(dy2.at[pl.ds(my_rows, 512)], dy2.at[pl.ds(my_rows, 512)], sib, s_dy)
+    w.arrived(unit(1, k, 2), s_f[0][2][1])
+    held.append(w.send(unit(1, k, 2), unit(1, k, 3), yp, s_f[0][3][1]))
+
+    w.arrived(wall.at[:, :, 0], s_ws)
+    w.arrived(mix, s_mix)
+
+    def attended_rows(rows):
+        total = None
+        for n in range(4):
+            term = _nn(mix[rows, 256 * n : 256 * (n + 1)], wall[n].reshape(256, 1024))
+            total = term if total is None else total + term
+        return total
+
+    def project_out(t, carry):
+        rows = pl.ds(pl.multiple_of(t * 256, 256), 256)
+        state = x[rows, :].astype(F32) + attended_rows(rows)
+        scale = lax.rsqrt(jnp.mean(state * state, axis=1, keepdims=True) + EPS)
+        mine = pl.ds(pl.multiple_of(my_rows + t * 256, 256), 256)
+        sec2[mine, :] = (state * scale * ffn_gain).astype(BF)
+        return carry
+
+    lax.fori_loop(0, 2, project_out, 0)
+    w.send(sec2.at[pl.ds(my_rows, 512)], sec2.at[pl.ds(my_rows, 512)], sib, s_sec)
+
+    for kind in range(3):
+        for slot in (1, 2, 3):
+            if not (slot == 2 and kind < 2):
+                w.arrived(unit(kind, k, slot), s_f[0][slot][kind])
+            if slot == 2 and kind == 2:
+                held.append(w.send(unit(kind, k, 2), unit(kind, k, 3), yp, s_f[0][3][kind]))
+            held.append(w.send(unit(kind, k, slot), unit(kind, k, slot), sib, s_f[1][slot][kind]))
+    for kind in range(3):
+        w.arrived(unit(kind, k, 0), s_f[0][0][kind])
+        for slot in range(4):
+            w.arrived(unit(kind, 1 - k, slot), s_f[1][slot][kind])
+    s_act = w.sem()
+    s_ds = [[w.sem() for _ in range(2)] for _ in range(3)]
+    s_os = [[w.sem() for _ in range(2)] for _ in range(3)]
+    s_da = [w.sem() for _ in range(3)]
+
+    def send_pieces(buf, into, t, sem):
+        for d in (1, 2, 3):
+            rows = pl.ds(pl.multiple_of(256 * t + 64 * piece(chips[d]), 64), 64)
+            w.send(buf.at[rows], into.at[d - 1, t], quad(d, 0), sem[d - 1][t])
+
+    for t in range(2):
+        rows = pl.ds(pl.multiple_of(my_rows + 256 * t, 256), 256)
+        here = pl.ds(256 * t, 256)
+        for e in (1, 0):
+            parity = cores[e]
+            gate = _nt(sec2[rows, :], wf[0, parity])
+            up = _nt(sec2[rows, :], wf[1, parity])
+            d_hidden = _nt(dy2[rows, :], wf[2, parity])
+            sigmoid = 1.0 / (1.0 + jnp.exp(-gate))
+            silu = gate * sigmoid
+            d_gate = (d_hidden * up * (sigmoid + silu * (1.0 - sigmoid))).astype(BF)
+            d_up = (d_hidden * silu).astype(BF)
+            hidden = (silu * up).astype(BF)
+            for n, value in enumerate((d_gate, d_up, hidden)):
+                if e == 1:
+                    asend[n, here, :] = value
+                else:
+                    acts[n, rows, :] = value
+            if e == 1:
+                w.send(asend.at[:, here], acts.at[:, rows], sib, s_act)
+        own = tuple(acts[n, rows, :] for n in range(3))
+        far = tuple(asend[n, here, :] for n in range(3))
+        dsb[here, :] = (
+            _nn(own[0], wf[0, k]) + _nn(far[0], wf[0, 1 - k])
+            + _nn(own[1], wf[1, k]) + _nn(far[1], wf[1, 1 - k])
+        ).astype(BF)
+        send_pieces(dsb, dsr, t, s_ds)
+        osb[here, :] = (_nn(own[2], wf[2, k]) + _nn(far[2], wf[2, 1 - k])).astype(BF)
+    w.finish(held)
+    w.arrived(acts.at[:, pl.ds(0, 512)], s_act)
+    w.arrived(sec2.at[pl.ds(0, 512)], s_sec)
+    w.arrived(dy2.at[pl.ds(0, 512)], s_dy)
+    s_gr = [[w.sem() for _ in range(3)] for _ in range(2)]
+    s_gt = [w.sem() for _ in range(3)]
+    for kind in range(3):
+        right = dy2 if kind == 2 else sec2
+        def columns(n, carry, kind=kind, right=right):
+            cols = pl.ds(pl.multiple_of(n * 256, 256), 256)
+            term = _tn(acts[kind], right[:, cols])
+            for slot in range(4):
+                wf[kind, 0, 144 * slot : 144 * (slot + 1), cols] = term[144 * slot : 144 * (slot + 1), :].astype(BF)
+            return carry
+        lax.fori_loop(0, 4, columns, 0)
+        w.send(unit(kind, 0, 3), gr.at[1, kind], yp, s_gr[1][kind])
+    for t in range(2):
+        send_pieces(osb, osr, t, s_os)
+    mine = piece(j)
+    s_dm = w.sem()
+    ffn_gain_grad = jnp.zeros((1, 1024), F32)
+    for t in range(2):
+        start = 256 * t + 64 * mine
+        rows = pl.ds(pl.multiple_of(start, 64), 64)
+        state = x[rows, :].astype(F32) + attended_rows(rows)
+        scale = lax.rsqrt(jnp.mean(state * state, axis=1, keepdims=True) + EPS)
+        normed = state * scale
+        total = dsb[rows, :].astype(F32)
+        for d in range(3):
+            w.arrived(dsr.at[d, t], s_ds[d][t])
+            total = total + dsr[d, t].astype(F32)
+        ffn_gain_grad = ffn_gain_grad + jnp.sum(total * normed, axis=0, keepdims=True)
+        weighted = total * ffn_gain
+        inner = jnp.mean(weighted * normed, axis=1, keepdims=True)
+        grad = dy2[pl.ds(pl.multiple_of(my_rows + start, 64), 64), :].astype(F32) + scale * (weighted - normed * inner)
+        dstate[t] = grad
+        low_grad = grad.astype(BF)
+        daf[k, t, mine] = low_grad
+        for n in range(4):
+            dmb[t, :, 256 * n : 256 * (n + 1)] = _nt(low_grad, wall[n].reshape(256, 1024)).astype(BF)
+        bos[t] = state
+        for d, e in others:
+            lanes = pl.ds(pl.multiple_of(LANES * (2 * chips[d] + cores[e]), LANES), LANES)
+            w.send(dmb.at[t, :, lanes], dmix.at[k, t, mine], quad(d, e), s_dm)
+        w.local(dmb.at[t, :, head_lanes], dmix.at[k, t, mine], s_dm)
+    gg[...] = jnp.zeros_like(gg)
+    gg[1:2, :] = ffn_gain_grad
+    for d in (1, 2, 3):
+        w.send(daf.at[k, :, mine], daf.at[k, :, mine], quad(d, 0), s_da[d - 1])
+
+    def pass_grads(kind):
+        w.arrived(gr.at[1, kind], s_gr[1][kind])
+        gs[kind] = (wf[kind, 0, 288:432, :].astype(F32) + gr[1, kind].astype(F32)).astype(BF)
+        w.send(gs.at[kind], gt.at[kind], zp, s_gt[kind])
+        w.send(unit(kind, 0, 1), gr.at[0, kind], yp, s_gr[0][kind])
+
+    home = zh + k * (1 - 2 * zh)
+
+    def send_home(buf, into, sem):
+        w.local(buf.at[home, 0], into.at[zh, k], sem)
+        w.send(buf.at[1 - home, 0], into.at[zh, k], zp, sem)
+        w.send(buf.at[1 - home, 1], into.at[zh, k], zps, sem)
+        w.send(buf.at[home, 1], into.at[zh, k], sib, sem)
+
+    s_bo = w.sem()
+
+    def finish_blocks():
+        for t in range(2):
+            rows = pl.ds(pl.multiple_of(256 * t + 64 * mine, 64), 64)
+            total = bos[t] + osb[rows, :].astype(F32)
+            for d in range(3):
+                w.arrived(osr.at[d, t], s_os[d][t])
+                total = total + osr[d, t].astype(F32)
+            obs[t] = total.astype(BF).reshape(2, 32, 1024)
+        send_home(obs, bor, s_bo)
+
+    s_das = w.sem()
+
+    def share_state_grads():
+        for d in range(3):
+            w.arrived(daf.at[k, :, mine], s_da[d])
+        w.send(daf.at[k], daf.at[k], sib, s_das)
+
+    w.arrived(dmix, s_dm)
+
+    def backward_tile(t):
+        lo, n = 256 * t, 256 * (t + 1)
+        d_out = dmix[...].reshape(1024, LANES)[lo : lo + 256, :].astype(F32)
+        product = d_out * att[lo : lo + 256, :]
+        parts = []
+        for h, q in enumerate((q0, q1)):
+            here = low if h == 0 else jnp.logical_not(low)
+            d_head = jnp.where(here, d_out, 0.0).astype(BF)
+            delta = jnp.sum(jnp.where(here, product, 0.0), axis=1, keepdims=True)
+            weights = prob[h, lo : lo + 256, 0:n]
+            pulled = _nt(d_head, vv[0:n, :])
+            d_scores = (weights.astype(F32) * (pulled - delta)).astype(BF)
+            parts.append(_nn(d_scores, kk[0:n, :]))
+            dkk[0:n, :] += _tn(d_scores, q[lo : lo + 256, :])
+            dvv[0:n, :] += _tn(weights, d_head)
+        dqq[lo : lo + 256, :] = jnp.where(low, parts[0], parts[1]) * (HEAD_DIM**-0.5)
+
+    dkk[...] = jnp.zeros_like(dkk)
+    dvv[...] = jnp.zeros_like(dvv)
+    backward_tile(3)
+    pass_grads(0)
+    finish_blocks()
+    backward_tile(2)
+    share_state_grads()
+    pass_grads(1)
+    backward_tile(1)
+    backward_tile(0)
+
+    def back_rows(t, carry):
+        query_sum, key_sum = carry
+        rows = pl.ds(pl.multiple_of(t * 256, 256), 256)
+        cosine, sine = cos_t[rows, :], sin_t[rows, :]
+        query = raw[rows, 0:LANES]
+        both = raw[rows, LANES : 2 * LANES]
+
+        def through(values, grads, gain_row):
+            scale = inverse_root(values)
+            normed = values * scale
+            grads = grads * cosine - swap(grads) * sine
+            weighted = grads * gain_row
+            inner = head_sum(weighted * normed) * (1.0 / HEAD_DIM)
+            return scale * (weighted - normed * inner), jnp.sum(grads * normed, axis=0, keepdims=True)
+
+        query_back, query_term = through(query, dqq[rows, :], query_gain)
+        d_key = dkk[rows, :]
+        d_key = d_key + pltpu.roll(d_key, HALF_LANES, 1)
+        key_back, key_term = through(both, d_key, key_gain)
+        d_value = dvv[rows, :]
+        d_value = d_value + pltpu.roll(d_value, HALF_LANES, 1)
+        dpj[rows, 0:LANES] = query_back.astype(BF)
+        dpj[rows, LANES : 2 * LANES] = jnp.where(low, key_back, d_value).astype(BF)
+        return query_sum + query_term, key_sum + key_term
+
+    zero_row = jnp.zeros((1, LANES), F32)
+    query_sum, key_sum = lax.fori_loop(0, 4, back_rows, (zero_row, zero_row))
+    s_dpx = w.sem()
+    w.send(dpj.at[pl.ds(other_rows, 512)], dpx, sib, s_dpx)
+    gg[2:3, 0:LANES] = query_sum + pltpu.roll(query_sum, HALF_LANES, 1)
+    gg[2:3, LANES : 2 * LANES] = key_sum
+    pass_grads(2)
+
+    w.arrived(daf.at[0], s_das)
+    flat_da = daf[...].reshape(1024, 1024)
+    out_term = _tn(mxs[...], flat_da)
+    s_df = [[w.sem() for _ in range(2)] for _ in range(3)]
+    w.arrived(dpx, s_dpx)
+    for t in range(2):
+        here = pl.ds(256 * t, 256)
+        rows = pl.ds(pl.multiple_of(my_rows + 256 * t, 256), 256)
+        dfb[here, :] = (_nn(dpj[rows, :], w2[own_head, :]) + _nn(dpx[here, :], w2[sib_head, :])).astype(BF)
+        send_pieces(dfb, dfr, t, s_df)
+    w.arrived(first2.at[pl.ds(0, 512)], s_first)
+    in_term = _tn(dpj[...], first2[...])
+    s_ag = w.sem()
+    for p in range(4):
+        igs[p, 0:64, :] = in_term[64 * p : 64 * (p + 1), :].astype(BF)
+        igs[p, 64:96, :] = out_term[32 * p : 32 * (p + 1), :].astype(BF)
+        target = 4 * k + p
+        away = pltpu.make_async_remote_copy(
+            src_ref=igs.at[p], dst_ref=ags.at[j], send_sem=w.sem(), recv_sem=s_ag,
+            device_id=(dp, zh * 8 + target), device_id_type=MESH,
+        )
+        pl.when(target == g)(lambda p=p: pltpu.make_async_copy(igs.at[p], ags.at[j], s_ag).start())
+        pl.when(target != g)(away.start)
+        late_grads.append((target, away))
+
+    s_ar = [w.sem(), w.sem()]
+    s_at = w.sem()
+    w.arrived(ags, s_ag)
+    w.send(ags.at[team_d], agr.at[1], yp, s_ar[1])
+    w.send(ags.at[team_y], agr.at[0], yp, s_ar[0])
+
+    attn_gain_grad = jnp.zeros((1, 1024), F32)
+    for t in range(2):
+        rows = pl.ds(pl.multiple_of(256 * t + 64 * mine, 64), 64)
+        values = x[rows, :].astype(F32)
+        scale = lax.rsqrt(jnp.mean(values * values, axis=1, keepdims=True) + EPS)
+        normed = values * scale
+        total = dfb[rows, :].astype(F32)
+        for d in range(3):
+            w.arrived(dfr.at[d, t], s_df[d][t])
+            total = total + dfr[d, t].astype(F32)
+        attn_gain_grad = attn_gain_grad + jnp.sum(total * normed, axis=0, keepdims=True)
+        weighted = total * attn_gain
+        inner = jnp.mean(weighted * normed, axis=1, keepdims=True)
+        grad = dstate[t] + scale * (weighted - normed * inner)
+        tgs[t] = grad.astype(BF).reshape(2, 32, 1024)
+    s_tg = w.sem()
+    send_home(tgs, tgr, s_tg)
+    gg[0:1, :] = attn_gain_grad
+
+    s_gg, s_gy, s_gz = w.sem(), w.sem(), w.sem()
+    for d, e in others:
+        w.send(gg, ggq.at[g], quad(d, e), s_gg)
+    w.local(gg, ggq.at[g], s_gg)
+    w.arrived(agr.at[1], s_ar[1])
+    agz[...] = (ags[team_z].astype(F32) + agr[1].astype(F32)).astype(BF)
+    w.send(agz, agt, zp, s_at)
+    w.arrived(ggq, s_gg)
+    total = ggq[0]
+    for n in range(1, 8):
+        total = total + ggq[n]
+    gsum[0] = total
+    w.send(gsum.at[0], ggy, yp, s_gy)
+
+    for kind in range(3):
+        w.arrived(gr.at[0, kind], s_gr[0][kind])
+        w.arrived(gt.at[kind], s_gt[kind])
+        o_ffn[kind] = wf[kind, 0, 0:144, :].astype(F32) + gr[0, kind].astype(F32) + gt[kind].astype(F32)
+    w.arrived(bor, s_bo)
+    o_block[...] = bor[...]
+    w.arrived(ggy, s_gy)
+    gsum[1] = total + ggy[...]
+    w.send(gsum.at[1], ggz, zp, s_gz)
+    w.arrived(agr.at[0], s_ar[0])
+    w.arrived(agt, s_at)
+    attn = ags[team].astype(F32) + agr[0].astype(F32) + agt[...].astype(F32)
+    o_in[...] = attn[0:64, :]
+    o_out[...] = attn[64:96, :]
+    w.arrived(tgr, s_tg)
+    o_tokens[...] = tgr[...].astype(F32)
+    w.arrived(ggz, s_gz)
+    o_gain[...] = gsum[1] + ggz[...]
+    w.finish()
+    for half, away in late:
+        pl.when(k != half)(away.wait_send)
+    for target, away in late_grads:
+        pl.when(target != g)(away.wait_send)
+
+
+TEAM_SCRATCH = (
+    ((512, 1024), BF), ((2, 32, 1024), BF), ((2, 32, 1024), BF), ((4, 64, 1024), BF), ((512, 1024), BF),
+    ((4, 4, 2, 32, 1024), BF), ((3, 2, 640, 1024), BF), ((4, 8, 8, 128), F32), ((8, 1024), F32),
+    ((1024, 1024), BF), ((1024, 256), F32), ((512, 256), F32),
+    ((1024, 128), BF), ((1024, 128), BF), ((1024, 128), BF), ((1024, 128), BF), ((2, 1024, 1024), BF),
+    ((1024, 128), F32), ((1024, 128), BF), ((512, 1024), BF), ((1024, 1024), BF), ((1024, 1024), BF),
+    ((3, 1024, 640), BF), ((3, 512, 640), BF),
+    ((512, 1024), BF), ((512, 1024), BF), ((3, 2, 64, 1024), BF), ((3, 2, 64, 1024), BF),
+    ((2, 3, 144, 1024), BF), ((3, 144, 1024), BF), ((3, 144, 1024), BF),
+    ((2, 64, 1024), F32), ((2, 64, 1024), BF), ((2, 2, 4, 64, 1024), BF), ((2, 2, 4, 64, 128), BF),
+    ((1024, 128), F32), ((1024, 128), F32), ((1024, 128), F32), ((1024, 256), BF), ((512, 256), BF),
+    ((512, 1024), BF), ((3, 2, 64, 1024), BF),
+    ((4, 96, 1024), BF), ((4, 96, 1024), BF), ((2, 96, 1024), BF), ((96, 1024), BF), ((96, 1024), BF),
+    ((2, 64, 1024), F32), ((2, 2, 32, 1024), BF), ((2, 2, 32, 1024), BF), ((2, 2, 32, 1024), BF),
+    ((2, 2, 32, 1024), BF),
+    ((8, 1024), F32), ((8, 8, 1024), F32), ((2, 8, 1024), F32), ((8, 1024), F32), ((8, 1024), F32),
+)
+
+
+def rotary_lanes(rows):
+    width = HEAD_DIM // 2
+    freq = (ROPE_BASE ** (-np.arange(width, dtype=np.float32) * np.float32(2.0 / HEAD_DIM))).astype(np.float32)
+    angle = (np.arange(rows, dtype=np.float32)[:, None] * freq).astype(np.float32).astype(np.float64)
+    cosine, sine = np.cos(angle), np.sin(angle)
+    return (
+        np.tile(np.concatenate([cosine, cosine], 1), (1, 2)).astype(np.float32),
+        np.tile(np.concatenate([-sine, sine], 1), (1, 2)).astype(np.float32),
+    )
+
+
+def on_team(tokens, segments, lengths, attn_in, attn_out, gains, ffn_weights, cotangent):
+    batches, block_len, halves, width = tokens.shape
+    here = lax.axis_index("ctx")
+    seq = here // 8
+    rows = segments.shape[1]
+    docs = lax.dynamic_index_in_dim(segments, seq, 0, False)
+    back = docs[:, 1].reshape(rows // block_len, block_len)[::-1].reshape(rows)
+    docs = jnp.concatenate([docs[:, 0], back])
+    limit = lax.dynamic_index_in_dim(lengths, seq, 0, False)
+    doc_row = jnp.where(jnp.arange(2 * rows, dtype=jnp.int32) < limit, docs, -1)
+    cosine, sine = rotary_lanes(2 * rows)
+    args = (
+        tokens.transpose(0, 2, 1, 3),
+        cotangent.transpose(0, 2, 1, 3),
+        attn_in,
+        attn_out,
+        jnp.pad(gains.astype(F32)[None], ((0, 7), (0, LANES - gains.shape[0]))),
+        ffn_weights.transpose(1, 0, 2),
+        docs[:, None],
+        doc_row[None],
+        jnp.broadcast_to(limit, (8, LANES)),
+        jnp.asarray(cosine),
+        jnp.asarray(sine),
+    )
+    vmem = pl.BlockSpec(memory_space=pltpu.VMEM)
+    outs = pl.pallas_call(
+        block_kernel,
+        out_shape=(
+            jax.ShapeDtypeStruct((2, 2, 32, 1024), BF),
+            jax.ShapeDtypeStruct((2, 2, 32, 1024), F32),
+            jax.ShapeDtypeStruct((64, 1024), F32),
+            jax.ShapeDtypeStruct((32, 1024), F32),
+            jax.ShapeDtypeStruct((8, 1024), F32),
+            jax.ShapeDtypeStruct((3, 144, 1024), F32),
+        ),
+        in_specs=[vmem] * len(args),
+        out_specs=(vmem,) * 6,
+        scratch_shapes=[pltpu.VMEM(shape, kind) for shape, kind in TEAM_SCRATCH]
+        + [pltpu.SemaphoreType.DMA((COPIES,))],
+        compiler_params=pltpu.CompilerParams(
+            collective_id=0, has_side_effects=True, vmem_limit_bytes=VMEM_BYTES
+        ),
+    )(*args)
+    block, token_grad, in_grad, out_grad, gain_grad, unit_grad = outs
+    every = jnp.concatenate([gain_grad[0], gain_grad[1], gain_grad[2, :64], gain_grad[2, 128:192]])
+    own = lax.axis_index("dp") * lax.axis_size("ctx") + here
+    return (
+        block.transpose(0, 2, 1, 3),
+        token_grad.transpose(0, 2, 1, 3),
+        in_grad,
+        out_grad,
+        lax.dynamic_slice_in_dim(every, own * gains.shape[0], gains.shape[0], 0),
+        unit_grad.transpose(1, 0, 2),
+    )
+
+
+VMEM_BYTES = 62 << 20
+
+
 def solution(mesh):
     dp, ctx = mesh.devices.shape
-    team = Mesh(mesh.devices.reshape(dp, 2, ctx // (2 * KV_HEADS), KV_HEADS), EVERY)
-    ring = ("s", "q", "g")
+    if ctx == 2 * KV_HEADS:
+        ring = "ctx"
+        every = ("dp", "ctx")
+        team, run = mesh, on_team
+    else:
+        ring = ("s", "q", "g")
+        every = EVERY
+        team = Mesh(mesh.devices.reshape(dp, 2, ctx // (2 * KV_HEADS), KV_HEADS), EVERY)
+        run = on_device
     placed = (
         P("dp", ring, None, None),
         P("dp", None, None),
         P("dp"),
-        P(EVERY, None),
-        P(EVERY, None),
-        P(EVERY),
-        P(EVERY, None, None),
+        P(every, None),
+        P(every, None),
+        P(every),
+        P(every, None, None),
         P("dp", ring, None, None),
     )
     return jax.shard_map(
-        on_device,
+        run,
         mesh=team,
         in_specs=placed,
         out_specs=(
             P("dp", ring, None, None),
             P("dp", ring, None, None),
-            P(EVERY, None),
-            P(EVERY, None),
-            P(EVERY),
-            P(EVERY, None, None),
+            P(every, None),
+            P(every, None),
+            P(every),
+            P(every, None, None),
         ),
         check_vma=False,
     )

time: 886 us -> 241 us (0.27); the launches traced: 877 us -> 241 us
  waiting for transfers between devices: 564 us -> 0 us
  Pallas kernels: 0 us -> 222 us
  blocking collectives: 124 us -> 0 us
  matrix products: 57.2 us -> 0 us
  other arithmetic: 50.2 us -> 2.5 us
  local copies, waits for them, and re-layouts: 58.3 us -> 15.7 us
  between operations: 15.1 us -> 0.7 us
    reduce_scatter x6 -> x0, waiting for transfers between devices: 406 us -> none  [the longest x1 148 us: on_device(): lax.psum_scatter(placed(in_term, QKV_ROWS), EVERY, scatter_dimension=0, t...]
    pallas_call x0 -> x1, Pallas kernels: none -> 222 us  [on_team(): pl.pallas_call(block_kernel, out_shape=(jax.ShapeDtypeStruct((2, 2, 32, 1...]
    all_gather x7 -> x0, waiting for transfers between devices: 156 us -> none  [the longest x1 67.7 us: on_device(): units = lax.all_gather(ffn_weights, TEAM, axis=0, tiled=True)]
    unnamed x2 -> x0, blocking collectives: 98.2 us -> none
    dot_general x20 -> x0, matrix products: 50.9 us -> none  [the longest x15 40.8 us: dot(): lax.dot_general(a, b, (((ca,), (cb,)), ((), ())), preferred_element_type=...]
    convert_element_type x11 -> x0, other arithmetic: 29.6 us -> none  [the longest x1 7.86 us: on_device(): first = (first_normed * attn_gain).astype(BF)]
    all_to_all x2 -> x0, blocking collectives: 25.5 us -> none  [spread(): mine = lax.all_to_all(local, 's', 0, 0, tiled=True)]
    convert_element_type x6 -> x0, local copies, waits for them, and re-layouts: 25 us -> none  [the longest x2 10.3 us: on_device(): inputs = inputs.reshape(count, width).astype(F32)]
  transfers between devices with their start and end apart: 15 -> 0, of which waited for: 10 -> 0; matrix products, arithmetic and copies ran while one was open for 15% -> 0% of each run, Pallas kernels for 0% -> 0%
where the time goes in v2:
time: 241 us
  Pallas kernels  222 us (92%)
  local copies, waits for them, and re-layouts  15.7 us (7%)
  other arithmetic  2.5 us (1%)
    pallas_call x1, Pallas kernels, on_team(): pl.pallas_call(block_kernel, out_shape=(jax.ShapeDtypeStruct((2, 2, 32, 1...  222 us
    unnamed x11, local copies, waits for them, and re-layouts  7.85 us

profile of v2, /device:TPU:0, one launch (start us, length us, event | category | flops | bytes accessed | tf_op | source)
XLA Modules:
  0.0 240.6 jit_solution(10794711675965915861)
XLA Ops:
  0.6 0.0 copy-start
  0.7 1.2 dynamic_slice.12
  1.9 0.0 copy-done
  1.9 1.2 broadcast_in_dim.18.length
  3.2 1.3 pad_convert_fusion.gain
  4.4 0.1 reshape_squeeze.3
  4.5 0.1 concatenate.21
  4.6 0.1 reshape.53
  4.7 1.2 compare_select_fusion.doc_row
  5.9 1.0 copy.22.doc_col
  7.0 1.9 copy_bitcast_fusion
  8.9 221.7 %shard_map.145 = (bf16[2,2,32,1024]{3,2,1,0:T(8,128)(2,1)}, f32[2,2,32,1024]{3,2,1,0:T(8,128)}, f32[64,1024]{1,0:T(8,128)}, f32[32,1024]{1,0:T(8,128)}, f32[8,1024]{1,0:T(8,128)}, /*index=5*/f32[3,144,1024]{2,1,0:T(8,128)}) custom-call(bf16[2,2,32,1024]{3,2,1,0:T(8,128)(2,1)} %get-tuple-element.38.tok, bf16[2,2,32,1024]{3,2,1,0:T(8,128)(2,1)} %get-tuple-element.37.cot, ...), custom_call_target="tpu_custom_call" | custom-call | tf_op jit(solution)/shard_map/pallas_call | solution.py:906
  230.6 0.0 copy-start.2
  230.6 0.0 copy-start.1
  230.6 2.1 copy.23
  232.7 2.2 copy.24
  234.9 0.7 slice_bitcast_fusion
  235.6 0.8 fusion
  236.4 0.1 concatenate.23
  236.5 0.6 dynamic_slice.13
  237.1 1.7 copy.30
  238.8 0.0 copy-done.2
  238.8 0.7 copy.31
  239.4 1.2 copy.32
  (5 shorter events, 0.0 us)
Async XLA Ops:
  0.6 1.3 copy-start
  230.6 8.2 %copy-start.2 = (f32[32,1024]{1,0:T(8,128)S(1)}, f32[32,1024]{1,0:T(8,128)}, u32[]{:S(2)}) copy-start(f32[32,1024]{1,0:T(8,128)} %get-tuple-element.48) | copy-start | bytes 393220
  230.6 8.8 %copy-start.1 = (f32[3,144,1024]{2,1,0:T(8,128)S(1)}, f32[3,144,1024]{2,1,0:T(8,128)}, u32[]{:S(2)}) copy-start(f32[3,144,1024]{2,1,0:T(8,128)} %get-tuple-element.17) | copy-start | bytes 5308420

commit v3 on v1

--- a/solution.py
+++ b/solution.py
@@ -2,6 +2,8 @@
 import jax.numpy as jnp
 import numpy as np
 from jax import lax
+from jax.experimental import pallas as pl
+from jax.experimental.pallas import tpu as pltpu
 from jax.sharding import Mesh
 from jax.sharding import PartitionSpec as P
 
@@ -222,31 +224,1035 @@
     )
 
 
+LANES = 128
+HALF_LANES = 64
+
+
+def _nt(a, b):
+    return lax.dot_general(a, b, (((1,), (1,)), ((), ())), preferred_element_type=F32)
+
+
+def _nn(a, b):
+    return lax.dot_general(a, b, (((1,), (0,)), ((), ())), preferred_element_type=F32)
+
+
+def _tn(a, b):
+    return lax.dot_general(a, b, (((0,), (0,)), ((), ())), preferred_element_type=F32)
+
+
+MESH = pl.DeviceIdType.MESH
+COPIES = 400
+
+
+class Wires:
+    def __init__(self, sems):
+        self.sems = sems
+        self.used = 0
+        self.pending = []
+
+    def sem(self):
+        self.used += 1
+        return self.sems.at[self.used - 1]
+
+    def send(self, src, dst, to, arrives):
+        copy = pltpu.make_async_remote_copy(
+            src_ref=src, dst_ref=dst, send_sem=self.sem(), recv_sem=arrives,
+            device_id=to, device_id_type=MESH,
+        )
+        copy.start()
+        self.pending.append(copy)
+        return copy
+
+    def local(self, src, dst, arrives):
+        copy = pltpu.make_async_copy(src, dst, arrives)
+        copy.start()
+        return copy
+
+    def arrived(self, ref, sem):
+        pltpu.make_async_copy(ref, ref, sem).wait()
+
+    def finish(self, copies=None):
+        copies = list(self.pending if copies is None else copies)
+        for copy in copies:
+            copy.wait_send()
+        done = {id(copy) for copy in copies}
+        self.pending = [copy for copy in self.pending if id(copy) not in done]
+
+
+def block_kernel(
+    tok, cot, win, wout, gain, wffn, doc_col, doc_row, length, cos_t, sin_t,
+    o_block, o_tokens, o_in, o_out, o_gain, o_ffn,
+    x, rel_t, rel_c, w2, wall, wfa, wfb, gb, grow, first2, raw, po,
+    q0, q1, kk, vv, prob, att, mxs, mix, sec2, dy2, acta, actb, asend,
+    dsb, osb, dsr, osr, rsz, gr, gs, gt, dstate, dmb, daf, dmix,
+    dkk, dvv, dqq, dpj, dpx, dfb, dfr, igs, agr, agz, agt, agh, ago,
+    bos, obs, bor, tgs, tgr, gg, ggq, gsum, ggt, sems,
+):
+    dp = lax.axis_index("dp")
+    c = lax.axis_index("ctx")
+    zh = lax.div(c, 8)
+    g = lax.rem(c, 8)
+    j = lax.div(g, 2)
+    k = lax.rem(c, 2)
+    chips = (j, j + 1 - 2 * lax.rem(j, 2), j + 2 - 4 * lax.div(j, 2), 3 - j)
+    cores = (k, 1 - k)
+
+    def quad(d, e):
+        return (dp, zh * 8 + 2 * chips[d] + cores[e])
+
+    sib = quad(0, 1)
+    czp = lax.rem(c + 8, 16)
+    zp = (dp, lax.rem(c + 8, 16))
+    zps = (dp, 8 * (1 - zh) + 2 * j + 1 - k)
+    yp = (1 - dp, c)
+    diag = (1 - dp, lax.rem(c + 8, 16))
+    team = 2 * dp + zh
+    team_y = 2 * (1 - dp) + zh
+    team_z = 2 * dp + 1 - zh
+    team_d = 3 - team
+    w = Wires(sems)
+    others = [(d, e) for d in range(4) for e in range(2) if (d, e) != (0, 0)]
+
+    zl, xx = lax.div(j, 2), lax.rem(j, 2)
+    keeper = (xx, 8 * k + 4 * dp + 2 * zh + zl)
+    owner_of = (zl, 8 * xx + 4 * k + 2 * dp + zh)
+    alone = jnp.logical_and(keeper[0] == dp, keeper[1] == c)
+    apart = jnp.logical_not(alone)
+
+    barrier = pltpu.get_barrier_semaphore()
+    peers = [quad(d, e) for d, e in others] + [zp, zps, yp, diag]
+    for peer in peers:
+        pl.semaphore_signal(barrier, inc=1, device_id=peer, device_id_type=MESH)
+
+    @pl.when(apart)
+    def _():
+        pl.semaphore_signal(barrier, inc=1, device_id=keeper, device_id_type=MESH)
+        pl.semaphore_signal(barrier, inc=1, device_id=owner_of, device_id_type=MESH)
+        pl.semaphore_wait(barrier, len(peers) + 2)
+
+    @pl.when(alone)
+    def _():
+        pl.semaphore_wait(barrier, len(peers))
+
+    def many(*shape):
+        return [many(*shape[1:]) for _ in range(shape[0])] if shape else w.sem()
+
+    def piece(chip):
+        return chip + k * (3 - 2 * chip)
+
+    def row_block(owner, half):
+        return owner + half * (15 - 2 * owner)
+
+    my_rows = pl.multiple_of(512 * k, 512)
+    other_rows = pl.multiple_of(512 * (1 - k), 512)
+    own_head, sib_head = pl.ds(0, 256), pl.ds(256, 256)
+    mine = piece(j)
+    steps = {}
+
+    def step(name):
+        def keep(body):
+            steps[name] = body
+            return body
+        return keep
+
+    def rows_of(buf, offset):
+        def at(half, start, count):
+            return buf.at[pl.ds(pl.multiple_of(offset * half + start, 32), count)]
+        return at
+
+    def rows_steps(name, source, relay, at):
+        s_rel, s_here, s_z, s_d = many(2), w.sem(), many(2), w.sem()
+        passed = []
+
+        def scatter(src, owner, e, which):
+            half = cores[e]
+            dst = at(half, pl.multiple_of(row_block(owner, half) * 32, 32), 32)
+            w.send(src, dst, quad(2, e), s_z[which])
+            w.send(src, dst, quad(1, e), s_here)
+            if e == 0:
+                w.local(src, dst, s_here)
+            else:
+                w.send(src, dst, sib, s_here)
+
+        def halves(e):
+            @step(f"{name}_out{e}")
+            def _():
+                w.send(source.at[1 - zh, cores[e]], relay.at[cores[e]], zp, s_rel[e])
+
+            @step(f"{name}_own{e}")
+            def _():
+                scatter(source.at[zh, cores[e]], c, e, 0)
+
+            @step(f"{name}_rel{e}")
+            def _():
+                w.arrived(relay.at[cores[e]], s_rel[e])
+                scatter(relay.at[cores[e]], czp, e, 1)
+
+            @step(f"{name}_fwd{e}")
+            def _():
+                first = (zh if e == 0 else 1 - zh) * 8 + 2 * chips[2]
+                rows = at(k, pl.multiple_of(32 * (first + k * (14 - 2 * first)), 64), 64)
+                w.arrived(rows, s_z[e])
+                passed.append(w.send(rows, rows, quad(1, 0), s_d))
+
+        halves(0)
+        halves(1)
+        return s_here, s_d, passed
+
+    s_x, s_xd, _ = rows_steps("tok", tok, rel_t, rows_of(x, 0))
+    s_c, s_cd, cot_passed = rows_steps("cot", cot, rel_c, rows_of(dy2, 512))
+
+    def head_rows(t):
+        return w2.at[pl.ds(pl.multiple_of(64 * t, 64), 64)]
+
+    def exchange(name, src, at, keep):
+        sem = many(4)
+
+        @step(f"{name}_start")
+        def _():
+            w.send(src, at(team), zp, sem[1])
+            w.send(src, at(team), yp, sem[0])
+            if keep:
+                w.local(src, at(team), sem[3])
+
+        @step(f"{name}_pass")
+        def _():
+            w.arrived(at(team_z), sem[1])
+            w.send(at(team_z), at(team_z), yp, sem[2])
+
+        def end():
+            w.arrived(at(team_y), sem[0])
+            w.arrived(at(team_d), sem[2])
+            if keep:
+                w.arrived(at(team), sem[3])
+
+        return end
+
+    s_move, s_w2, s_gq, s_wq, s_ws = w.sem(), w.sem(), w.sem(), many(3), w.sem()
+    gains_end = exchange("gain", gain, lambda t: gb.at[t, g], True)
+    heads_end = exchange("win", head_rows(team), head_rows, False)
+    wout_end = exchange("wout", wout, lambda t: wall.at[t, j, k], True)
+    move = pltpu.make_async_remote_copy(
+        src_ref=win, dst_ref=head_rows(lax.rem(g, 4)), send_sem=w.sem(), recv_sem=s_move,
+        device_id=keeper, device_id_type=MESH,
+    )
+
+    @step("move")
+    def _():
+        pl.when(apart)(move.start)
+        pl.when(alone)(lambda: pltpu.make_async_copy(win, head_rows(team), s_move).start())
+
+    @step("moved")
+    def _():
+        w.arrived(head_rows(team), s_move)
+
+    @step("gain_end")
+    def _():
+        gains_end()
+        for d, e in others:
+            w.send(gb.at[:, g], gb.at[:, g], quad(d, e), s_gq)
+
+    @step("win_end")
+    def _():
+        heads_end()
+        w.send(w2.at[own_head], w2.at[sib_head], sib, s_w2)
+
+    @step("wout_end")
+    def _():
+        wout_end()
+        for d in (2, 1):
+            w.send(wall.at[:, j, k], wall.at[:, j, k], quad(d, 0), s_wq[d - 1])
+
+    @step("wout_fwd")
+    def _():
+        w.arrived(wall.at[:, chips[2], k], s_wq[1])
+        w.send(wall.at[:, chips[2], k], wall.at[:, chips[2], k], quad(1, 0), s_wq[2])
+
+    @step("wout_sib")
+    def _():
+        for d in (1, 3):
+            w.arrived(wall.at[:, j, k], s_wq[d - 1])
+        w.send(wall.at[:, :, k], wall.at[:, :, k], sib, s_ws)
+
+    parts = ((0, 80, wfa, acta, 320, 384), (80, 64, wfb, actb, 256, 256))
+    s_f = many(2, 2, 4, 3)
+    held = [[], []]
+
+    def source(part, kind):
+        return wffn.at[kind, pl.ds(parts[part][0], parts[part][1])]
+
+    def unit(part, kind, far, slot):
+        _, rows, buf, _, _, second = parts[part]
+        return buf.at[kind, pl.ds(second * far + rows * slot, rows)]
+
+    def unit_steps(part):
+        sem = s_f[part]
+
+        @step(f"u{part}_own")
+        def _():
+            for kind in range(3):
+                w.local(source(part, kind), unit(part, kind, 0, 0), sem[0][0][kind])
+                w.send(source(part, kind), unit(part, kind, 1, 0), sib, sem[1][0][kind])
+                if part == 0:
+                    wfa[kind, 320:384, :] = jnp.zeros((64, 1024), BF)
+
+        @step(f"u{part}_y")
+        def _():
+            for kind in range(3):
+                w.send(source(part, kind), unit(part, kind, 0, 1), yp, sem[0][1][kind])
+
+        def from_z(kind):
+            @step(f"u{part}_z{kind}")
+            def _():
+                w.send(source(part, kind), unit(part, kind, 0, 2), zp, sem[0][2][kind])
+
+            @step(f"u{part}_f{kind}")
+            def _():
+                here = unit(part, kind, 0, 2)
+                w.arrived(here, sem[0][2][kind])
+                held[part].append(w.send(here, unit(part, kind, 0, 3), yp, sem[0][3][kind]))
+                held[part].append(w.send(here, unit(part, kind, 1, 2), sib, sem[1][2][kind]))
+
+        def ready(slot):
+            @step(f"u{part}_s{slot}")
+            def _():
+                for kind in range(3):
+                    here = unit(part, kind, 0, slot)
+                    w.arrived(here, sem[0][slot][kind])
+                    held[part].append(w.send(here, unit(part, kind, 1, slot), sib, sem[1][slot][kind]))
+
+        for kind in range(3):
+            from_z(kind)
+        ready(1)
+        ready(3)
+
+        @step(f"u{part}_all")
+        def _():
+            for kind in range(3):
+                w.arrived(unit(part, kind, 0, 0), sem[0][0][kind])
+                for slot in range(4):
+                    w.arrived(unit(part, kind, 1, slot), sem[1][slot][kind])
+
+    unit_steps(0)
+    unit_steps(1)
+
+    lane = lax.broadcasted_iota(jnp.int32, (1, LANES), 1)
+    low_row = lane < HALF_LANES
+
+    @step("gains")
+    def _():
+        w.arrived(gb.at[:, pl.ds(0, 7)], s_gq)
+        chunks = [jnp.zeros((1, LANES), F32) for _ in range(18)]
+        for i in range(32):
+            row = gb[i // 8, i % 8, 0:1, :]
+            place, shift = divmod(68 * i, LANES)
+            moved = pltpu.roll(row, shift, 1) if shift else row
+            chunks[place] = chunks[place] + jnp.where(lane >= shift, moved, 0.0)
+            if shift + 68 > LANES:
+                chunks[place + 1] = chunks[place + 1] + jnp.where(lane < shift, moved, 0.0)
+        for n in range(8):
+            grow[0:1, LANES * n : LANES * (n + 1)] = chunks[n]
+            grow[1:2, LANES * n : LANES * (n + 1)] = chunks[8 + n]
+        flipped = pltpu.roll(chunks[16], HALF_LANES, 1)
+        grow[2:3, 0:LANES] = jnp.where(low_row, chunks[16], flipped)
+        grow[2:3, LANES : 2 * LANES] = jnp.where(low_row, flipped, chunks[16])
+
+    def attn_gain():
+        return grow[0:1, :]
+
+    def ffn_gain():
+        return grow[1:2, :]
+
+    def query_gain():
+        return grow[2:3, 0:LANES]
+
+    def key_gain():
+        return grow[2:3, LANES : 2 * LANES]
+
+    s_raw, s_first = w.sem(), w.sem()
+
+    @step("project")
+    def _():
+        w.arrived(x.at[pl.ds(0, 256)], s_x)
+        w.arrived(x.at[pl.ds(0, 128)], s_xd)
+        w.arrived(w2.at[sib_head], s_w2)
+        weight = attn_gain()
+
+        def rows_of_256(t, carry):
+            rows = pl.multiple_of(t * 256, 256)
+            values = x[pl.ds(rows, 256), :].astype(F32)
+            scale = lax.rsqrt(jnp.mean(values * values, axis=1, keepdims=True) + EPS)
+            first = (values * scale * weight).astype(BF)
+            here = pl.multiple_of(my_rows + rows, 256)
+            first2[pl.ds(here, 256), :] = first
+            po[pl.ds(rows, 256), :] = _nt(first, w2[sib_head, :])
+            raw[pl.ds(here, 256), :] = _nt(first, w2[own_head, :])
+            return carry
+
+        lax.fori_loop(0, 2, rows_of_256, 0)
+        w.send(po, raw.at[pl.ds(my_rows, 512)], sib, s_raw)
+
+    @step("first_sib")
+    def _():
+        w.send(first2.at[pl.ds(my_rows, 512)], first2.at[pl.ds(my_rows, 512)], sib, s_first)
+
+    low = lax.broadcasted_iota(jnp.int32, (256, LANES), 1) < HALF_LANES
+    quarter = lax.rem(lax.broadcasted_iota(jnp.int32, (256, LANES), 1), HALF_LANES) < 32
+
+    def swap(v):
+        return jnp.where(quarter, pltpu.roll(v, 96, 1), pltpu.roll(v, 32, 1))
+
+    def head_sum(v):
+        first = jnp.sum(jnp.where(low, v, 0.0), axis=1, keepdims=True)
+        second = jnp.sum(jnp.where(low, 0.0, v), axis=1, keepdims=True)
+        return jnp.where(low, first, second)
+
+    def inverse_root(v):
+        return lax.rsqrt(head_sum(v * v) * (1.0 / HEAD_DIM) + EPS)
+
+    @step("rotate")
+    def _():
+        w.arrived(raw.at[pl.ds(0, 512)], s_raw)
+        query_weight, key_weight = query_gain(), key_gain()
+
+        def rotate_rows(t, carry):
+            rows = pl.ds(pl.multiple_of(t * 256, 256), 256)
+            cosine, sine = cos_t[rows, :], sin_t[rows, :]
+            query = raw[rows, 0:LANES]
+            both = raw[rows, LANES : 2 * LANES]
+            query = query * inverse_root(query) * query_weight
+            query = (query * cosine + swap(query) * sine) * (HEAD_DIM**-0.5)
+            q0[rows, :] = jnp.where(low, query, 0.0).astype(BF)
+            q1[rows, :] = jnp.where(low, 0.0, query).astype(BF)
+            key = both * inverse_root(both) * key_weight
+            key = key * cosine + swap(key) * sine
+            kk[rows, :] = jnp.where(low, key, pltpu.roll(key, HALF_LANES, 1)).astype(BF)
+            vv[rows, :] = jnp.where(low, pltpu.roll(both, HALF_LANES, 1), both).astype(BF)
+            return carry
+
+        lax.fori_loop(0, 4, rotate_rows, 0)
+
+    s_mix, s_md, s_mz = w.sem(), w.sem(), many(2)
+    head_lanes = pl.ds(pl.multiple_of(LANES * g, LANES), LANES)
+    z_lanes = pl.ds(pl.multiple_of(256 * chips[2], 256), 256)
+    late = []
+
+    def forward_tile(t):
+        @step(f"at{t}")
+        def _():
+            lo, n = 256 * t, 256 * (t + 1)
+            place = lax.broadcasted_iota(jnp.int32, (256, n), 0) + lo
+            key_place = lax.broadcasted_iota(jnp.int32, (256, n), 1)
+            same = doc_col[lo : lo + 256, :] == doc_row[0:1, 0:n]
+            mask = (same & (key_place <= place)) | (key_place == place)
+            outs = []
+            for h, q in enumerate((q0, q1)):
+                scores = jnp.where(mask, _nt(q[lo : lo + 256, :], kk[0:n, :]), MASKED)
+                peak = jnp.max(scores, axis=1, keepdims=True)
+                expo = jnp.exp(scores - peak)
+                weights = (expo * (1.0 / jnp.sum(expo, axis=1, keepdims=True))).astype(BF)
+                prob[h, lo : lo + 256, 0:n] = weights
+                outs.append(_nn(weights, vv[0:n, :]))
+            attended = jnp.where(low, outs[0], outs[1])
+            att[lo : lo + 256, :] = attended
+            mxs[lo : lo + 256, :] = attended.astype(BF)
+            half = t // 2
+            dst = mix.at[pl.ds(256 * (t % 2), 256), head_lanes]
+            src = mxs.at[pl.ds(lo, 256)]
+            w.send(src, dst, (dp, zh * 8 + 2 * chips[2] + half), s_mz[t % 2])
+            w.send(src, dst, (dp, zh * 8 + 2 * chips[1] + half), s_mix)
+            away = pltpu.make_async_remote_copy(
+                src_ref=src, dst_ref=dst, send_sem=w.sem(), recv_sem=s_mix, device_id=sib, device_id_type=MESH
+            )
+            pl.when(k == half)(lambda: pltpu.make_async_copy(src, dst, s_mix).start())
+            pl.when(k != half)(away.start)
+            late.append((half, away))
+
+    def pass_mixed(r):
+        @step(f"mix_fwd{r}")
+        def _():
+            part = mix.at[pl.ds(256 * r, 256), z_lanes]
+            w.arrived(part, s_mz[r])
+            w.send(part, part, quad(1, 0), s_md)
+
+    for t in range(4):
+        forward_tile(t)
+    pass_mixed(0)
+    pass_mixed(1)
+
+    s_dy, s_sec = w.sem(), w.sem()
+
+    @step("dy")
+    def _():
+        w.arrived(dy2.at[pl.ds(0, 256)], s_c)
+        w.arrived(dy2.at[pl.ds(0, 128)], s_cd)
+        w.finish(cot_passed)
+        limit = length[0:1, 0:1]
+
+        def drop_rows(t, carry):
+            rows = pl.ds(pl.multiple_of(my_rows + t * 128, 128), 128)
+            place = lax.broadcasted_iota(jnp.int32, (128, 1), 0) + (my_rows + t * 128)
+            kept = (place < limit).astype(F32)
+            dy2[rows, :] = (dy2[rows, :].astype(F32) * kept).astype(BF)
+            return carry
+
+        lax.fori_loop(0, 4, drop_rows, 0)
+        w.send(dy2.at[pl.ds(my_rows, 512)], dy2.at[pl.ds(my_rows, 512)], sib, s_dy)
+
+    def attended_rows(rows):
+        total = None
+        for n in range(4):
+            term = _nn(mix[rows, 256 * n : 256 * (n + 1)], wall[n].reshape(256, 1024))
+            total = term if total is None else total + term
+        return total
+
+    @step("second")
+    def _():
+        w.arrived(wall.at[:, :, 0], s_ws)
+        w.arrived(mix.at[pl.ds(0, 256)], s_mix)
+        w.arrived(mix.at[:, pl.ds(0, 256)], s_md)
+        weight = ffn_gain()
+
+        def project_out(t, carry):
+            rows = pl.ds(pl.multiple_of(t * 256, 256), 256)
+            state = x[rows, :].astype(F32) + attended_rows(rows)
+            scale = lax.rsqrt(jnp.mean(state * state, axis=1, keepdims=True) + EPS)
+            here = pl.ds(pl.multiple_of(my_rows + t * 256, 256), 256)
+            sec2[here, :] = (state * scale * weight).astype(BF)
+            return carry
+
+        lax.fori_loop(0, 2, project_out, 0)
+        w.send(sec2.at[pl.ds(my_rows, 512)], sec2.at[pl.ds(my_rows, 512)], sib, s_sec)
+
+    class Sum:
+        def __init__(self, name, buf, into, which):
+            self.buf, self.into, self.which = buf, into, which
+            self.sems = many(3, 2)
+            for t in range(2):
+                if name == "os":
+                    step(f"{name}_x{t}")(lambda t=t: self.over_x(t))
+                step(f"{name}_z{t}")(lambda t=t: self.over_z(t))
+
+        def rows(self, d, t):
+            return pl.ds(pl.multiple_of(256 * t + 64 * piece(chips[d]), 64), 64)
+
+        def over_x(self, t):
+            for d, slot in ((3, 1), (1, 0)):
+                w.send(self.buf.at[self.rows(d, t)], self.into.at[slot, t], quad(1, 0), self.sems[slot][t])
+
+        def over_z(self, t):
+            w.arrived(self.into.at[1, t], self.sems[1][t])
+            total = self.buf[self.rows(2, t), :].astype(F32) + self.into[1, t].astype(F32)
+            rsz[self.which, t] = total.astype(BF)
+            w.send(rsz.at[self.which, t], self.into.at[2, t], quad(2, 0), self.sems[2][t])
+
+        def result(self, t):
+            total = self.buf[self.rows(0, t), :].astype(F32)
+            for slot in (0, 2):
+                w.arrived(self.into.at[slot, t], self.sems[slot][t])
+                total = total + self.into[slot, t].astype(F32)
+            return total
+
+    sum_ds, sum_os, sum_df = Sum("ds", dsb, dsr, 0), Sum("os", osb, osr, 1), Sum("df", dfb, dfr, 2)
+
+    s_act, s_gr, s_gt = many(2), many(2, 2), many(2)
+    acted = []
+
+    def part_steps(part):
+        start, rows_kept, buf, acts, count, second = parts[part]
+        span = pl.ds(start, rows_kept)
+
+        def feed_forward(t):
+            @step(f"ff{part}{t}")
+            def _():
+                if part == 1 and t == 0:
+                    w.finish(acted)
+                rows = pl.ds(pl.multiple_of(my_rows + 256 * t, 256), 256)
+                here = pl.ds(256 * t, 256)
+                gate = _nt(sec2[rows, :], buf[0])
+                up = _nt(sec2[rows, :], buf[1])
+                d_hidden = _nt(dy2[rows, :], buf[2])
+                sigmoid = 1.0 / (1.0 + jnp.exp(-gate))
+                silu = gate * sigmoid
+                d_gate = (d_hidden * up * (sigmoid + silu * (1.0 - sigmoid))).astype(BF)
+                d_up = (d_hidden * silu).astype(BF)
+                hidden = (silu * up).astype(BF)
+                for n, value in enumerate((d_gate, d_up, hidden)):
+                    acts[n, rows, :] = value[:, 0:second]
+                    asend[n, here, 0:count] = value[:, second : second + count]
+                lanes = pl.ds(0, second)
+                acted.append(w.send(asend.at[:, here, lanes], acts.at[:, rows], sib, s_act[part]))
+                d_second = _nn(d_gate, buf[0]) + _nn(d_up, buf[1])
+                result = _nn(hidden, buf[2])
+                if part == 1:
+                    d_second = d_second + dsb[here, :].astype(F32)
+                    result = result + osb[here, :].astype(F32)
+                dsb[here, :] = d_second.astype(BF)
+                osb[here, :] = result.astype(BF)
+                if part == 1:
+                    sum_ds.over_x(t)
+
+        @step(f"wg{part}_in")
+        def _():
+            w.finish(held[part])
+            w.arrived(acts.at[:, pl.ds(0, 512)], s_act[part])
+            if part == 0:
+                w.arrived(sec2.at[pl.ds(0, 512)], s_sec)
+                w.arrived(dy2.at[pl.ds(0, 512)], s_dy)
+
+        def weight_grads(kind):
+            @step(f"wg{part}{kind}")
+            def _():
+                right = dy2 if kind == 2 else sec2
+
+                def columns(n, carry):
+                    cols = pl.ds(pl.multiple_of(n * 512, 512), 512)
+                    buf[kind, 0:count, cols] = _tn(acts[kind], right[:, cols])[0:count, :].astype(BF)
+                    return carry
+
+                lax.fori_loop(0, 2, columns, 0)
+
+        def send_grads(slot, to_slot):
+            @step(f"gr{part}_y{to_slot}")
+            def _():
+                rows = buf.at[:, pl.ds(rows_kept * slot, rows_kept)]
+                w.send(rows, gr.at[to_slot, :, span], yp, s_gr[to_slot][part])
+
+        @step(f"gr{part}_z")
+        def _():
+            w.arrived(gr.at[1, :, span], s_gr[1][part])
+            for kind in range(3):
+                gs[kind, span, :] = (
+                    buf[kind, 2 * rows_kept : 3 * rows_kept, :].astype(F32) + gr[1, kind, span, :].astype(F32)
+                ).astype(BF)
+            w.send(gs.at[:, span], gt.at[:, span], zp, s_gt[part])
+
+        @step(f"gr{part}_end")
+        def _():
+            w.arrived(gr.at[0, :, span], s_gr[0][part])
+            w.arrived(gt.at[:, span], s_gt[part])
+            for kind in range(3):
+                o_ffn[kind, span, :] = (
+                    buf[kind, 0:rows_kept, :].astype(F32)
+                    + gr[0, kind, span, :].astype(F32) + gt[kind, span, :].astype(F32)
+                )
+
+        feed_forward(0)
+        feed_forward(1)
+        for kind in range(3):
+            weight_grads(kind)
+        send_grads(3, 1)
+        send_grads(1, 0)
+
+    part_steps(0)
+    part_steps(1)
+
+    s_dm, s_da, s_das = w.sem(), many(3), w.sem()
+    terms = {"ffn": jnp.zeros((1, 1024), F32), "attn": jnp.zeros((1, 1024), F32)}
+
+    def state_steps(t):
+        @step(f"st{t}")
+        def _():
+            start = 256 * t + 64 * mine
+            rows = pl.ds(pl.multiple_of(start, 64), 64)
+            state = x[rows, :].astype(F32) + attended_rows(rows)
+            bos[t] = state
+            scale = lax.rsqrt(jnp.mean(state * state, axis=1, keepdims=True) + EPS)
+            normed = state * scale
+            total = sum_ds.result(t)
+            terms["ffn"] = terms["ffn"] + jnp.sum(total * normed, axis=0, keepdims=True)
+            weighted = total * ffn_gain()
+            inner = jnp.mean(weighted * normed, axis=1, keepdims=True)
+            grad = dy2[pl.ds(pl.multiple_of(my_rows + start, 64), 64), :].astype(F32) + scale * (weighted - normed * inner)
+            dstate[t] = grad
+            low_grad = grad.astype(BF)
+            daf[k, t, mine] = low_grad
+            for n in range(4):
+                dmb[t, :, 256 * n : 256 * (n + 1)] = _nt(low_grad, wall[n].reshape(256, 1024)).astype(BF)
+            for d, e in others:
+                lanes = pl.ds(pl.multiple_of(LANES * (2 * chips[d] + cores[e]), LANES), LANES)
+                w.send(dmb.at[t, :, lanes], dmix.at[k, t, mine], quad(d, e), s_dm)
+            w.local(dmb.at[t, :, head_lanes], dmix.at[k, t, mine], s_dm)
+
+    state_steps(0)
+    state_steps(1)
+
+    @step("da_out")
+    def _():
+        for d in (2, 1):
+            w.send(daf.at[k, :, mine], daf.at[k, :, mine], quad(d, 0), s_da[d - 1])
+
+    @step("da_fwd")
+    def _():
+        far = piece(chips[2])
+        w.arrived(daf.at[k, :, far], s_da[1])
+        w.send(daf.at[k, :, far], daf.at[k, :, far], quad(1, 0), s_da[2])
+
+    @step("da_sib")
+    def _():
+        for d in (1, 3):
+            w.arrived(daf.at[k, :, mine], s_da[d - 1])
+        w.send(daf.at[k], daf.at[k], sib, s_das)
+
+    home = zh + k * (1 - 2 * zh)
+
+    def send_home(buf, into, sem):
+        w.send(buf.at[1 - home, 0], into.at[zh, k], zp, sem)
+        w.send(buf.at[1 - home, 1], into.at[zh, k], zps, sem)
+        w.send(buf.at[home, 1], into.at[zh, k], sib, sem)
+        w.local(buf.at[home, 0], into.at[zh, k], sem)
+
+    s_bo, s_tg = w.sem(), w.sem()
+
+    @step("block")
+    def _():
+        for t in range(2):
+            total = bos[t] + sum_os.result(t)
+            obs[t] = total.astype(BF).reshape(2, 32, 1024)
+        send_home(obs, bor, s_bo)
+
+    @step("block_end")
+    def _():
+        w.arrived(bor, s_bo)
+        o_block[...] = bor[...]
+
+    @step("bw_in")
+    def _():
+        w.arrived(dmix, s_dm)
+        dkk[...] = jnp.zeros_like(dkk)
+        dvv[...] = jnp.zeros_like(dvv)
+
+    def backward_tile(t):
+        @step(f"bw{t}")
+        def _():
+            lo, n = 256 * t, 256 * (t + 1)
+            d_out = dmix[...].reshape(1024, LANES)[lo : lo + 256, :].astype(F32)
+            product = d_out * att[lo : lo + 256, :]
+            results = []
+            for h, q in enumerate((q0, q1)):
+                here = low if h == 0 else jnp.logical_not(low)
+                d_head = jnp.where(here, d_out, 0.0).astype(BF)
+                delta = jnp.sum(jnp.where(here, product, 0.0), axis=1, keepdims=True)
+                weights = prob[h, lo : lo + 256, 0:n]
+                pulled = _nt(d_head, vv[0:n, :])
+                d_scores = (weights.astype(F32) * (pulled - delta)).astype(BF)
+                results.append(_nn(d_scores, kk[0:n, :]))
+                dkk[0:n, :] += _tn(d_scores, q[lo : lo + 256, :])
+                dvv[0:n, :] += _tn(weights, d_head)
+            dqq[lo : lo + 256, :] = jnp.where(low, results[0], results[1]) * (HEAD_DIM**-0.5)
+
+    for t in range(4):
+        backward_tile(t)
+    s_dpx = w.sem()
+
+    @step("back")
+    def _():
+        query_weight, key_weight = query_gain(), key_gain()
+
+        def back_rows(t, carry):
+            query_sum, key_sum = carry
+            rows = pl.ds(pl.multiple_of(t * 256, 256), 256)
+            cosine, sine = cos_t[rows, :], sin_t[rows, :]
+            query = raw[rows, 0:LANES]
+            both = raw[rows, LANES : 2 * LANES]
+
+            def through(values, grads, gain_row):
+                scale = inverse_root(values)
+                normed = values * scale
+                grads = grads * cosine - swap(grads) * sine
+                weighted = grads * gain_row
+                inner = head_sum(weighted * normed) * (1.0 / HEAD_DIM)
+                return scale * (weighted - normed * inner), jnp.sum(grads * normed, axis=0, keepdims=True)
+
+            query_back, query_term = through(query, dqq[rows, :], query_weight)
+            d_key = dkk[rows, :]
+            d_key = d_key + pltpu.roll(d_key, HALF_LANES, 1)
+            key_back, key_term = through(both, d_key, key_weight)
+            d_value = dvv[rows, :]
+            d_value = d_value + pltpu.roll(d_value, HALF_LANES, 1)
+            dpj[rows, 0:LANES] = query_back.astype(BF)
+            dpj[rows, LANES : 2 * LANES] = jnp.where(low, key_back, d_value).astype(BF)
+            return query_sum + query_term, key_sum + key_term
+
+        zero_row = jnp.zeros((1, LANES), F32)
+        query_sum, key_sum = lax.fori_loop(0, 4, back_rows, (zero_row, zero_row))
+        w.send(dpj.at[pl.ds(other_rows, 512)], dpx, sib, s_dpx)
+        gg[:, 2 * LANES : 3 * LANES] = jnp.zeros((8, LANES), F32)
+        gg[0:1, 2 * LANES : 3 * LANES] = query_sum + pltpu.roll(query_sum, HALF_LANES, 1)
+        gg[1:2, 2 * LANES : 3 * LANES] = key_sum
+
+    def first_steps(t):
+        @step(f"df{t}")
+        def _():
+            if t == 0:
+                w.arrived(dpx, s_dpx)
+            here = pl.ds(256 * t, 256)
+            rows = pl.ds(pl.multiple_of(my_rows + 256 * t, 256), 256)
+            dfb[here, :] = (_nn(dpj[rows, :], w2[own_head, :]) + _nn(dpx[here, :], w2[sib_head, :])).astype(BF)
+            sum_df.over_x(t)
+
+    first_steps(0)
+    first_steps(1)
+    s_back = w.sem()
+
+    def term_steps(name, rows, value):
+        sem = many(3)
+
+        @step(f"{name}_y")
+        def _():
+            term = value()
+            count = rows.stop - rows.start
+            for p in range(4):
+                igs[p, rows, :] = term[count * p : count * (p + 1), :].astype(BF)
+            at = pl.ds(rows.start, count)
+            w.send(igs.at[team_d, at], agr.at[1, at], yp, sem[1])
+            w.send(igs.at[team_y, at], agr.at[0, at], yp, sem[0])
+
+        at = pl.ds(rows.start, rows.stop - rows.start)
+
+        @step(f"{name}_z")
+        def _():
+            w.arrived(agr.at[1, at], sem[1])
+            agz[rows, :] = (igs[team_z, rows, :].astype(F32) + agr[1, rows, :].astype(F32)).astype(BF)
+            w.send(agz.at[at], agt.at[at], zp, sem[2])
+
+        @step(f"{name}_sum")
+        def _():
+            w.arrived(agr.at[0, at], sem[0])
+            w.arrived(agt.at[at], sem[2])
+            agh[rows, :] = (
+                igs[team, rows, :].astype(F32) + agr[0, rows, :].astype(F32) + agt[rows, :].astype(F32)
+            ).astype(BF)
+
+    def in_value():
+        w.arrived(first2.at[pl.ds(0, 512)], s_first)
+        return _tn(dpj[...], first2[...])
+
+    def out_value():
+        w.arrived(daf.at[0], s_das)
+        return _tn(mxs[...], daf[...].reshape(1024, 1024))
+
+    term_steps("in", slice(0, 64), in_value)
+    term_steps("out", slice(64, 96), out_value)
+    give = pltpu.make_async_remote_copy(
+        src_ref=agh, dst_ref=ago, send_sem=w.sem(), recv_sem=s_back, device_id=owner_of, device_id_type=MESH,
+    )
+
+    @step("give")
+    def _():
+        pl.when(apart)(give.start)
+        pl.when(alone)(lambda: pltpu.make_async_copy(agh, ago, s_back).start())
+
+    @step("given")
+    def _():
+        w.arrived(ago, s_back)
+        o_in[...] = ago[0:64, :].astype(F32)
+        o_out[...] = ago[64:96, :].astype(F32)
+
+    def token_steps(t):
+        @step(f"tg{t}")
+        def _():
+            rows = pl.ds(pl.multiple_of(256 * t + 64 * mine, 64), 64)
+            values = x[rows, :].astype(F32)
+            scale = lax.rsqrt(jnp.mean(values * values, axis=1, keepdims=True) + EPS)
+            normed = values * scale
+            total = sum_df.result(t)
+            terms["attn"] = terms["attn"] + jnp.sum(total * normed, axis=0, keepdims=True)
+            weighted = total * attn_gain()
+            inner = jnp.mean(weighted * normed, axis=1, keepdims=True)
+            grad = dstate[t] + scale * (weighted - normed * inner)
+            tgs[t] = grad.astype(BF).reshape(2, 32, 1024)
+
+    token_steps(0)
+    token_steps(1)
+
+    @step("tok_home")
+    def _():
+        send_home(tgs, tgr, s_tg)
+
+    @step("tok_end")
+    def _():
+        w.arrived(tgr, s_tg)
+        o_tokens[...] = tgr[...].astype(F32)
+
+    s_gg, s_gt4 = w.sem(), many(3)
+
+    @step("gg_out")
+    def _():
+        for n in range(8):
+            gg[n : n + 1, 0:LANES] = terms["attn"][:, LANES * n : LANES * (n + 1)]
+            gg[n : n + 1, LANES : 2 * LANES] = terms["ffn"][:, LANES * n : LANES * (n + 1)]
+        for d, e in others:
+            w.send(gg, ggq.at[g], quad(d, e), s_gg)
+        w.local(gg, ggq.at[g], s_gg)
+
+    @step("gg_sum")
+    def _():
+        w.arrived(ggq, s_gg)
+        total = ggq[0]
+        for n in range(1, 8):
+            total = total + ggq[n]
+        gsum[...] = total
+        for n, peer in enumerate((yp, zp, diag)):
+            w.send(gsum, ggt.at[n], peer, s_gt4[n])
+
+    @step("gg_end")
+    def _():
+        total = gsum[...]
+        for n in range(3):
+            w.arrived(ggt.at[n], s_gt4[n])
+            total = total + ggt[n]
+        o_gain[...] = total
+
+    for name in ORDER:
+        steps.pop(name)()
+    assert not steps, sorted(steps)
+    w.finish()
+    for half, away in late:
+        pl.when(k != half)(away.wait_send)
+    pl.when(apart)(move.wait_send)
+    pl.when(apart)(give.wait_send)
+
+
+ORDER = (
+    "tok_out0", "wout_start", "u1_own", "tok_out1", "u0_z0", "move", "u0_y", "tok_own0", "cot_own1",
+    "wout_pass", "tok_rel1", "gain_start", "tok_rel0", "cot_out1", "moved", "win_start", "u0_f0", "u1_y",
+    "u0_z2", "u0_s1", "wout_end", "tok_fwd1", "tok_own1", "tok_fwd0", "gain_pass", "u1_z1", "win_pass",
+    "u0_f2", "u1_z0", "gain_end", "win_end", "cot_rel1", "cot_own0", "wout_fwd", "cot_out0", "gains", "u1_s1",
+    "u1_z2", "project", "rotate", "at1", "at3", "wout_sib", "at0", "u1_f1", "cot_fwd0", "u0_z1", "u1_f0",
+    "at2", "mix_fwd1", "u1_f2", "cot_rel0", "mix_fwd0", "u0_own", "u0_f1", "u1_s3", "cot_fwd1", "second",
+    "u0_s3", "u1_all", "dy", "u0_all", "ff00", "ff01", "ff10", "wg0_in", "wg01", "wg02", "wg00", "gr0_y1",
+    "ff11", "ds_z0", "st0", "ds_z1", "wg1_in", "wg10", "wg11", "wg12", "os_x0", "gr0_z", "st1", "os_z0",
+    "gr1_y1", "os_x1", "bw_in", "bw3", "bw2", "da_out", "first_sib", "bw1", "bw0", "back", "gr0_y0", "df0",
+    "gr1_z", "in_y", "da_fwd", "df_z0", "da_sib", "os_z1", "df1", "in_z", "out_y", "tg0", "df_z1", "out_z",
+    "in_sum", "gr1_y0", "block", "tg1", "gg_out", "tok_home", "gr0_end", "out_sum", "give", "block_end",
+    "gr1_end", "gg_sum", "tok_end", "gg_end", "given",
+)
+
+
+TEAM_SCRATCH = (
+    ((512, 1024), BF), ((2, 32, 1024), BF), ((2, 32, 1024), BF), ((512, 1024), BF),
+    ((4, 4, 2, 32, 1024), BF), ((3, 704, 1024), BF), ((3, 512, 1024), BF), ((4, 8, 8, 128), F32), ((8, 1024), F32),
+    ((1024, 1024), BF), ((1024, 256), F32), ((512, 256), F32),
+    ((1024, 128), BF), ((1024, 128), BF), ((1024, 128), BF), ((1024, 128), BF), ((2, 1024, 1024), BF),
+    ((1024, 128), F32), ((1024, 128), BF), ((512, 1024), BF), ((1024, 1024), BF), ((1024, 1024), BF),
+    ((3, 1024, 384), BF), ((3, 1024, 256), BF), ((3, 512, 384), BF),
+    ((512, 1024), BF), ((512, 1024), BF), ((3, 2, 64, 1024), BF), ((3, 2, 64, 1024), BF), ((3, 2, 64, 1024), BF),
+    ((2, 3, 144, 1024), BF), ((3, 144, 1024), BF), ((3, 144, 1024), BF),
+    ((2, 64, 1024), F32), ((2, 64, 1024), BF), ((2, 2, 4, 64, 1024), BF), ((2, 2, 4, 64, 128), BF),
+    ((1024, 128), F32), ((1024, 128), F32), ((1024, 128), F32), ((1024, 256), BF), ((512, 256), BF),
+    ((512, 1024), BF), ((3, 2, 64, 1024), BF),
+    ((4, 96, 1024), BF), ((2, 96, 1024), BF), ((96, 1024), BF), ((96, 1024), BF), ((96, 1024), BF), ((96, 1024), BF),
+    ((2, 64, 1024), F32), ((2, 2, 32, 1024), BF), ((2, 2, 32, 1024), BF), ((2, 2, 32, 1024), BF),
+    ((2, 2, 32, 1024), BF),
+    ((8, 384), F32), ((8, 8, 384), F32), ((8, 384), F32), ((3, 8, 384), F32),
+)
+
+
+def rotary_lanes(rows):
+    width = HEAD_DIM // 2
+    freq = (ROPE_BASE ** (-np.arange(width, dtype=np.float32) * np.float32(2.0 / HEAD_DIM))).astype(np.float32)
+    angle = (np.arange(rows, dtype=np.float32)[:, None] * freq).astype(np.float32).astype(np.float64)
+    cosine, sine = np.cos(angle), np.sin(angle)
+    return (
+        np.tile(np.concatenate([cosine, cosine], 1), (1, 2)).astype(np.float32),
+        np.tile(np.concatenate([-sine, sine], 1), (1, 2)).astype(np.float32),
+    )
+
+
+def on_team(tokens, segments, lengths, attn_in, attn_out, gains, ffn_weights, cotangent):
+    batches, block_len, halves, width = tokens.shape
+    here = lax.axis_index("ctx")
+    seq = here // 8
+    rows = segments.shape[1]
+    docs = lax.dynamic_index_in_dim(segments, seq, 0, False)
+    back = docs[:, 1].reshape(rows // block_len, block_len)[::-1].reshape(rows)
+    docs = jnp.concatenate([docs[:, 0], back])
+    limit = lax.dynamic_index_in_dim(lengths, seq, 0, False)
+    doc_row = jnp.where(jnp.arange(2 * rows, dtype=jnp.int32) < limit, docs, -1)
+    cosine, sine = rotary_lanes(2 * rows)
+    args = (
+        tokens.transpose(0, 2, 1, 3),
+        cotangent.transpose(0, 2, 1, 3),
+        attn_in,
+        attn_out,
+        jnp.pad(gains.astype(F32)[None], ((0, 7), (0, LANES - gains.shape[0]))),
+        ffn_weights.transpose(1, 0, 2),
+        docs[:, None],
+        doc_row[None],
+        jnp.broadcast_to(limit, (8, LANES)),
+        jnp.asarray(cosine),
+        jnp.asarray(sine),
+    )
+    vmem = pl.BlockSpec(memory_space=pltpu.VMEM)
+    outs = pl.pallas_call(
+        block_kernel,
+        out_shape=(
+            jax.ShapeDtypeStruct((2, 2, 32, 1024), BF),
+            jax.ShapeDtypeStruct((2, 2, 32, 1024), F32),
+            jax.ShapeDtypeStruct((64, 1024), F32),
+            jax.ShapeDtypeStruct((32, 1024), F32),
+            jax.ShapeDtypeStruct((8, 384), F32),
+            jax.ShapeDtypeStruct((3, 144, 1024), F32),
+        ),
+        in_specs=[vmem] * len(args),
+        out_specs=(vmem,) * 6,
+        scratch_shapes=[pltpu.VMEM(shape, kind) for shape, kind in TEAM_SCRATCH]
+        + [pltpu.SemaphoreType.DMA((COPIES,))],
+        compiler_params=pltpu.CompilerParams(
+            collective_id=0, has_side_effects=True, vmem_limit_bytes=VMEM_BYTES
+        ),
+    )(*args)
+    block, token_grad, in_grad, out_grad, gain_grad, unit_grad = outs
+    every = jnp.concatenate(
+        [gain_grad[:, :128].reshape(-1), gain_grad[:, 128:256].reshape(-1), gain_grad[0, 256:320], gain_grad[1, 256:320]]
+    )
+    own = lax.axis_index("dp") * lax.axis_size("ctx") + here
+    return (
+        block.transpose(0, 2, 1, 3),
+        token_grad.transpose(0, 2, 1, 3),
+        in_grad,
+        out_grad,
+        lax.dynamic_slice_in_dim(every, own * gains.shape[0], gains.shape[0], 0),
+        unit_grad.transpose(1, 0, 2),
+    )
+
+
+VMEM_BYTES = 62 << 20
+
+
 def solution(mesh):
     dp, ctx = mesh.devices.shape
-    team = Mesh(mesh.devices.reshape(dp, 2, ctx // (2 * KV_HEADS), KV_HEADS), EVERY)
-    ring = ("s", "q", "g")
+    if ctx == 2 * KV_HEADS:
+        ring = "ctx"
+        every = ("dp", "ctx")
+        team, run = mesh, on_team
+    else:
+        ring = ("s", "q", "g")
+        every = EVERY
+        team = Mesh(mesh.devices.reshape(dp, 2, ctx // (2 * KV_HEADS), KV_HEADS), EVERY)
+        run = on_device
     placed = (
         P("dp", ring, None, None),
         P("dp", None, None),
         P("dp"),
-        P(EVERY, None),
-        P(EVERY, None),
-        P(EVERY),
-        P(EVERY, None, None),
+        P(every, None),
+        P(every, None),
+        P(every),
+        P(every, None, None),
         P("dp", ring, None, None),
     )
     return jax.shard_map(
-        on_device,
+        run,
         mesh=team,
         in_specs=placed,
         out_specs=(
             P("dp", ring, None, None),
             P("dp", ring, None, None),
-            P(EVERY, None),
-            P(EVERY, None),
-            P(EVERY),
-            P(EVERY, None, None),
+            P(every, None),
+            P(every, None),
+            P(every),
+            P(every, None, None),
         ),
         check_vma=False,
     )

time: 886 us -> 202 us (0.23); the launches traced: 877 us -> 202 us
  waiting for transfers between devices: 564 us -> 0 us
  Pallas kernels: 0 us -> 183 us
  blocking collectives: 124 us -> 0 us
  matrix products: 57.2 us -> 0 us
  other arithmetic: 50.2 us -> 2.5 us
  local copies, waits for them, and re-layouts: 58.3 us -> 15.7 us
  between operations: 15.1 us -> 0.7 us
    reduce_scatter x6 -> x0, waiting for transfers between devices: 406 us -> none  [the longest x1 148 us: on_device(): lax.psum_scatter(placed(in_term, QKV_ROWS), EVERY, scatter_dimension=0, t...]
    pallas_call x0 -> x1, Pallas kernels: none -> 183 us  [on_team(): pl.pallas_call(block_kernel, out_shape=(jax.ShapeDtypeStruct((2, 2, 32, 1...]
    all_gather x7 -> x0, waiting for transfers between devices: 156 us -> none  [the longest x1 67.7 us: on_device(): units = lax.all_gather(ffn_weights, TEAM, axis=0, tiled=True)]
    unnamed x2 -> x0, blocking collectives: 98.2 us -> none
    dot_general x20 -> x0, matrix products: 50.9 us -> none  [the longest x15 40.8 us: dot(): lax.dot_general(a, b, (((ca,), (cb,)), ((), ())), preferred_element_type=...]
    convert_element_type x11 -> x0, other arithmetic: 29.6 us -> none  [the longest x1 7.86 us: on_device(): first = (first_normed * attn_gain).astype(BF)]
    all_to_all x2 -> x0, blocking collectives: 25.5 us -> none  [spread(): mine = lax.all_to_all(local, 's', 0, 0, tiled=True)]
    convert_element_type x6 -> x0, local copies, waits for them, and re-layouts: 25 us -> none  [the longest x2 10.3 us: on_device(): inputs = inputs.reshape(count, width).astype(F32)]
  transfers between devices with their start and end apart: 15 -> 0, of which waited for: 10 -> 0; matrix products, arithmetic and copies ran while one was open for 15% -> 0% of each run, Pallas kernels for 0% -> 0%
where the time goes in v3:
time: 202 us
  Pallas kernels  183 us (91%)
  local copies, waits for them, and re-layouts  15.7 us (8%)
  other arithmetic  2.5 us (1%)
    pallas_call x1, Pallas kernels, on_team(): pl.pallas_call(block_kernel, out_shape=(jax.ShapeDtypeStruct((2, 2, 32, 1...  183 us
    unnamed x11, local copies, waits for them, and re-layouts  7.85 us

profile of v3, /device:TPU:0, one launch (start us, length us, event | category | flops | bytes accessed | tf_op | source)
XLA Modules:
  0.0 201.6 jit_solution(9198979637915655177)
XLA Ops:
  0.6 0.0 copy-start
  0.7 1.2 dynamic_slice.12
  1.9 0.0 copy-done
  1.9 1.2 broadcast_in_dim.18.length
  3.2 1.3 pad_convert_fusion.gain
  4.4 0.1 reshape_squeeze.3
  4.5 0.1 concatenate.21
  4.6 0.1 reshape.59
  4.7 1.2 compare_select_fusion.doc_row
  5.9 1.0 copy.22.doc_col
  7.0 1.9 copy_bitcast_fusion
  8.9 182.8 %shard_map.145 = (bf16[2,2,32,1024]{3,2,1,0:T(8,128)(2,1)}, f32[2,2,32,1024]{3,2,1,0:T(8,128)}, f32[64,1024]{1,0:T(8,128)}, f32[32,1024]{1,0:T(8,128)}, f32[8,384]{1,0:T(8,128)}, /*index=5*/f32[3,144,1024]{2,1,0:T(8,128)}) custom-call(bf16[2,2,32,1024]{3,2,1,0:T(8,128)(2,1)} %get-tuple-element.38.tok, bf16[2,2,32,1024]{3,2,1,0:T(8,128)(2,1)} %get-tuple-element.37.cot, ...), custom_call_target="tpu_custom_call" | custom-call | tf_op jit(solution)/shard_map/pallas_call | solution.py:1188
  191.7 0.0 copy-start.2
  191.7 2.1 %copy.23 = bf16[2,32,2,1024]{3,2,1,0:T(2,128)(2,1)} copy(bf16[2,32,2,1024]{3,1,2,0:T(8,128)(2,1)} %bitcast.27) | data formatting | bytes 524288
  193.8 2.2 %copy.24 = f32[2,32,2,1024]{3,2,1,0:T(2,128)} copy(f32[2,32,2,1024]{3,1,2,0:T(8,128)} %bitcast.26) | data formatting | bytes 1048576
  196.0 0.8 slice_bitcast_fusion.2
  196.8 0.7 slice_bitcast_fusion
  197.4 0.1 concatenate.23
  197.5 0.6 dynamic_slice.13
  198.1 1.7 copy.30
  199.8 0.0 copy-done.2
  199.8 0.7 copy.31
  200.4 0.0 copy-done.1
  200.4 1.2 copy.32
  (5 shorter events, 0.0 us)
Async XLA Ops:
  0.6 1.3 copy-start
  191.7 8.1 %copy-start.2 = (f32[32,1024]{1,0:T(8,128)S(1)}, f32[32,1024]{1,0:T(8,128)}, u32[]{:S(2)}) copy-start(f32[32,1024]{1,0:T(8,128)} %get-tuple-element.48) | copy-start | bytes 393220
  191.7 8.7 %copy-start.1 = (f32[3,144,1024]{2,1,0:T(8,128)S(1)}, f32[3,144,1024]{2,1,0:T(8,128)}, u32[]{:S(2)}) copy-start(f32[3,144,1024]{2,1,0:T(8,128)} %get-tuple-element.17) | copy-start | bytes 5308420

commit v4 on v3

--- a/solution.py
+++ b/solution.py
@@ -280,13 +280,13 @@
 
 
 def block_kernel(
-    tok, cot, win, wout, gain, wffn, doc_col, doc_row, length, cos_t, sin_t,
+    tok, cot, win, wout, gain_in, wffn, segments, lengths, cos_t, sin_t,
     o_block, o_tokens, o_in, o_out, o_gain, o_ffn,
     x, rel_t, rel_c, w2, wall, wfa, wfb, gb, grow, first2, raw, po,
     q0, q1, kk, vv, prob, att, mxs, mix, sec2, dy2, acta, actb, asend,
     dsb, osb, dsr, osr, rsz, gr, gs, gt, dstate, dmb, daf, dmix,
     dkk, dvv, dqq, dpj, dpx, dfb, dfr, igs, agr, agz, agt, agh, ago,
-    bos, obs, bor, tgs, tgr, gg, ggq, gsum, ggt, sems,
+    bos, obs, bor, tgs, tgr, gg, ggq, gsum, ggt, gain, gflat, doc_col, doc_row, sems,
 ):
     dp = lax.axis_index("dp")
     c = lax.axis_index("ctx")
@@ -323,6 +323,20 @@
     peers = [quad(d, e) for d, e in others] + [zp, zps, yp, diag]
     for peer in peers:
         pl.semaphore_signal(barrier, inc=1, device_id=peer, device_id_type=MESH)
+
+    limit = lengths[zh]
+    docs = segments[zh].astype(F32).astype(BF)
+    line = lax.broadcasted_iota(jnp.int32, (512, 512), 0)
+    cell = lax.broadcasted_iota(jnp.int32, (512, 512), 1)
+    same_place = (line == cell).astype(F32).astype(BF)
+    mirrored = (line + 480 - 2 * (line - lax.rem(line, 32)) == cell).astype(F32).astype(BF)
+    for half, order in enumerate((same_place, mirrored)):
+        ids = jnp.broadcast_to(docs[half : half + 1, :], (16, 512))
+        key = lax.broadcasted_iota(jnp.int32, (1, 512), 1) + 512 * half
+        doc_row[0:1, 512 * half : 512 * (half + 1)] = jnp.where(key < limit, _nn(ids, order)[0:1, :], -1.0)
+        doc_col[512 * half : 512 * (half + 1), :] = _nt(order, ids)[:, 0:8]
+    gain[...] = jnp.zeros_like(gain)
+    gain[0:1, 0:68] = gain_in[...].astype(F32)
 
     @pl.when(apart)
     def _():
@@ -643,7 +657,7 @@
             lo, n = 256 * t, 256 * (t + 1)
             place = lax.broadcasted_iota(jnp.int32, (256, n), 0) + lo
             key_place = lax.broadcasted_iota(jnp.int32, (256, n), 1)
-            same = doc_col[lo : lo + 256, :] == doc_row[0:1, 0:n]
+            same = doc_col[lo : lo + 256, 0:1] == doc_row[0:1, 0:n]
             mask = (same & (key_place <= place)) | (key_place == place)
             outs = []
             for h, q in enumerate((q0, q1)):
@@ -687,7 +701,6 @@
         w.arrived(dy2.at[pl.ds(0, 256)], s_c)
         w.arrived(dy2.at[pl.ds(0, 128)], s_cd)
         w.finish(cot_passed)
-        limit = length[0:1, 0:1]
 
         def drop_rows(t, carry):
             rows = pl.ds(pl.multiple_of(my_rows + t * 128, 128), 128)
@@ -1046,8 +1059,8 @@
     @step("given")
     def _():
         w.arrived(ago, s_back)
-        o_in[...] = ago[0:64, :].astype(F32)
-        o_out[...] = ago[64:96, :].astype(F32)
+        o_in[...] = ago[0:64, :]
+        o_out[...] = ago[64:96, :]
 
     def token_steps(t):
         @step(f"tg{t}")
@@ -1073,7 +1086,7 @@
     @step("tok_end")
     def _():
         w.arrived(tgr, s_tg)
-        o_tokens[...] = tgr[...].astype(F32)
+        o_tokens[...] = tgr[...]
 
     s_gg, s_gt4 = w.sem(), many(3)
 
@@ -1102,7 +1115,16 @@
         for n in range(3):
             w.arrived(ggt.at[n], s_gt4[n])
             total = total + ggt[n]
-        o_gain[...] = total
+        gflat[0:8, :] = total[:, 0:LANES]
+        gflat[8:16, :] = total[:, LANES : 2 * LANES]
+        key_part = pltpu.roll(total[1:2, 2 * LANES : 3 * LANES], HALF_LANES, 1)
+        gflat[16:17, :] = jnp.where(low_row, total[0:1, 2 * LANES : 3 * LANES], key_part)
+        place = 68 * (8 * team + g)
+        line, shift = lax.div(place, LANES), lax.rem(place, LANES)
+        back = lax.rem(LANES - shift, LANES)
+        left = pltpu.roll(gflat[pl.ds(line, 1), :], back, 1)
+        right = pltpu.roll(gflat[pl.ds(line + 1, 1), :], back, 1)
+        o_gain[...] = jnp.where(lane < LANES - shift, left, right)[:, 0:68]
 
     for name in ORDER:
         steps.pop(name)()
@@ -1115,18 +1137,18 @@
 
 
 ORDER = (
-    "tok_out0", "wout_start", "u1_own", "tok_out1", "u0_z0", "move", "u0_y", "tok_own0", "cot_own1",
-    "wout_pass", "tok_rel1", "gain_start", "tok_rel0", "cot_out1", "moved", "win_start", "u0_f0", "u1_y",
-    "u0_z2", "u0_s1", "wout_end", "tok_fwd1", "tok_own1", "tok_fwd0", "gain_pass", "u1_z1", "win_pass",
-    "u0_f2", "u1_z0", "gain_end", "win_end", "cot_rel1", "cot_own0", "wout_fwd", "cot_out0", "gains", "u1_s1",
-    "u1_z2", "project", "rotate", "at1", "at3", "wout_sib", "at0", "u1_f1", "cot_fwd0", "u0_z1", "u1_f0",
-    "at2", "mix_fwd1", "u1_f2", "cot_rel0", "mix_fwd0", "u0_own", "u0_f1", "u1_s3", "cot_fwd1", "second",
-    "u0_s3", "u1_all", "dy", "u0_all", "ff00", "ff01", "ff10", "wg0_in", "wg01", "wg02", "wg00", "gr0_y1",
-    "ff11", "ds_z0", "st0", "ds_z1", "wg1_in", "wg10", "wg11", "wg12", "os_x0", "gr0_z", "st1", "os_z0",
-    "gr1_y1", "os_x1", "bw_in", "bw3", "bw2", "da_out", "first_sib", "bw1", "bw0", "back", "gr0_y0", "df0",
-    "gr1_z", "in_y", "da_fwd", "df_z0", "da_sib", "os_z1", "df1", "in_z", "out_y", "tg0", "df_z1", "out_z",
-    "in_sum", "gr1_y0", "block", "tg1", "gg_out", "tok_home", "gr0_end", "out_sum", "give", "block_end",
-    "gr1_end", "gg_sum", "tok_end", "gg_end", "given",
+    "tok_own1", "tok_out0", "tok_out1", "gain_start", "move", "tok_own0", "tok_rel0", "wout_start",
+    "gain_pass", "moved", "win_start", "cot_out1", "tok_rel1", "tok_fwd0", "wout_pass", "u0_own", "gain_end",
+    "cot_own0", "cot_own1", "win_pass", "tok_fwd1", "u0_z0", "win_end", "u1_y", "wout_end", "gains",
+    "project", "u0_z2", "cot_out0", "rotate", "at2", "at0", "u0_z1", "u0_y", "cot_fwd0", "u0_f0", "at3",
+    "wout_fwd", "u1_s1", "at1", "u1_own", "cot_rel0", "u0_f2", "u0_f1", "u0_s1", "mix_fwd0", "cot_rel1",
+    "u1_z0", "u1_z1", "wout_sib", "mix_fwd1", "cot_fwd1", "u0_s3", "u1_f0", "u1_z2", "second", "u0_all",
+    "u1_f1", "dy", "ff00", "u1_f2", "ff01", "wg0_in", "wg00", "u1_s3", "wg02", "u1_all", "wg01", "gr0_y1",
+    "ff10", "ff11", "wg1_in", "wg11", "wg12", "wg10", "ds_z0", "ds_z1", "gr1_y1", "first_sib", "gr0_y0",
+    "os_x0", "gr0_z", "st0", "os_x1", "st1", "da_out", "os_z0", "os_z1", "bw_in", "gr1_z", "bw1", "bw3",
+    "gr0_end", "da_fwd", "bw0", "bw2", "back", "in_y", "df0", "df1", "da_sib", "df_z0", "in_z", "out_y",
+    "df_z1", "out_z", "block", "in_sum", "tg0", "gr1_y0", "tg1", "gg_out", "out_sum", "give", "tok_home",
+    "gr1_end", "gg_sum", "tok_end", "block_end", "gg_end", "given",
 )
 
 
@@ -1145,7 +1167,7 @@
     ((4, 96, 1024), BF), ((2, 96, 1024), BF), ((96, 1024), BF), ((96, 1024), BF), ((96, 1024), BF), ((96, 1024), BF),
     ((2, 64, 1024), F32), ((2, 2, 32, 1024), BF), ((2, 2, 32, 1024), BF), ((2, 2, 32, 1024), BF),
     ((2, 2, 32, 1024), BF),
-    ((8, 384), F32), ((8, 8, 384), F32), ((8, 384), F32), ((3, 8, 384), F32),
+    ((8, 384), F32), ((8, 8, 384), F32), ((8, 384), F32), ((3, 8, 384), F32), ((8, 128), F32), ((24, 128), F32), ((1024, 8), F32), ((8, 1024), F32),
 )
 
 
@@ -1162,25 +1184,17 @@
 
 def on_team(tokens, segments, lengths, attn_in, attn_out, gains, ffn_weights, cotangent):
     batches, block_len, halves, width = tokens.shape
-    here = lax.axis_index("ctx")
-    seq = here // 8
     rows = segments.shape[1]
-    docs = lax.dynamic_index_in_dim(segments, seq, 0, False)
-    back = docs[:, 1].reshape(rows // block_len, block_len)[::-1].reshape(rows)
-    docs = jnp.concatenate([docs[:, 0], back])
-    limit = lax.dynamic_index_in_dim(lengths, seq, 0, False)
-    doc_row = jnp.where(jnp.arange(2 * rows, dtype=jnp.int32) < limit, docs, -1)
     cosine, sine = rotary_lanes(2 * rows)
     args = (
         tokens.transpose(0, 2, 1, 3),
         cotangent.transpose(0, 2, 1, 3),
         attn_in,
         attn_out,
-        jnp.pad(gains.astype(F32)[None], ((0, 7), (0, LANES - gains.shape[0]))),
+        gains[None],
         ffn_weights.transpose(1, 0, 2),
-        docs[:, None],
-        doc_row[None],
-        jnp.broadcast_to(limit, (8, LANES)),
+        segments.transpose(0, 2, 1),
+        lengths,
         jnp.asarray(cosine),
         jnp.asarray(sine),
     )
@@ -1189,13 +1203,13 @@
         block_kernel,
         out_shape=(
             jax.ShapeDtypeStruct((2, 2, 32, 1024), BF),
-            jax.ShapeDtypeStruct((2, 2, 32, 1024), F32),
-            jax.ShapeDtypeStruct((64, 1024), F32),
-            jax.ShapeDtypeStruct((32, 1024), F32),
-            jax.ShapeDtypeStruct((8, 384), F32),
+            jax.ShapeDtypeStruct((2, 2, 32, 1024), BF),
+            jax.ShapeDtypeStruct((64, 1024), BF),
+            jax.ShapeDtypeStruct((32, 1024), BF),
+            jax.ShapeDtypeStruct((1, 68), F32),
             jax.ShapeDtypeStruct((3, 144, 1024), F32),
         ),
-        in_specs=[vmem] * len(args),
+        in_specs=[vmem] * 7 + [pl.BlockSpec(memory_space=pltpu.SMEM)] + [vmem] * 2,
         out_specs=(vmem,) * 6,
         scratch_shapes=[pltpu.VMEM(shape, kind) for shape, kind in TEAM_SCRATCH]
         + [pltpu.SemaphoreType.DMA((COPIES,))],
@@ -1204,16 +1218,12 @@
         ),
     )(*args)
     block, token_grad, in_grad, out_grad, gain_grad, unit_grad = outs
-    every = jnp.concatenate(
-        [gain_grad[:, :128].reshape(-1), gain_grad[:, 128:256].reshape(-1), gain_grad[0, 256:320], gain_grad[1, 256:320]]
-    )
-    own = lax.axis_index("dp") * lax.axis_size("ctx") + here
     return (
         block.transpose(0, 2, 1, 3),
-        token_grad.transpose(0, 2, 1, 3),
-        in_grad,
-        out_grad,
-        lax.dynamic_slice_in_dim(every, own * gains.shape[0], gains.shape[0], 0),
+        token_grad.transpose(0, 2, 1, 3).astype(F32),
+        in_grad.astype(F32),
+        out_grad.astype(F32),
+        gain_grad[0],
         unit_grad.transpose(1, 0, 2),
     )
 

time: 202 us -> 182 us (0.901)
  Pallas kernels: 183 us -> 172 us
  local copies, waits for them, and re-layouts: 15.7 us -> 5.85 us
    pallas_call x1, Pallas kernels: 183 us -> 172 us  [on_team(): pl.pallas_call(block_kernel, out_shape=(jax.ShapeDtypeStruct((2, 2, 32, 1...]
    unnamed x11 -> x12, local copies, waits for them, and re-layouts: 7.85 us -> 3.91 us
    convert_element_type x0 -> x3, other arithmetic: none -> 3.42 us  [the longest x1 1.62 us: on_team(): in_grad.astype(F32)]
    broadcast_in_dim x2 -> x0, local copies, waits for them, and re-layouts: 2.27 us -> none  [the longest x1 1.24 us: on_team(): jnp.broadcast_to(limit, (8, LANES))]
where the time goes in v4:
time: 182 us
  Pallas kernels  172 us (95%)
  local copies, waits for them, and re-layouts  5.85 us (3%)
  other arithmetic  3.42 us (2%)
    pallas_call x1, Pallas kernels, on_team(): pl.pallas_call(block_kernel, out_shape=(jax.ShapeDtypeStruct((2, 2, 32, 1...  172 us
    unnamed x12, local copies, waits for them, and re-layouts  3.91 us

profile of v4, /device:TPU:0, one launch (start us, length us, event | category | flops | bytes accessed | tf_op | source)
XLA Modules:
  0.0 182.2 jit_solution(160585068017275868)
XLA Ops:
  0.6 1.9 %copy_bitcast_fusion = (bf16[2,2,32,1024]{3,2,1,0:T(8,128)(2,1)}, bf16[2,2,32,1024]{3,2,1,0:T(8,128)(2,1)}) fusion(bf16[2,32,2,1024]{3,2,1,0:T(2,128)(2,1)} %param.17, bf16[2,32,2,1024]{3,2,1,0:T(2,128)(2,1)} %param.10), kind=kLoop, calls=%fused_computation.1 | loop fusion | bytes 1048576 | tf_op jit(solution)/shard_map/transpose | solution.py:1191
  2.6 172.2 %shard_map.145 = (bf16[2,2,32,1024]{3,2,1,0:T(8,128)(2,1)}, bf16[2,2,32,1024]{3,2,1,0:T(8,128)(2,1)}, bf16[64,1024]{1,0:T(8,128)(2,1)}, bf16[32,1024]{1,0:T(8,12...) custom-call(bf16[2,2,32,1024]{3,2,1,0:T(8,128)(2,1)} %get-tuple-element.25.tok, ...), custom_call_target="tpu_custom_call" | custom-call | tf_op jit(solution)/shard_map/pallas_call | solution.py:1202
  174.8 0.0 copy-start.1
  174.8 0.0 copy-start.2
  174.8 0.0 copy-start.3
  174.8 0.0 copy-start
  174.8 1.1 convert_bitcast_fusion
  176.0 1.2 copy.19
  177.2 1.6 convert_element_type.14
  178.8 0.0 copy-done.1
  178.8 1.0 copy.18
  179.8 0.0 copy-done.2
  179.8 0.7 convert_element_type.15
  180.4 0.0 copy-done.3
  180.4 0.5 copy.24
  180.9 0.0 copy-done
  181.0 1.2 copy.25
Async XLA Ops:
  174.8 4.0 %copy-start.1 = (bf16[2,2,32,1024]{3,2,1,0:T(8,128)(2,1)S(1)}, bf16[2,2,32,1024]{3,2,1,0:T(8,128)(2,1)}, u32[]{:S(2)}) copy-start(bf16[2,2,32,1024]{3,2,1,0:T(8,128)(2,1)} %get-tuple-element.12) | copy-start | bytes 786436
  174.8 5.0 %copy-start.2 = (bf16[32,1024]{1,0:T(8,128)(2,1)S(1)}, bf16[32,1024]{1,0:T(8,128)(2,1)}, u32[]{:S(2)}) copy-start(bf16[32,1024]{1,0:T(8,128)(2,1)} %get-tuple-element.15) | copy-start | bytes 196612
  174.8 5.6 %copy-start.3 = (f32[1,68]{1,0:T(1,128)S(1)}, f32[1,68]{1,0:T(1,128)}, u32[]{:S(2)}) copy-start(f32[1,68]{1,0:T(1,128)} %get-tuple-element.16) | copy-start | bytes 820
  174.8 6.1 %copy-start = (f32[3,144,1024]{2,1,0:T(8,128)S(1)}, f32[3,144,1024]{2,1,0:T(8,128)}, u32[]{:S(2)}) copy-start(f32[3,144,1024]{2,1,0:T(8,128)} %get-tuple-element.17) | copy-start | bytes 5308420

commit v5 on v4

--- a/solution.py
+++ b/solution.py
@@ -705,8 +705,8 @@
         def drop_rows(t, carry):
             rows = pl.ds(pl.multiple_of(my_rows + t * 128, 128), 128)
             place = lax.broadcasted_iota(jnp.int32, (128, 1), 0) + (my_rows + t * 128)
-            kept = (place < limit).astype(F32)
-            dy2[rows, :] = (dy2[rows, :].astype(F32) * kept).astype(BF)
+            kept = (place < limit).astype(F32).astype(BF)
+            dy2[rows, :] = dy2[rows, :] * kept
             return carry
 
         lax.fori_loop(0, 4, drop_rows, 0)
@@ -768,7 +768,7 @@
 
     sum_ds, sum_os, sum_df = Sum("ds", dsb, dsr, 0), Sum("os", osb, osr, 1), Sum("df", dfb, dfr, 2)
 
-    s_act, s_gr, s_gt = many(2), many(2, 2), many(2)
+    s_act, s_gr, s_near, s_gt = many(2), many(2, 3), many(2), many(2, 3)
     acted = []
 
     def part_steps(part):
@@ -825,26 +825,29 @@
 
                 lax.fori_loop(0, 2, columns, 0)
 
-        def send_grads(slot, to_slot):
-            @step(f"gr{part}_y{to_slot}")
+        def pass_grads(kind):
+            @step(f"gr{part}_y{kind}")
             def _():
-                rows = buf.at[:, pl.ds(rows_kept * slot, rows_kept)]
-                w.send(rows, gr.at[to_slot, :, span], yp, s_gr[to_slot][part])
-
-        @step(f"gr{part}_z")
-        def _():
-            w.arrived(gr.at[1, :, span], s_gr[1][part])
-            for kind in range(3):
+                rows = buf.at[kind, pl.ds(rows_kept * 3, rows_kept)]
+                w.send(rows, gr.at[1, kind, span], yp, s_gr[part][kind])
+
+            @step(f"gr{part}_z{kind}")
+            def _():
+                w.arrived(gr.at[1, kind, span], s_gr[part][kind])
                 gs[kind, span, :] = (
                     buf[kind, 2 * rows_kept : 3 * rows_kept, :].astype(F32) + gr[1, kind, span, :].astype(F32)
                 ).astype(BF)
-            w.send(gs.at[:, span], gt.at[:, span], zp, s_gt[part])
+                w.send(gs.at[kind, span], gt.at[kind, span], zp, s_gt[part][kind])
+
+        @step(f"gr{part}_near")
+        def _():
+            w.send(buf.at[:, pl.ds(rows_kept, rows_kept)], gr.at[0, :, span], yp, s_near[part])
 
         @step(f"gr{part}_end")
         def _():
-            w.arrived(gr.at[0, :, span], s_gr[0][part])
-            w.arrived(gt.at[:, span], s_gt[part])
+            w.arrived(gr.at[0, :, span], s_near[part])
             for kind in range(3):
+                w.arrived(gt.at[kind, span], s_gt[part][kind])
                 o_ffn[kind, span, :] = (
                     buf[kind, 0:rows_kept, :].astype(F32)
                     + gr[0, kind, span, :].astype(F32) + gt[kind, span, :].astype(F32)
@@ -854,8 +857,7 @@
         feed_forward(1)
         for kind in range(3):
             weight_grads(kind)
-        send_grads(3, 1)
-        send_grads(1, 0)
+            pass_grads(kind)
 
     part_steps(0)
     part_steps(1)
@@ -1006,10 +1008,10 @@
 
     first_steps(0)
     first_steps(1)
-    s_back = w.sem()
-
-    def term_steps(name, rows, value):
-        sem = many(3)
+    returned = []
+
+    def term_steps(name, rows, value, result):
+        sem = many(4)
 
         @step(f"{name}_y")
         def _():
@@ -1037,6 +1039,22 @@
                 igs[team, rows, :].astype(F32) + agr[0, rows, :].astype(F32) + agt[rows, :].astype(F32)
             ).astype(BF)
 
+        back = pltpu.make_async_remote_copy(
+            src_ref=agh.at[at], dst_ref=ago.at[at], send_sem=w.sem(), recv_sem=sem[3],
+            device_id=owner_of, device_id_type=MESH,
+        )
+        returned.append(back)
+
+        @step(f"{name}_give")
+        def _():
+            pl.when(apart)(back.start)
+            pl.when(alone)(lambda: pltpu.make_async_copy(agh.at[at], ago.at[at], sem[3]).start())
+
+        @step(f"{name}_end")
+        def _():
+            w.arrived(ago.at[at], sem[3])
+            result[...] = ago[rows, :]
+
     def in_value():
         w.arrived(first2.at[pl.ds(0, 512)], s_first)
         return _tn(dpj[...], first2[...])
@@ -1045,22 +1063,8 @@
         w.arrived(daf.at[0], s_das)
         return _tn(mxs[...], daf[...].reshape(1024, 1024))
 
-    term_steps("in", slice(0, 64), in_value)
-    term_steps("out", slice(64, 96), out_value)
-    give = pltpu.make_async_remote_copy(
-        src_ref=agh, dst_ref=ago, send_sem=w.sem(), recv_sem=s_back, device_id=owner_of, device_id_type=MESH,
-    )
-
-    @step("give")
-    def _():
-        pl.when(apart)(give.start)
-        pl.when(alone)(lambda: pltpu.make_async_copy(agh, ago, s_back).start())
-
-    @step("given")
-    def _():
-        w.arrived(ago, s_back)
-        o_in[...] = ago[0:64, :]
-        o_out[...] = ago[64:96, :]
+    term_steps("in", slice(0, 64), in_value, o_in)
+    term_steps("out", slice(64, 96), out_value, o_out)
 
     def token_steps(t):
         @step(f"tg{t}")
@@ -1133,22 +1137,24 @@
     for half, away in late:
         pl.when(k != half)(away.wait_send)
     pl.when(apart)(move.wait_send)
-    pl.when(apart)(give.wait_send)
+    for back in returned:
+        pl.when(apart)(back.wait_send)
 
 
 ORDER = (
-    "tok_own1", "tok_out0", "tok_out1", "gain_start", "move", "tok_own0", "tok_rel0", "wout_start",
-    "gain_pass", "moved", "win_start", "cot_out1", "tok_rel1", "tok_fwd0", "wout_pass", "u0_own", "gain_end",
-    "cot_own0", "cot_own1", "win_pass", "tok_fwd1", "u0_z0", "win_end", "u1_y", "wout_end", "gains",
-    "project", "u0_z2", "cot_out0", "rotate", "at2", "at0", "u0_z1", "u0_y", "cot_fwd0", "u0_f0", "at3",
-    "wout_fwd", "u1_s1", "at1", "u1_own", "cot_rel0", "u0_f2", "u0_f1", "u0_s1", "mix_fwd0", "cot_rel1",
-    "u1_z0", "u1_z1", "wout_sib", "mix_fwd1", "cot_fwd1", "u0_s3", "u1_f0", "u1_z2", "second", "u0_all",
-    "u1_f1", "dy", "ff00", "u1_f2", "ff01", "wg0_in", "wg00", "u1_s3", "wg02", "u1_all", "wg01", "gr0_y1",
-    "ff10", "ff11", "wg1_in", "wg11", "wg12", "wg10", "ds_z0", "ds_z1", "gr1_y1", "first_sib", "gr0_y0",
-    "os_x0", "gr0_z", "st0", "os_x1", "st1", "da_out", "os_z0", "os_z1", "bw_in", "gr1_z", "bw1", "bw3",
-    "gr0_end", "da_fwd", "bw0", "bw2", "back", "in_y", "df0", "df1", "da_sib", "df_z0", "in_z", "out_y",
-    "df_z1", "out_z", "block", "in_sum", "tg0", "gr1_y0", "tg1", "gg_out", "out_sum", "give", "tok_home",
-    "gr1_end", "gg_sum", "tok_end", "block_end", "gg_end", "given",
+    "tok_out0", "cot_own1", "wout_start", "tok_out1", "cot_own0", "u0_y", "u1_own", "tok_own0", "move",
+    "tok_own1", "gain_start", "tok_rel0", "wout_pass", "cot_out0", "cot_fwd0", "tok_rel1", "gain_pass",
+    "moved", "cot_out1", "u0_s1", "gain_end", "win_start", "tok_fwd1", "tok_fwd0", "wout_end", "win_pass",
+    "u0_z1", "gains", "win_end", "u0_own", "cot_rel1", "project", "u1_y", "u0_z0", "wout_fwd", "cot_rel0",
+    "u0_z2", "rotate", "at1", "u0_f1", "at3", "u0_f0", "at0", "at2", "u1_z2", "cot_fwd1", "mix_fwd1", "u0_f2",
+    "mix_fwd0", "wout_sib", "u1_f2", "u0_s3", "u1_z1", "u0_all", "u1_z0", "dy", "second", "ff00", "u1_f1",
+    "ff01", "first_sib", "u1_f0", "u1_s1", "wg0_in", "wg01", "gr0_y1", "wg00", "u1_s3", "gr0_y0", "u1_all",
+    "ff10", "gr0_z1", "ff11", "ds_z0", "wg02", "gr0_z0", "wg1_in", "wg11", "wg12", "gr1_y1", "os_x0",
+    "gr0_y2", "wg10", "gr1_y2", "ds_z1", "gr1_y0", "st0", "gr1_z1", "st1", "gr0_near", "gr0_z2", "da_out",
+    "os_x1", "bw_in", "bw3", "bw2", "bw1", "gr1_z0", "bw0", "back", "gr1_z2", "os_z0", "os_z1", "da_fwd",
+    "in_y", "gr1_near", "df0", "in_z", "da_sib", "df_z0", "df1", "out_y", "block", "in_sum", "df_z1", "tg0",
+    "out_z", "in_give", "gr1_end", "tg1", "out_sum", "tok_home", "gg_out", "gg_sum", "in_end", "out_give",
+    "block_end", "gr0_end", "tok_end", "gg_end", "out_end",
 )
 
 

time: 182 us -> 169 us (0.929)
  Pallas kernels: 172 us -> 158 us
    pallas_call x1, Pallas kernels: 172 us -> 158 us  [on_team(): pl.pallas_call(block_kernel, out_shape=(jax.ShapeDtypeStruct((2, 2, 32, 1...]
where the time goes in v5:
time: 169 us; the launch traced here: 168 us
  Pallas kernels  158 us (93%)
  local copies, waits for them, and re-layouts  5.85 us (3%)
  other arithmetic  3.42 us (2%)
    pallas_call x1, Pallas kernels, on_team(): pl.pallas_call(block_kernel, out_shape=(jax.ShapeDtypeStruct((2, 2, 32, 1...  158 us
    unnamed x12, local copies, waits for them, and re-layouts  3.91 us

profile of v5, /device:TPU:0, one launch (start us, length us, event | category | flops | bytes accessed | tf_op | source)
XLA Modules:
  0.0 168.3 jit_solution(14352167831490077649)
XLA Ops:
  0.6 1.9 %copy_bitcast_fusion = (bf16[2,2,32,1024]{3,2,1,0:T(8,128)(2,1)}, bf16[2,2,32,1024]{3,2,1,0:T(8,128)(2,1)}) fusion(bf16[2,32,2,1024]{3,2,1,0:T(2,128)(2,1)} %param.17, bf16[2,32,2,1024]{3,2,1,0:T(2,128)(2,1)} %param.10), kind=kLoop, calls=%fused_computation.1 | loop fusion | bytes 1048576 | tf_op jit(solution)/shard_map/transpose | solution.py:1197
  2.6 158.3 %shard_map.145 = (bf16[2,2,32,1024]{3,2,1,0:T(8,128)(2,1)}, bf16[2,2,32,1024]{3,2,1,0:T(8,128)(2,1)}, bf16[64,1024]{1,0:T(8,128)(2,1)}, bf16[32,1024]{1,0:T(8,12...) custom-call(bf16[2,2,32,1024]{3,2,1,0:T(8,128)(2,1)} %get-tuple-element.25.tok, ...), custom_call_target="tpu_custom_call" | custom-call | tf_op jit(solution)/shard_map/pallas_call | solution.py:1208
  160.9 0.0 copy-start.1
  160.9 0.0 copy-start.2
  160.9 0.0 copy-start.3
  160.9 0.0 copy-start
  161.0 1.1 convert_bitcast_fusion
  162.1 1.2 copy.19
  163.3 1.6 convert_element_type.14
  164.9 0.0 copy-done.1
  164.9 1.0 copy.18
  165.9 0.0 copy-done.2
  165.9 0.7 convert_element_type.15
  166.6 0.0 copy-done.3
  166.6 0.5 copy.24
  167.1 0.0 copy-done
  167.1 1.2 copy.25
Async XLA Ops:
  160.9 4.0 %copy-start.1 = (bf16[2,2,32,1024]{3,2,1,0:T(8,128)(2,1)S(1)}, bf16[2,2,32,1024]{3,2,1,0:T(8,128)(2,1)}, u32[]{:S(2)}) copy-start(bf16[2,2,32,1024]{3,2,1,0:T(8,128)(2,1)} %get-tuple-element.12) | copy-start | bytes 786436
  160.9 5.0 %copy-start.2 = (bf16[32,1024]{1,0:T(8,128)(2,1)S(1)}, bf16[32,1024]{1,0:T(8,128)(2,1)}, u32[]{:S(2)}) copy-start(bf16[32,1024]{1,0:T(8,128)(2,1)} %get-tuple-element.15) | copy-start | bytes 196612
  160.9 5.6 %copy-start.3 = (f32[1,68]{1,0:T(1,128)S(1)}, f32[1,68]{1,0:T(1,128)}, u32[]{:S(2)}) copy-start(f32[1,68]{1,0:T(1,128)} %get-tuple-element.16) | copy-start | bytes 820
  160.9 6.1 %copy-start = (f32[3,144,1024]{2,1,0:T(8,128)S(1)}, f32[3,144,1024]{2,1,0:T(8,128)}, u32[]{:S(2)}) copy-start(f32[3,144,1024]{2,1,0:T(8,128)} %get-tuple-element.17) | copy-start | bytes 5308420

commit v6 on v5

--- a/solution.py
+++ b/solution.py
@@ -242,6 +242,7 @@
 
 MESH = pl.DeviceIdType.MESH
 COPIES = 400
+LEFT_ALONE = 25
 
 
 class Wires:
@@ -249,6 +250,7 @@
         self.sems = sems
         self.used = 0
         self.pending = []
+        self.turn, self.born = 0, {}
 
     def sem(self):
         self.used += 1
@@ -261,6 +263,7 @@
         )
         copy.start()
         self.pending.append(copy)
+        self.born[id(copy)] = self.turn
         return copy
 
     def local(self, src, dst, arrives):
@@ -272,7 +275,8 @@
         pltpu.make_async_copy(ref, ref, sem).wait()
 
     def finish(self, copies=None):
-        copies = list(self.pending if copies is None else copies)
+        known = {id(copy) for copy in self.pending}
+        copies = [copy for copy in (self.pending if copies is None else copies) if id(copy) in known]
         for copy in copies:
             copy.wait_send()
         done = {id(copy) for copy in copies}
@@ -280,13 +284,13 @@
 
 
 def block_kernel(
-    tok, cot, win, wout, gain_in, wffn, segments, lengths, cos_t, sin_t,
+    tok, cot, win, wout, gain_in, wffn, segments, lengths, cos_in, sin_in,
     o_block, o_tokens, o_in, o_out, o_gain, o_ffn,
     x, rel_t, rel_c, w2, wall, wfa, wfb, gb, grow, first2, raw, po,
     q0, q1, kk, vv, prob, att, mxs, mix, sec2, dy2, acta, actb, asend,
     dsb, osb, dsr, osr, rsz, gr, gs, gt, dstate, dmb, daf, dmix,
     dkk, dvv, dqq, dpj, dpx, dfb, dfr, igs, agr, agz, agt, agh, ago,
-    bos, obs, bor, tgs, tgr, gg, ggq, gsum, ggt, gain, gflat, doc_col, doc_row, sems,
+    bos, obs, bor, tgs, tgr, gg, ggq, gsum, ggt, gain, gflat, doc_col, doc_row, cos_t, sin_t, sems,
 ):
     dp = lax.axis_index("dp")
     c = lax.axis_index("ctx")
@@ -323,6 +327,10 @@
     peers = [quad(d, e) for d, e in others] + [zp, zps, yp, diag]
     for peer in peers:
         pl.semaphore_signal(barrier, inc=1, device_id=peer, device_id_type=MESH)
+
+    s_cos, s_sin = w.sem(), w.sem()
+    w.local(cos_in, cos_t, s_cos)
+    w.local(sin_in, sin_t, s_sin)
 
     limit = lengths[zh]
     docs = segments[zh].astype(F32).astype(BF)
@@ -627,6 +635,8 @@
     @step("rotate")
     def _():
         w.arrived(raw.at[pl.ds(0, 512)], s_raw)
+        w.arrived(cos_t, s_cos)
+        w.arrived(sin_t, s_sin)
         query_weight, key_weight = query_gain(), key_gain()
 
         def rotate_rows(t, carry):
@@ -1130,8 +1140,10 @@
         right = pltpu.roll(gflat[pl.ds(line + 1, 1), :], back, 1)
         o_gain[...] = jnp.where(lane < LANES - shift, left, right)[:, 0:68]
 
-    for name in ORDER:
+    for turn, name in enumerate(ORDER):
+        w.turn = turn
         steps.pop(name)()
+        w.finish([copy for copy in w.pending if w.born[id(copy)] < turn - LEFT_ALONE])
     assert not steps, sorted(steps)
     w.finish()
     for half, away in late:
@@ -1174,6 +1186,7 @@
     ((2, 64, 1024), F32), ((2, 2, 32, 1024), BF), ((2, 2, 32, 1024), BF), ((2, 2, 32, 1024), BF),
     ((2, 2, 32, 1024), BF),
     ((8, 384), F32), ((8, 8, 384), F32), ((8, 384), F32), ((3, 8, 384), F32), ((8, 128), F32), ((24, 128), F32), ((1024, 8), F32), ((8, 1024), F32),
+    ((1024, 128), F32), ((1024, 128), F32),
 )
 
 
@@ -1205,6 +1218,7 @@
         jnp.asarray(sine),
     )
     vmem = pl.BlockSpec(memory_space=pltpu.VMEM)
+    anywhere = pl.BlockSpec(memory_space=pl.ANY)
     outs = pl.pallas_call(
         block_kernel,
         out_shape=(
@@ -1215,7 +1229,8 @@
             jax.ShapeDtypeStruct((1, 68), F32),
             jax.ShapeDtypeStruct((3, 144, 1024), F32),
         ),
-        in_specs=[vmem] * 7 + [pl.BlockSpec(memory_space=pltpu.SMEM)] + [vmem] * 2,
+        in_specs=[vmem] * 5
+        + [anywhere, vmem, pl.BlockSpec(memory_space=pltpu.SMEM), anywhere, anywhere],
         out_specs=(vmem,) * 6,
         scratch_shapes=[pltpu.VMEM(shape, kind) for shape, kind in TEAM_SCRATCH]
         + [pltpu.SemaphoreType.DMA((COPIES,))],

time: 169 us -> 168 us (level)
  no operation moved by 1% of the time
where the time goes in v6:
time: 168 us; the launch traced here: 167 us
  Pallas kernels  157 us (93%)
  local copies, waits for them, and re-layouts  5.85 us (3%)
  other arithmetic  3.42 us (2%)
    pallas_call x1, Pallas kernels, on_team(): pl.pallas_call(block_kernel, out_shape=(jax.ShapeDtypeStruct((2, 2, 32, 1...  157 us
    unnamed x12, local copies, waits for them, and re-layouts  3.91 us

profile of v6, /device:TPU:0, one launch (start us, length us, event | category | flops | bytes accessed | tf_op | source)
XLA Modules:
  0.0 166.7 jit_solution(12556477088202482546)
XLA Ops:
  0.6 1.9 %copy_bitcast_fusion = (bf16[2,2,32,1024]{3,2,1,0:T(8,128)(2,1)}, bf16[2,2,32,1024]{3,2,1,0:T(8,128)(2,1)}) fusion(bf16[2,32,2,1024]{3,2,1,0:T(2,128)(2,1)} %param.17, bf16[2,32,2,1024]{3,2,1,0:T(2,128)(2,1)} %param.10), kind=kLoop, calls=%fused_computation.1 | loop fusion | bytes 1048576 | tf_op jit(solution)/shard_map/transpose | solution.py:1210
  2.6 156.7 %shard_map.145 = (bf16[2,2,32,1024]{3,2,1,0:T(8,128)(2,1)}, bf16[2,2,32,1024]{3,2,1,0:T(8,128)(2,1)}, bf16[64,1024]{1,0:T(8,128)(2,1)}, bf16[32,1024]{1,0:T(8,12...) custom-call(bf16[2,2,32,1024]{3,2,1,0:T(8,128)(2,1)} %get-tuple-element.25.tok, ...), custom_call_target="tpu_custom_call" | custom-call | tf_op jit(solution)/shard_map/pallas_call | solution.py:1222
  159.3 0.0 copy-start.1
  159.3 0.0 copy-start.2
  159.3 0.0 copy-start.3
  159.3 0.0 copy-start
  159.3 1.1 convert_bitcast_fusion
  160.5 1.2 copy.19
  161.7 1.6 convert_element_type.14
  163.3 0.0 copy-done.1
  163.3 1.0 copy.18
  164.3 0.0 copy-done.2
  164.3 0.7 convert_element_type.15
  164.9 0.0 copy-done.3
  165.0 0.5 copy.24
  165.5 0.0 copy-done
  165.5 1.2 copy.25
Async XLA Ops:
  159.3 4.0 %copy-start.1 = (bf16[2,2,32,1024]{3,2,1,0:T(8,128)(2,1)S(1)}, bf16[2,2,32,1024]{3,2,1,0:T(8,128)(2,1)}, u32[]{:S(2)}) copy-start(bf16[2,2,32,1024]{3,2,1,0:T(8,128)(2,1)} %get-tuple-element.12) | copy-start | bytes 786436
  159.3 5.0 %copy-start.2 = (bf16[32,1024]{1,0:T(8,128)(2,1)S(1)}, bf16[32,1024]{1,0:T(8,128)(2,1)}, u32[]{:S(2)}) copy-start(bf16[32,1024]{1,0:T(8,128)(2,1)} %get-tuple-element.15) | copy-start | bytes 196612
  159.3 5.6 %copy-start.3 = (f32[1,68]{1,0:T(1,128)S(1)}, f32[1,68]{1,0:T(1,128)}, u32[]{:S(2)}) copy-start(f32[1,68]{1,0:T(1,128)} %get-tuple-element.16) | copy-start | bytes 820
  159.3 6.1 %copy-start = (f32[3,144,1024]{2,1,0:T(8,128)S(1)}, f32[3,144,1024]{2,1,0:T(8,128)}, u32[]{:S(2)}) copy-start(f32[3,144,1024]{2,1,0:T(8,128)} %get-tuple-element.17) | copy-start | bytes 5308420

commit v7 on v6

--- a/solution.py
+++ b/solution.py
@@ -861,7 +861,7 @@
                 o_ffn[kind, span, :] = (
                     buf[kind, 0:rows_kept, :].astype(F32)
                     + gr[0, kind, span, :].astype(F32) + gt[kind, span, :].astype(F32)
-                )
+                ).astype(BF)
 
         feed_forward(0)
         feed_forward(1)
@@ -1227,7 +1227,7 @@
             jax.ShapeDtypeStruct((64, 1024), BF),
             jax.ShapeDtypeStruct((32, 1024), BF),
             jax.ShapeDtypeStruct((1, 68), F32),
-            jax.ShapeDtypeStruct((3, 144, 1024), F32),
+            jax.ShapeDtypeStruct((3, 144, 1024), BF),
         ),
         in_specs=[vmem] * 5
         + [anywhere, vmem, pl.BlockSpec(memory_space=pltpu.SMEM), anywhere, anywhere],
@@ -1245,7 +1245,7 @@
         in_grad.astype(F32),
         out_grad.astype(F32),
         gain_grad[0],
-        unit_grad.transpose(1, 0, 2),
+        unit_grad.transpose(1, 0, 2).astype(F32),
     )
 
 

time: 168 us -> 167 us (level)
    convert_element_type x0 -> x1, other arithmetic: none -> 2.62 us  [on_team(): unit_grad.transpose(1, 0, 2).astype(F32)]
    unnamed x12 -> x13, local copies, waits for them, and re-layouts: 3.91 us -> 2.7 us
where the time goes in v7:
time: 167 us; the launch traced here: 166 us
  Pallas kernels  156 us (93%)
  local copies, waits for them, and re-layouts  4.64 us (3%)
  other arithmetic  4.05 us (2%)
    pallas_call x1, Pallas kernels, on_team(): pl.pallas_call(block_kernel, out_shape=(jax.ShapeDtypeStruct((2, 2, 32, 1...  156 us

profile of v7, /device:TPU:0, one launch (start us, length us, event | category | flops | bytes accessed | tf_op | source)
XLA Modules:
  0.0 165.8 jit_solution(1486200395210442938)
XLA Ops:
  0.6 1.9 %copy_bitcast_fusion = (bf16[2,2,32,1024]{3,2,1,0:T(8,128)(2,1)}, bf16[2,2,32,1024]{3,2,1,0:T(8,128)(2,1)}) fusion(bf16[2,32,2,1024]{3,2,1,0:T(2,128)(2,1)} %param.17, bf16[2,32,2,1024]{3,2,1,0:T(2,128)(2,1)} %param.10), kind=kLoop, calls=%fused_computation.2 | loop fusion | bytes 1048576 | tf_op jit(solution)/shard_map/transpose | solution.py:1210
  2.6 156.4 %shard_map.145 = (bf16[2,2,32,1024]{3,2,1,0:T(8,128)(2,1)}, bf16[2,2,32,1024]{3,2,1,0:T(8,128)(2,1)}, bf16[64,1024]{1,0:T(8,128)(2,1)}, bf16[32,1024]{1,0:T(8,12...) custom-call(bf16[2,2,32,1024]{3,2,1,0:T(8,128)(2,1)} %get-tuple-element.25.tok, ...), custom_call_target="tpu_custom_call" | custom-call | tf_op jit(solution)/shard_map/pallas_call | solution.py:1222
  159.0 0.0 copy-start
  159.0 0.0 copy-start.2
  159.0 2.6 %convert_bitcast_fusion = f32[144,3,1024]{2,0,1:T(8,128)} fusion(bf16[3,144,1024]{2,1,0:T(8,128)(2,1)} %get-tuple-element.17), kind=kLoop, calls=%fused_computation | loop fusion | flops 442368 | bytes 2654208 | tf_op jit(solution)/shard_map/convert_element_type | solution.py:1248
  161.6 0.0 copy-start.1
  161.6 0.0 copy-start.3
  161.7 0.0 copy-start.4
  161.7 0.0 copy-done
  161.7 1.2 copy.19
  162.9 0.0 copy-done.2
  162.9 0.7 convert_element_type.20
  163.6 0.0 copy-done.1
  163.6 1.0 copy.18
  164.6 0.0 copy-done.3
  164.6 0.7 convert_element_type.21
  165.3 0.0 copy-done.4
  165.3 0.5 copy.23
  (1 shorter events, 0.0 us)
Async XLA Ops:
  159.0 2.7 %copy-start = (bf16[2,2,32,1024]{3,2,1,0:T(8,128)(2,1)S(1)}, bf16[2,2,32,1024]{3,2,1,0:T(8,128)(2,1)}, u32[]{:S(2)}) copy-start(bf16[2,2,32,1024]{3,2,1,0:T(8,128)(2,1)} %get-tuple-element.13) | copy-start | bytes 786436
  159.0 3.9 %copy-start.2 = (bf16[64,1024]{1,0:T(8,128)(2,1)S(1)}, bf16[64,1024]{1,0:T(8,128)(2,1)}, u32[]{:S(2)}) copy-start(bf16[64,1024]{1,0:T(8,128)(2,1)} %get-tuple-element.14) | copy-start | bytes 393220
  161.6 2.0 %copy-start.1 = (bf16[2,2,32,1024]{3,2,1,0:T(8,128)(2,1)S(1)}, bf16[2,2,32,1024]{3,2,1,0:T(8,128)(2,1)}, u32[]{:S(2)}) copy-start(bf16[2,2,32,1024]{3,2,1,0:T(8,128)(2,1)} %get-tuple-element.12) | copy-start | bytes 786436
  161.6 3.0 %copy-start.3 = (bf16[32,1024]{1,0:T(8,128)(2,1)S(1)}, bf16[32,1024]{1,0:T(8,128)(2,1)}, u32[]{:S(2)}) copy-start(bf16[32,1024]{1,0:T(8,128)(2,1)} %get-tuple-element.15) | copy-start | bytes 196612
  161.7 3.6 %copy-start.4 = (f32[1,68]{1,0:T(1,128)S(1)}, f32[1,68]{1,0:T(1,128)}, u32[]{:S(2)}) copy-start(f32[1,68]{1,0:T(1,128)} %get-tuple-element.16) | copy-start | bytes 820
